TPU v7x, 32 devices: a whole 2x2x4 slice. The times are simulated.
32 devices in a mesh: dom: 16 (over z, y, core), grid: 2 (over x).
Axes of the slice: x: 2, y: 2, z: 4, core: 2. Of those that a mesh axis runs over, the one named last changes fastest.
Arguments:
- rhs: bfloat16 [2, 96, 16, 320], P('grid', 'dom'), may hold values from -24 to 24
- blocks: bfloat16 [2, 96, 3, 320, 320], P('grid', 'dom'), may hold values from -0.1875 to 0.1875
- offsets: int32 [2, 96, 3], P('grid', 'dom'), may hold values from -1 to 1
- donor_elem: int32 [2, 16, 2, 2], P('grid', 'dom'), may hold values from 0 to 5
- fringe_elem: int32 [2, 16, 2, 2], P('grid', 'dom'), may hold values from 0 to 5
- donor_weight: float32 [2, 16, 2, 2], P('grid', 'dom'), may hold values from 0.25 to 1
- fringe_count: int32 [2, 16, 2], P('grid', 'dom'), may hold values from 0 to 2, as said below
Outputs:
- powers: bfloat16 [2, 96, 4, 16, 320], P('grid', 'dom')
- r_factor: float32 [80, 80], replicated
Inputs may be any that keep to these rules, and one draw needn't show every extreme that they name: `fringe_count`: the count from a grid to its own partitions is 0. In every draw some partition of each grid receives 2 slots from every other grid.
All inputs are finite; a program needn't handle non-finite values.
Results may differ from a plain program's by a relative error of at most 0.0033.
The roundings to bfloat16 on the way count: a program that leaves them out, or rounds other values in their place, can miss the bound.
Values may be sent and summed in bfloat16 or wider, within the bound.
No kernel may reach another device: no remote copies, remote signals or barrier semaphores. Data moves between devices by JAX's collectives and lax.ppermute only.
A program may use at most 64 MiB of HBM per device.

v0:
```python
import jax
import jax.numpy as jnp
from jax import lax
from jax.sharding import PartitionSpec as P

S = 4
H = 1


def extended_2(array, sides, width):
    for axis, dim in sides:
        peers, length = (lax.axis_size(axis), array.shape[dim])
        up = [(i, (i + 1) % peers) for i in range(peers - 1)]
        down = [(j, i) for i, j in up]
        last = lax.slice_in_dim(array, length - width, length, axis=dim)
        leading = lax.slice_in_dim(array, 0, width, axis=dim)
        before = lax.ppermute(last, axis, up)
        after = lax.ppermute(leading, axis, down)
        array = jnp.concatenate([before, array, after], axis=dim)
    return array


def local(rhs, blocks, offsets, donor_elem, fringe_elem, donor_weight, fringe_count):
    elem_count = rhs.shape[1]
    rhs_count = rhs.shape[2]
    unknowns = rhs.shape[3]
    slot_count = donor_elem.shape[3]
    grid_count = lax.axis_size("grid")
    col_index = offsets[0] + jnp.arange(elem_count, dtype=jnp.int32)[:, None] + H
    live_slot = jnp.arange(slot_count, dtype=jnp.int32)[None, :] < fringe_count[0, 0][:, None]
    weights = jnp.where(live_slot, donor_weight[0, 0], 0.0)
    hit_target = (
        fringe_elem[0, 0][None, :, :] == jnp.arange(elem_count, dtype=jnp.int32)[:, None, None]
    )
    spread = jnp.where(hit_target, weights[None], 0.0)
    columns = (S + 1) * rhs_count
    field = rhs[0]
    basis = [field]
    for level in range(S):
        extended = extended_2(field, (("dom", 0),), H)
        taken_cols = extended[col_index]
        blockpart = jnp.einsum(
            "ekra,ekab->erb", taken_cols, blocks[0], preferred_element_type=jnp.float32
        )
        gathered = lax.all_gather(field, "grid", axis=0, tiled=True)
        source_index = (
            jnp.arange(grid_count, dtype=jnp.int32)[:, None] * elem_count + donor_elem[0, 0]
        )
        picked = gathered[source_index]
        donorpart = jnp.einsum(
            "egc,gcrw->erw", spread, picked.astype(jnp.float32), precision=lax.Precision.HIGHEST
        )
        field = (blockpart + donorpart).astype(jnp.bfloat16)
        basis.append(field)
    stacked = jnp.stack(basis, axis=1)
    partial_gram = jnp.einsum(
        "ekrw,elqw->krlq", stacked, stacked, preferred_element_type=jnp.float32
    )
    gram = lax.psum(partial_gram.reshape(columns, columns), ("dom", "grid"))
    row_total = grid_count * lax.axis_size("dom") * elem_count * unknowns
    gram = gram / row_total
    r_factor = jnp.linalg.cholesky(gram).T
    powers = jnp.stack(basis[1:], axis=1)[None]
    return (powers, r_factor)


def solution(mesh):
    in_specs = (
        P("grid", "dom", None, None),
        P("grid", "dom", None, None, None),
        P("grid", "dom", None),
        P("grid", "dom", None, None),
        P("grid", "dom", None, None),
        P("grid", "dom", None, None),
        P("grid", "dom", None),
    )
    out_specs = (P("grid", "dom", None, None, None), P())
    return jax.shard_map(local, mesh=mesh, in_specs=in_specs, out_specs=out_specs, check_vma=False)
```

profile of v0, /device:TPU:0, one launch (start us, length us, event | category | flops | bytes accessed | tf_op | source)
XLA Modules:
  0.0 126.1 jit_solution(3580005175848588244)
XLA Ops:
  0.6 0.7 slice_bitcast_fusion.1
  1.4 2.3 %collective-permute-start = (bf16[1,16,320]{2,1,0:T(8,128)(2,1)S(1)}, bf16[1,16,320]{2,1,0:T(8,128)(2,1)S(1)}, u32[]{:S(2)}, u32[]{:S(2)}) collective-permute-start(bf16[1,16,320]{2,1,0:T(8,128)(2,1)S(1)} %get-tuple-element.14), channel_id=1, source_target_pairs={{0,2},{2,4},{4,6},{6,8},{8,10},{10,12},{12,14},{14,16},{16,18},{18... | collective-permute-start | bytes 30728 | tf_op jit(solution)/shard_map/ppermute | solution.py:17
  3.7 1.3 %collective-permute-start.1 = (bf16[1,16,320]{2,1,0:T(8,128)(2,1)S(1)}, bf16[1,16,320]{2,1,0:T(8,128)(2,1)S(1)}, u32[]{:S(2)}, u32[]{:S(2)}) collective-permute-start(bf16[1,16,320]{2,1,0:T(8,128)(2,1)S(1)} %get-tuple-element.15), channel_id=1, source_target_pairs={{2,0},{4,2},{6,4},{8,6},{10,8},{12,10},{14,12},{16,14},{18,16},{20... | collective-permute-start | bytes 30728 | tf_op jit(solution)/shard_map/ppermute | solution.py:18
  5.0 0.9 bitcast_dynamic-update-slice_fusion
  5.9 0.7 compare_select_fusion.1
  6.8 0.8 copy.41
  7.5 0.8 compare_select_fusion.3
  8.4 0.7 compare_select_fusion
  9.2 5.6 %all-gather = bf16[1,12,16,320]{3,2,0,1:T(8,128)(2,1)S(1)} all-gather(bf16[1,6,16,320]{3,2,0,1:T(8,128)(2,1)} %bitcast.163), channel_id=2, replica_groups=mesh['dom'=16,'grid'=2] {'grid'}, dimensions={1}, use_global_device_ids=true | all-gather | bytes 184320 | tf_op jit(solution)/shard_map/all_gather | solution.py:45
  15.8 0.9 pad_maximum_fusion
  17.3 3.0 %constant_dynamic-update-slice_fusion.3 = (bf16[6,5,16,320]{3,2,0,1:T(8,128)(2,1)S(1)}, bf16[6,16,320]{2,1,0:T(8,128)(2,1)S(1)}) fusion(bf16[6,5,16,320]{3,2,0,1:T(8,128)(2,1)S(1)} %bitcast_dynamic-update-slice_fusion, f32[6,16,320]{2,0,1:T(8,128)S(1)} %convolution_bitcast_fusion.4, bf16[6,3,16,320]{3,2,1,0:T(8,128)(2,1)S(1)} %bitcast.162, ...), kind=kOutput, calls=%fused_computation.58 | convolution fusion | flops 59043840 | bytes 4251648 | tf_op jit(solution)/shard_map/ekra,ekab->erb/dot_general | solution.py:42
  20.3 5.0 %all_gather.13 = bf16[12,16,320]{2,1,0:T(8,128)(2,1)S(1)} all-gather(bf16[6,16,320]{2,1,0:T(8,128)(2,1)S(1)} %get-tuple-element.17), channel_id=1, replica_groups=mesh['dom'=16,'grid'=2] {'grid'}, dimensions={0}, use_global_device_ids=true | all-gather | bytes 184320 | tf_op jit(solution)/shard_map/all_gather | solution.py:45
  25.4 2.5 %collective-permute-start.2 = (bf16[1,16,320]{2,1,0:T(8,128)(2,1)S(1)}, bf16[1,16,320]{2,1,0:T(8,128)(2,1)S(1)}, u32[]{:S(2)}, u32[]{:S(2)}) collective-permute-start(bf16[1,16,320]{2,1,0:T(8,128)(2,1)S(1)} %get-tuple-element.12), channel_id=1, source_target_pairs={{0,2},{2,4},{4,6},{6,8},{8,10},{10,12},{12,14},{14,16},{16,18},{18... | collective-permute-start | bytes 30728 | tf_op jit(solution)/shard_map/ppermute | solution.py:17
  27.9 1.3 %collective-permute-start.3 = (bf16[1,16,320]{2,1,0:T(8,128)(2,1)S(1)}, bf16[1,16,320]{2,1,0:T(8,128)(2,1)S(1)}, u32[]{:S(2)}, u32[]{:S(2)}) collective-permute-start(bf16[1,16,320]{2,1,0:T(8,128)(2,1)S(1)} %get-tuple-element.13), channel_id=1, source_target_pairs={{2,0},{4,2},{6,4},{8,6},{10,8},{12,10},{14,12},{16,14},{18,16},{20... | collective-permute-start | bytes 30728 | tf_op jit(solution)/shard_map/ppermute | solution.py:18
  30.2 4.3 %collective-permute-done.3 = bf16[1,16,320]{2,1,0:T(8,128)(2,1)S(1)} collective-permute-done((bf16[1,16,320]{2,1,0:T(8,128)(2,1)S(1)}, bf16[1,16,320]{2,1,0:T(8,128)(2,1)S(1)}, u32[]{:S(2)}, u32[]{:S(2)}) %collective-permute-start.3) | collective-permute-done | bytes 10272 | tf_op jit(solution)/shard_map/ppermute | solution.py:18
  35.1 3.0 %constant_dynamic-update-slice_fusion.2 = (bf16[6,5,16,320]{3,2,0,1:T(8,128)(2,1)S(1)}, bf16[6,16,320]{2,1,0:T(8,128)(2,1)S(1)}) fusion(bf16[6,5,16,320]{3,2,0,1:T(8,128)(2,1)S(1)} %get-tuple-element.16, f32[6,16,320]{2,0,1:T(8,128)S(1)} %convolution_bitcast_fusion.3, bf16[6,3,16,320]{3,2,1,0:T(8,128)(2,1)S(1)} %bitcast.160, ...), kind=kOutput, calls=%fused_computation.57 | convolution fusion | flops 59043840 | bytes 4251648 | tf_op jit(solution)/shard_map/ekra,ekab->erb/dot_general | solution.py:42
  38.2 5.0 %all_gather.14 = bf16[12,16,320]{2,1,0:T(8,128)(2,1)S(1)} all-gather(bf16[6,16,320]{2,1,0:T(8,128)(2,1)S(1)} %get-tuple-element.19), channel_id=1, replica_groups=mesh['dom'=16,'grid'=2] {'grid'}, dimensions={0}, use_global_device_ids=true | all-gather | bytes 184320 | tf_op jit(solution)/shard_map/all_gather | solution.py:45
  43.2 3.2 %collective-permute-start.4 = (bf16[1,16,320]{2,1,0:T(8,128)(2,1)S(1)}, bf16[1,16,320]{2,1,0:T(8,128)(2,1)S(1)}, u32[]{:S(2)}, u32[]{:S(2)}) collective-permute-start(bf16[1,16,320]{2,1,0:T(8,128)(2,1)S(1)} %get-tuple-element.10), channel_id=1, source_target_pairs={{0,2},{2,4},{4,6},{6,8},{8,10},{10,12},{12,14},{14,16},{16,18},{18... | collective-permute-start | bytes 30728 | tf_op jit(solution)/shard_map/ppermute | solution.py:17
  46.4 1.3 %collective-permute-start.5 = (bf16[1,16,320]{2,1,0:T(8,128)(2,1)S(1)}, bf16[1,16,320]{2,1,0:T(8,128)(2,1)S(1)}, u32[]{:S(2)}, u32[]{:S(2)}) collective-permute-start(bf16[1,16,320]{2,1,0:T(8,128)(2,1)S(1)} %get-tuple-element.11), channel_id=1, source_target_pairs={{2,0},{4,2},{6,4},{8,6},{10,8},{12,10},{14,12},{16,14},{18,16},{20... | collective-permute-start | bytes 30728 | tf_op jit(solution)/shard_map/ppermute | solution.py:18
  48.7 1.6 %collective-permute-done.5 = bf16[1,16,320]{2,1,0:T(8,128)(2,1)S(1)} collective-permute-done((bf16[1,16,320]{2,1,0:T(8,128)(2,1)S(1)}, bf16[1,16,320]{2,1,0:T(8,128)(2,1)S(1)}, u32[]{:S(2)}, u32[]{:S(2)}) %collective-permute-start.5) | collective-permute-done | bytes 10272 | tf_op jit(solution)/shard_map/ppermute | solution.py:18
  50.9 3.0 %constant_dynamic-update-slice_fusion.1 = (bf16[6,5,16,320]{3,2,0,1:T(8,128)(2,1)S(1)}, bf16[6,16,320]{2,1,0:T(8,128)(2,1)S(1)}) fusion(bf16[6,5,16,320]{3,2,0,1:T(8,128)(2,1)S(1)} %get-tuple-element.18, f32[6,16,320]{2,0,1:T(8,128)S(1)} %convolution_bitcast_fusion.2, bf16[6,3,16,320]{3,2,1,0:T(8,128)(2,1)S(1)} %bitcast.161, ...), kind=kOutput, calls=%fused_computation.56 | convolution fusion | flops 59043840 | bytes 4251648 | tf_op jit(solution)/shard_map/ekra,ekab->erb/dot_general | solution.py:42
  53.9 5.0 %all_gather.15 = bf16[12,16,320]{2,1,0:T(8,128)(2,1)S(1)} all-gather(bf16[6,16,320]{2,1,0:T(8,128)(2,1)S(1)} %get-tuple-element.21), channel_id=1, replica_groups=mesh['dom'=16,'grid'=2] {'grid'}, dimensions={0}, use_global_device_ids=true | all-gather | bytes 184320 | tf_op jit(solution)/shard_map/all_gather | solution.py:45
  58.9 3.6 %collective-permute-start.6 = (bf16[1,16,320]{2,1,0:T(8,128)(2,1)S(1)}, bf16[1,16,320]{2,1,0:T(8,128)(2,1)S(1)}, u32[]{:S(2)}, u32[]{:S(2)}) collective-permute-start(bf16[1,16,320]{2,1,0:T(8,128)(2,1)S(1)} %get-tuple-element.8), channel_id=1, source_target_pairs={{0,2},{2,4},{4,6},{6,8},{8,10},{10,12},{12,14},{14,16},{16,18},{18... | collective-permute-start | bytes 30728 | tf_op jit(solution)/shard_map/ppermute | solution.py:17
  62.6 1.3 %collective-permute-start.7 = (bf16[1,16,320]{2,1,0:T(8,128)(2,1)S(1)}, bf16[1,16,320]{2,1,0:T(8,128)(2,1)S(1)}, u32[]{:S(2)}, u32[]{:S(2)}) collective-permute-start(bf16[1,16,320]{2,1,0:T(8,128)(2,1)S(1)} %get-tuple-element.9), channel_id=1, source_target_pairs={{2,0},{4,2},{6,4},{8,6},{10,8},{12,10},{14,12},{16,14},{18,16},{20... | collective-permute-start | bytes 30728 | tf_op jit(solution)/shard_map/ppermute | solution.py:18
  64.8 1.9 %collective-permute-done.7 = bf16[1,16,320]{2,1,0:T(8,128)(2,1)S(1)} collective-permute-done((bf16[1,16,320]{2,1,0:T(8,128)(2,1)S(1)}, bf16[1,16,320]{2,1,0:T(8,128)(2,1)S(1)}, u32[]{:S(2)}, u32[]{:S(2)}) %collective-permute-start.7) | collective-permute-done | bytes 10272 | tf_op jit(solution)/shard_map/ppermute | solution.py:18
  67.4 3.0 %constant_dynamic-update-slice_fusion = (bf16[6,5,16,320]{3,2,0,1:T(8,128)(2,1)S(1)}, bf16[6,1,16,320]{3,2,0,1:T(8,128)(2,1)S(1)}) fusion(bf16[6,5,16,320]{3,2,0,1:T(8,128)(2,1)S(1)} %get-tuple-element.20, f32[6,16,320]{2,0,1:T(8,128)S(1)} %convolution_bitcast_fusion.1, bf16[6,3,16,320]{3,2,1,0:T(8,128)(2,1)S(1)} %bitcast.159, ...), kind=kOutput, calls=%fused_computation.55 | convolution fusion | flops 59043840 | bytes 4251648 | tf_op jit(solution)/shard_map/ekra,ekab->erb/dot_general | solution.py:42
  70.4 0.7 convolution_bitcast_fusion
  71.2 0.7 copy.55
  72.2 44.4 %psum.7 = f32[80,80]{0,1:T(8,128)S(1)} all-reduce(f32[80,80]{0,1:T(8,128)S(1)} %reshape.201), channel_id=1, replica_groups=mesh['dom'=16,'grid'=2] {'dom','grid'}, use_global_device_ids=true, to_apply=%region_0.1 | all-reduce | flops 6400 | bytes 51200 | tf_op jit(solution)/shard_map/psum | solution.py:59
  116.8 7.3 %cholesky.18 = f32[80,80]{1,0:T(8,128)S(1)} custom-call(f32[80,80]{1,0:T(8,128)S(1)} %fusion.53), custom_call_target="Cholesky" | custom-call | tf_op jit(solution)/shard_map/jit(cholesky)/cholesky | solution.py:62
  124.7 0.7 select_bitcast_fusion
  125.4 0.7 copy.56
  (38 shorter events, 7.8 us)
Async XLA Ops:
  1.4 14.4 %collective-permute-start = (bf16[1,16,320]{2,1,0:T(8,128)(2,1)S(1)}, bf16[1,16,320]{2,1,0:T(8,128)(2,1)S(1)}, u32[]{:S(2)}, u32[]{:S(2)}) collective-permute-start(bf16[1,16,320]{2,1,0:T(8,128)(2,1)S(1)} %get-tuple-element.14), channel_id=1, source_target_pairs={{0,2},{2,4},{4,6},{6,8},{8,10},{10,12},{12,14},{14,16},{16,18},{18... | collective-permute-start | bytes 30728 | tf_op jit(solution)/shard_map/ppermute | solution.py:17
  3.7 12.1 %collective-permute-start.1 = (bf16[1,16,320]{2,1,0:T(8,128)(2,1)S(1)}, bf16[1,16,320]{2,1,0:T(8,128)(2,1)S(1)}, u32[]{:S(2)}, u32[]{:S(2)}) collective-permute-start(bf16[1,16,320]{2,1,0:T(8,128)(2,1)S(1)} %get-tuple-element.15), channel_id=1, source_target_pairs={{2,0},{4,2},{6,4},{8,6},{10,8},{12,10},{14,12},{16,14},{18,16},{20... | collective-permute-start | bytes 30728 | tf_op jit(solution)/shard_map/ppermute | solution.py:18
  25.4 4.8 %collective-permute-start.2 = (bf16[1,16,320]{2,1,0:T(8,128)(2,1)S(1)}, bf16[1,16,320]{2,1,0:T(8,128)(2,1)S(1)}, u32[]{:S(2)}, u32[]{:S(2)}) collective-permute-start(bf16[1,16,320]{2,1,0:T(8,128)(2,1)S(1)} %get-tuple-element.12), channel_id=1, source_target_pairs={{0,2},{2,4},{4,6},{6,8},{8,10},{10,12},{12,14},{14,16},{16,18},{18... | collective-permute-start | bytes 30728 | tf_op jit(solution)/shard_map/ppermute | solution.py:17
  27.9 6.6 %collective-permute-start.3 = (bf16[1,16,320]{2,1,0:T(8,128)(2,1)S(1)}, bf16[1,16,320]{2,1,0:T(8,128)(2,1)S(1)}, u32[]{:S(2)}, u32[]{:S(2)}) collective-permute-start(bf16[1,16,320]{2,1,0:T(8,128)(2,1)S(1)} %get-tuple-element.13), channel_id=1, source_target_pairs={{2,0},{4,2},{6,4},{8,6},{10,8},{12,10},{14,12},{16,14},{18,16},{20... | collective-permute-start | bytes 30728 | tf_op jit(solution)/shard_map/ppermute | solution.py:18
  43.2 5.5 %collective-permute-start.4 = (bf16[1,16,320]{2,1,0:T(8,128)(2,1)S(1)}, bf16[1,16,320]{2,1,0:T(8,128)(2,1)S(1)}, u32[]{:S(2)}, u32[]{:S(2)}) collective-permute-start(bf16[1,16,320]{2,1,0:T(8,128)(2,1)S(1)} %get-tuple-element.10), channel_id=1, source_target_pairs={{0,2},{2,4},{4,6},{6,8},{8,10},{10,12},{12,14},{14,16},{16,18},{18... | collective-permute-start | bytes 30728 | tf_op jit(solution)/shard_map/ppermute | solution.py:17
  46.4 3.8 %collective-permute-start.5 = (bf16[1,16,320]{2,1,0:T(8,128)(2,1)S(1)}, bf16[1,16,320]{2,1,0:T(8,128)(2,1)S(1)}, u32[]{:S(2)}, u32[]{:S(2)}) collective-permute-start(bf16[1,16,320]{2,1,0:T(8,128)(2,1)S(1)} %get-tuple-element.11), channel_id=1, source_target_pairs={{2,0},{4,2},{6,4},{8,6},{10,8},{12,10},{14,12},{16,14},{18,16},{20... | collective-permute-start | bytes 30728 | tf_op jit(solution)/shard_map/ppermute | solution.py:18
  58.9 5.9 %collective-permute-start.6 = (bf16[1,16,320]{2,1,0:T(8,128)(2,1)S(1)}, bf16[1,16,320]{2,1,0:T(8,128)(2,1)S(1)}, u32[]{:S(2)}, u32[]{:S(2)}) collective-permute-start(bf16[1,16,320]{2,1,0:T(8,128)(2,1)S(1)} %get-tuple-element.8), channel_id=1, source_target_pairs={{0,2},{2,4},{4,6},{6,8},{8,10},{10,12},{12,14},{14,16},{16,18},{18... | collective-permute-start | bytes 30728 | tf_op jit(solution)/shard_map/ppermute | solution.py:17
  62.6 4.2 %collective-permute-start.7 = (bf16[1,16,320]{2,1,0:T(8,128)(2,1)S(1)}, bf16[1,16,320]{2,1,0:T(8,128)(2,1)S(1)}, u32[]{:S(2)}, u32[]{:S(2)}) collective-permute-start(bf16[1,16,320]{2,1,0:T(8,128)(2,1)S(1)} %get-tuple-element.9), channel_id=1, source_target_pairs={{2,0},{4,2},{6,4},{8,6},{10,8},{12,10},{14,12},{16,14},{18,16},{20... | collective-permute-start | bytes 30728 | tf_op jit(solution)/shard_map/ppermute | solution.py:18
where the time goes:
time: 127 us; the launch traced here: 126 us
  blocking collectives  65.1 us (51%)
  starting transfers between devices  16.8 us (13%)
  matrix products  14.3 us (11%)
  other arithmetic  11.9 us (9%)
  local copies, waits for them, and re-layouts  9.22 us (7%)
  waiting for transfers between devices  7.85 us (6%)
    psum x1, blocking collectives, local(): gram = lax.psum(partial_gram.reshape(columns, columns), ('dom', 'grid'))  44.4 us
    all_gather x4, blocking collectives, local(): gathered = lax.all_gather(field, 'grid', axis=0, tiled=True)  20.7 us
    dot_general x4, matrix products, local(): jnp.einsum('ekra,ekab->erb', taken_cols, blocks[0], preferred_element_typ...  12.1 us
    ppermute x4, starting transfers between devices, extended_2(): before = lax.ppermute(last, axis, up)  11.7 us
    another operation x3, other arithmetic, local(): r_factor = jnp.linalg.cholesky(gram).T  7.98 us
    ppermute x4, waiting for transfers between devices, extended_2(): after = lax.ppermute(leading, axis, down)  7.84 us
    ppermute x4, starting transfers between devices, extended_2(): after = lax.ppermute(leading, axis, down)  5.17 us
  transfers between devices with their start and end apart: 8, of which 3 were waited for; matrix products, arithmetic and copies ran while one was open for 6% of the time, Pallas kernels for 0%

commit v1 on v0

v1 whole, which is shorter than its diff:
```python
import functools

import jax
import jax.numpy as jnp
from jax import lax
from jax.experimental import pallas as pl
from jax.experimental.pallas import tpu as pltpu
from jax.sharding import Mesh
from jax.sharding import PartitionSpec as P

S = 4
H = 1
CORES = 2

VMEM = pl.BlockSpec(memory_space=pltpu.VMEM)
SMEM = pl.BlockSpec(memory_space=pltpu.SMEM)


def edges_kernel(v_ref, side_ref, chip_ref):
    last = v_ref.shape[0] - 1
    core = lax.axis_index("core")
    side_ref[...] = v_ref[core * last]
    chip_ref[...] = v_ref[(1 - core) * last]


def inner_kernel(offsets_ref, v_ref, blocks_ref, acc_ref):
    count, kinds = blocks_ref.shape[:2]
    for e in range(count):
        total = None
        for k in range(kinds):
            col = e + offsets_ref[0, e, k]
            inside = jnp.logical_and(col >= 0, col < count)
            lhs = v_ref[jnp.clip(col, 0, count - 1)]
            lhs = jnp.where(inside, lhs, jnp.zeros_like(lhs))
            part = jnp.dot(lhs, blocks_ref[e, k], preferred_element_type=jnp.float32)
            total = part if total is None else total + part
        acc_ref[e] = total


def outer_kernel(
    grids, offsets_ref, donor_ref, fringe_ref, weight_ref, live_ref,
    acc_ref, blocks_ref, side_ref, chip_ref, *rest
):
    others, (v_ref, side_out, chip_out, total_ref) = rest[: grids - 1], rest[grids - 1 :]
    count, kinds = blocks_ref.shape[:2]
    last = count - 1
    chips = lax.axis_size("chip")
    chip, core, grid = (lax.axis_index(a) for a in ("chip", "core", "grid"))
    total_ref[...] = acc_ref[...]
    has_before = jnp.logical_or(chip > 0, core > 0)
    has_after = jnp.logical_or(chip < chips - 1, core == 0)
    before = jnp.where(core == 0, side_ref[...], chip_ref[...])
    after = jnp.where(core == 0, chip_ref[...], side_ref[...])
    for e, halo, there, offset in ((0, before, has_before, -H), (last, after, has_after, H)):
        for k in range(kinds):
            @pl.when(jnp.logical_and(offsets_ref[0, e, k] == offset, there))
            def _(e=e, k=k, halo=halo):
                total_ref[e] += jnp.dot(halo, blocks_ref[e, k], preferred_element_type=jnp.float32)
    for s, other in enumerate(others):
        g = lax.rem(grid + grids - 1 - s, grids)
        for c in range(donor_ref.shape[3]):
            @pl.when(c < live_ref[0, 0, g])
            def _(g=g, c=c, other=other):
                f = fringe_ref[0, 0, g, c]
                value = other[donor_ref[0, 0, g, c]].astype(jnp.float32)
                total_ref[f] += weight_ref[0, 0, g, c] * value
    for e in range(count):
        v_ref[e] = total_ref[e].astype(jnp.bfloat16)
    side_out[...] = v_ref[core * last]
    chip_out[...] = v_ref[(1 - core) * last]


def gram_kernel(*refs):
    fields, (keep_ref, send_ref) = refs[: S + 1], refs[S + 1 :]
    count, n = fields[0].shape[:2]
    total = None
    for e in range(count):
        rows = jnp.concatenate([f[e] for f in fields], axis=0)
        part = lax.dot_general(rows, rows, (((1,), (1,)), ((), ())), preferred_element_type=jnp.float32)
        total = part if total is None else total + part
    b = lambda i, j0, j1: total[i * n : (i + 1) * n, j0 * n : j1 * n]
    one = jnp.concatenate([b(4, 0, 5), b(3, 0, 3)], axis=1)
    two = jnp.concatenate([b(3, 3, 4), b(2, 0, 3), b(1, 0, 2), b(0, 0, 1), jnp.zeros((n, n), jnp.float32)], axis=1)
    first = lax.axis_index("core") == 0
    keep_ref[...] = jnp.where(first, one, two)
    send_ref[...] = jnp.where(first, two, one)


def factor_kernel(scale, mine_ref, other_ref, r_ref, a_ref):
    first = lax.axis_index("core") == 0
    mine, other = mine_ref[...] * scale, other_ref[...] * scale
    one, two = jnp.where(first, mine, other), jnp.where(first, other, mine)
    n = one.shape[0]
    size = (S + 1) * n
    b = lambda x, j0, j1: x[:, j0 * n : j1 * n]
    wide = lambda x: jnp.concatenate([x, jnp.zeros((n, size - x.shape[1]), jnp.float32)], axis=1) if x.shape[1] < size else x
    low = jnp.concatenate([
        wide(b(two, 6, 7)),
        wide(b(two, 4, 6)),
        wide(b(two, 1, 4)),
        wide(jnp.concatenate([b(one, 5, 8), b(two, 0, 1)], axis=1)),
        b(one, 0, 5),
    ], axis=0)
    row = lax.broadcasted_iota(jnp.int32, (size, size), 0)
    col = lax.broadcasted_iota(jnp.int32, (size, size), 1)
    a = jnp.where(row >= col, low, low.T)
    r = jnp.zeros((size, size), jnp.float32)
    for j in range(size):
        top = a[j : j + 1, :]
        side = a[:, j : j + 1]
        pivot = a[j : j + 1, j : j + 1]
        scaled = top * lax.rsqrt(pivot)
        r = jnp.where(row == j, scaled, r)
        a = a - side * (top / pivot)
    r_ref[...] = jnp.where(col >= row, r, 0.0)


def local(rhs, blocks, offsets, donor_elem, fringe_elem, donor_weight, fringe_count):
    _, elem_count, n, unknowns = rhs.shape
    chips, cores, grids = (lax.axis_size(a) for a in ("chip", "core", "grid"))
    axes = ("chip", "core", "grid")
    at = lambda chip, core, grid: (chip * cores + core) * grids + grid % grids
    side = []
    for g in range(grids):
        for chip in range(chips - 1):
            side += [(at(chip, 1, g), at(chip + 1, 0, g)), (at(chip + 1, 0, g), at(chip, 1, g))]
        side += [(at(0, 0, g), at(0, 0, g + 1)), (at(chips - 1, 1, g), at(chips - 1, 1, g + 1))]
    swap = [(0, 1), (1, 0)]

    def exchange(v, to_side, to_chip):
        others = [
            lax.ppermute(v, "grid", [(g, (g + s) % grids) for g in range(grids)])
            for s in range(1, grids)
        ]
        return lax.ppermute(to_side, axes, side), lax.ppermute(to_chip, "core", swap), others

    halo_type = jax.ShapeDtypeStruct((n, unknowns), jnp.bfloat16)
    field_type = jax.ShapeDtypeStruct((elem_count, n, unknowns), jnp.bfloat16)
    acc_type = jax.ShapeDtypeStruct((elem_count, n, unknowns), jnp.float32)
    half_type = jax.ShapeDtypeStruct((n, 8 * n), jnp.float32)
    limit = pltpu.CompilerParams(vmem_limit_bytes=24 << 20)
    flops = 2 * elem_count * n * unknowns * unknowns * blocks.shape[2]

    field = rhs[0]
    to_side, to_chip = pl.pallas_call(
        edges_kernel, out_shape=(halo_type, halo_type), in_specs=[VMEM], out_specs=(VMEM, VMEM),
        compiler_params=limit, name="edges",
    )(field)
    blocks = pltpu.with_memory_space_constraint(blocks[0], pltpu.VMEM)
    basis = [field]
    for level in range(S):
        from_side, from_chip, others = exchange(field, to_side, to_chip)
        acc = pl.pallas_call(
            inner_kernel, out_shape=acc_type, in_specs=[SMEM, VMEM, VMEM], out_specs=VMEM,
            compiler_params=limit, name="inner",
            cost_estimate=pl.CostEstimate(flops=flops, bytes_accessed=blocks.size * 2, transcendentals=0),
        )(offsets, field, blocks)
        field, to_side, to_chip = pl.pallas_call(
            functools.partial(outer_kernel, grids),
            out_shape=(field_type, halo_type, halo_type),
            in_specs=[SMEM] * 5 + [VMEM] * (4 + grids - 1),
            out_specs=(VMEM, VMEM, VMEM),
            scratch_shapes=[pltpu.VMEM((elem_count, n, unknowns), jnp.float32)],
            compiler_params=limit, name="outer",
        )(offsets, donor_elem, fringe_elem, donor_weight, fringe_count, acc, blocks, from_side, from_chip, *others)
        basis.append(field)
    keep, send = pl.pallas_call(
        gram_kernel, out_shape=(half_type, half_type), in_specs=[VMEM] * (S + 1), out_specs=(VMEM, VMEM),
        compiler_params=limit, name="gram",
    )(*basis)
    half = keep + lax.ppermute(send, "core", swap)
    parts = lax.all_to_all(jnp.broadcast_to(half[None], (chips * grids, n, 8 * n)), ("chip", "grid"), 0, 0, tiled=True)
    mine = parts.sum(axis=0)
    other = lax.ppermute(mine, "core", swap)
    columns = (S + 1) * n
    row_total = grids * chips * cores * elem_count * unknowns
    r_factor = pl.pallas_call(
        functools.partial(factor_kernel, 1.0 / row_total),
        out_shape=jax.ShapeDtypeStruct((columns, columns), jnp.float32),
        in_specs=[VMEM] * 2, out_specs=VMEM,
        scratch_shapes=[pltpu.VMEM((columns, columns), jnp.float32)],
        compiler_params=limit, name="factor",
    )(mine, other)
    powers = jnp.stack(basis[1:], axis=1)[None]
    return (powers, r_factor)


def solution(mesh):
    dom, grids = mesh.shape["dom"], mesh.shape["grid"]
    split = Mesh(mesh.devices.reshape(dom // CORES, CORES, grids), ("chip", "core", "grid"))
    where = ("chip", "core")
    in_specs = (
        P("grid", where, None, None),
        P("grid", where, None, None, None),
        P("grid", where, None),
        P("grid", where, None, None),
        P("grid", where, None, None),
        P("grid", where, None, None),
        P("grid", where, None),
    )
    out_specs = (P("grid", where, None, None, None), P())
    return jax.shard_map(local, mesh=split, in_specs=in_specs, out_specs=out_specs, check_vma=False)
```

time: 127 us -> 56.5 us (0.44)
  blocking collectives: 65.1 us -> 14.6 us
  Pallas kernels: 0 us -> 17.7 us
  matrix products: 14.3 us -> 0 us
  other arithmetic: 11.9 us -> 0.1 us
  starting transfers between devices: 16.8 us -> 11.4 us
  waiting for transfers between devices: 7.85 us -> 4.95 us
  local copies, waits for them, and re-layouts: 9.22 us -> 6.45 us
    psum x1 -> x0, blocking collectives: 44.4 us -> none  [local(): gram = lax.psum(partial_gram.reshape(columns, columns), ('dom', 'grid'))]
    all_gather x4 -> x0, blocking collectives: 20.7 us -> none  [local(): gathered = lax.all_gather(field, 'grid', axis=0, tiled=True)]
    pallas_call x0 -> x11, Pallas kernels: none -> 17.7 us  [the longest x1 7.41 us: local(): pl.pallas_call(functools.partial(factor_kernel, 1.0 / row_total), out_sha...]
    all_to_all x0 -> x1, blocking collectives: none -> 14.6 us  [local(): lax.all_to_all(jnp.broadcast_to(half[None], (chips * grids, n, 8 * n)), (...]
    dot_general x9 -> x0, matrix products: 14.3 us -> none  [the longest x4 12.1 us: local(): jnp.einsum('ekra,ekab->erb', taken_cols, blocks[0], preferred_element_typ...]
    another operation x3 -> x0, other arithmetic: 7.98 us -> none  [local(): r_factor = jnp.linalg.cholesky(gram).T]
    ppermute x8 -> x14, starting transfers between devices: 16.8 us -> 11.4 us  [the longest x4 5.53 us: exchange(): lax.ppermute(v, 'grid', [(g, (g + s) % grids) for g in range(grids)])]
    gather x8 -> x0, local copies, waits for them, and re-layouts: 4.66 us -> none  [the longest x4 2.4 us: local(): taken_cols = extended[col_index]]
  transfers between devices with their start and end apart: 8 -> 14, of which waited for: 3 -> 5; matrix products, arithmetic and copies ran while one was open for 6% -> 3% of each run, Pallas kernels for 0% -> 9%
where the time goes in v1:
time: 56.5 us; the launch traced here: 56 us
  Pallas kernels  17.7 us (31%)
  blocking collectives  14.6 us (26%)
  starting transfers between devices  11.4 us (20%)
  local copies, waits for them, and re-layouts  6.45 us (11%)
  waiting for transfers between devices  4.95 us (9%)
  between operations  0.77 us (1%)
    all_to_all x1, blocking collectives, local(): lax.all_to_all(jnp.broadcast_to(half[None], (chips * grids, n, 8 * n)), (...  14.6 us
    pallas_call x1, Pallas kernels, local(): pl.pallas_call(functools.partial(factor_kernel, 1.0 / row_total), out_sha...  7.41 us
    unnamed x18, local copies, waits for them, and re-layouts  6.44 us
    ppermute x4, starting transfers between devices, exchange(): lax.ppermute(v, 'grid', [(g, (g + s) % grids) for g in range(grids)])  5.53 us
    pallas_call x4, Pallas kernels, local(): pl.pallas_call(inner_kernel, out_shape=acc_type, in_specs=[SMEM, VMEM, VM...  5.3 us
    pallas_call x4, Pallas kernels, local(): pl.pallas_call(functools.partial(outer_kernel, grids), out_shape=(field_t...  4.65 us
    ppermute x4, starting transfers between devices, exchange(): lax.ppermute(to_side, axes, side)  3.82 us
    ppermute x4, waiting for transfers between devices, exchange(): lax.ppermute(to_side, axes, side)  3.43 us
  transfers between devices with their start and end apart: 14, of which 5 were waited for; matrix products, arithmetic and copies ran while one was open for 3% of the time, Pallas kernels for 9%

profile of v1, /device:TPU:0, one launch (start us, length us, event | category | flops | bytes accessed | tf_op | source)
XLA Modules:
  0.0 56.0 jit_solution(13042888619110840530)
XLA Ops:
  0.7 3.0 %collective-permute-start.2 = (bf16[6,16,320]{2,1,0:T(8,128)(2,1)}, bf16[6,16,320]{2,1,0:T(8,128)(2,1)S(1)}, u32[]{:S(2)}, u32[]{:S(2)}) collective-permute-start(bf16[6,16,320]{2,1,0:T(8,128)(2,1)} %bitcast.19), channel_id=1, source_target_pairs={{0,1},{1,0},{2,3},{3,2},{4,5},{5,4},{6,7},{7,6},{8,9},{9,8},{10,11... | collective-permute-start | bytes 184328 | tf_op jit(solution)/shard_map/ppermute | solution.py:132
  3.7 0.9 %copy-done.2 = bf16[1,6,16,320]{3,2,1,0:T(8,128)(2,1)S(1)} copy-done((bf16[1,6,16,320]{3,2,1,0:T(8,128)(2,1)S(1)}, bf16[1,6,16,320]{3,2,1,0:T(8,128)(2,1)}, u32[]{:S(2)}) %copy-start.2) | copy-done | bytes 61464
  4.7 1.6 %collective-permute-start.1 = (bf16[16,320]{1,0:T(8,128)(2,1)S(1)}, bf16[16,320]{1,0:T(8,128)(2,1)S(1)}, u32[]{:S(2)}, u32[]{:S(2)}) collective-permute-start(bf16[16,320]{1,0:T(8,128)(2,1)S(1)} %get-tuple-element.17), channel_id=1, source_target_pairs={{0,2},{2,0},{1,3},{3,1},{4,6},{6,4},{5,7},{7,5},{8,10},{10,8},{9,1... | collective-permute-start | bytes 30728 | tf_op jit(solution)/shard_map/ppermute | solution.py:135
  6.3 0.8 %copy.19.offsets_ref = s32[1,6,3]{2,1,0:T(8,128)S(1)} copy(s32[1,6,3]{1,0,2:T(1,128)} %param.9) | data formatting | bytes 144 | tf_op args[2]
  7.1 2.3 %copy-done = bf16[1,6,3,320,320]{4,3,2,1,0:T(8,128)(2,1)S(1)} copy-done((bf16[1,6,3,320,320]{4,3,2,1,0:T(8,128)(2,1)S(1)}, bf16[1,6,3,320,320]{4,3,2,1,0:T(8,128)(2,1)}, u32[]{:S(2)}) %copy-start) | copy-done | bytes 3686424
  9.3 0.9 %copy-done.3 = bf16[1,6,16,320]{3,2,1,0:T(8,128)(2,1)S(1)} copy-done((bf16[1,6,16,320]{3,2,1,0:T(8,128)(2,1)S(1)}, bf16[1,6,16,320]{3,2,1,0:T(8,128)(2,1)}, u32[]{:S(2)}) %copy-start.3) | copy-done | bytes 61464
  10.2 1.3 %inner.4.acc_ref = f32[6,16,320]{2,1,0:T(8,128)S(1)} custom-call(s32[1,6,3]{2,1,0:T(8,128)S(1)} %copy.19.offsets_ref, bf16[6,16,320]{2,1,0:T(8,128)(2,1)S(1)} %bitcast.21, bf16[6,3,320,320]{3,2,1,0:T(8,128)(2,1)S(1)} %bitcast.8), custom_call_target="tpu_custom_call" | custom-call | flops 58982400 | bytes 3686400 | tf_op jit(solution)/shard_map/inner/pallas_call | solution.py:153
  11.6 0.9 %copy-done.1 = bf16[1,6,3,320,320]{4,3,2,1,0:T(8,128)(2,1)S(1)} copy-done((bf16[1,6,3,320,320]{4,3,2,1,0:T(8,128)(2,1)S(1)}, bf16[1,6,3,320,320]{4,3,2,1,0:T(8,128)(2,1)}, u32[]{:S(2)}) %copy-start.1) | copy-done | bytes 3686424
  12.4 1.0 %outer.4 = (bf16[6,16,320]{2,1,0:T(8,128)(2,1)S(1)}, bf16[16,320]{1,0:T(8,128)(2,1)S(1)}, bf16[16,320]{1,0:T(8,128)(2,1)S(1)}) custom-call(s32[1,6,3]{2,1,0:T(8,128)S(1)} %copy.19.offsets_ref, s32[1,1,2,2]{3,2,1,0:T(2,128)S(1)} %copy-done.4, s32[1,1,2,2]{3,2,1,0:T(2,128)S(1)} %copy-done.5, f32[1,1,2,2]{3,2,1,0:T(2,128)S(1)} %copy-done.6, ...), custom_call_target="tpu_custom_call" | custom-call | tf_op jit(solution)/shard_map/outer/pallas_call | solution.py:158
  13.5 0.5 collective-permute-start.5
  13.9 1.6 %collective-permute-start.3 = (bf16[16,320]{1,0:T(8,128)(2,1)S(1)}, bf16[16,320]{1,0:T(8,128)(2,1)S(1)}, u32[]{:S(2)}, u32[]{:S(2)}) collective-permute-start(bf16[16,320]{1,0:T(8,128)(2,1)S(1)} %get-tuple-element.19), channel_id=1, source_target_pairs={{2,4},{4,2},{6,8},{8,6},{10,12},{12,10},{14,16},{16,14},{18,20},{2... | collective-permute-start | bytes 30728 | tf_op jit(solution)/shard_map/ppermute | solution.py:135
  15.6 1.3 %inner.5.acc_ref = f32[6,16,320]{2,1,0:T(8,128)S(1)} custom-call(s32[1,6,3]{2,1,0:T(8,128)S(1)} %copy.19.offsets_ref, bf16[6,16,320]{2,1,0:T(8,128)(2,1)S(1)} %get-tuple-element.18.v_ref.refs_1_, bf16[6,3,320,320]{3,2,1,0:T(8,128)(2,1)S(1)} %bitcast.10), custom_call_target="tpu_custom_call" | custom-call | flops 58982400 | bytes 3686400 | tf_op jit(solution)/shard_map/inner/pallas_call | solution.py:153
  16.9 1.1 %collective-permute-done.3.side_ref = bf16[16,320]{1,0:T(8,128)(2,1)S(1)} collective-permute-done((bf16[16,320]{1,0:T(8,128)(2,1)S(1)}, bf16[16,320]{1,0:T(8,128)(2,1)S(1)}, u32[]{:S(2)}, u32[]{:S(2)}) %collective-permute-start.3) | collective-permute-done | bytes 10272 | tf_op jit(solution)/shard_map/ppermute | solution.py:135
  18.0 1.0 %outer.5 = (bf16[6,16,320]{2,1,0:T(8,128)(2,1)S(1)}, bf16[16,320]{1,0:T(8,128)(2,1)S(1)}, bf16[16,320]{1,0:T(8,128)(2,1)S(1)}) custom-call(s32[1,6,3]{2,1,0:T(8,128)S(1)} %copy.19.offsets_ref, s32[1,1,2,2]{3,2,1,0:T(2,128)S(1)} %copy-done.4, s32[1,1,2,2]{3,2,1,0:T(2,128)S(1)} %copy-done.5, f32[1,1,2,2]{3,2,1,0:T(2,128)S(1)} %copy-done.6, ...), custom_call_target="tpu_custom_call" | custom-call | tf_op jit(solution)/shard_map/outer/pallas_call | solution.py:158
  19.0 1.2 %collective-permute-start.8 = (bf16[6,16,320]{2,1,0:T(8,128)(2,1)S(1)}, bf16[6,16,320]{2,1,0:T(8,128)(2,1)S(1)}, u32[]{:S(2)}, u32[]{:S(2)}) collective-permute-start(bf16[6,16,320]{2,1,0:T(8,128)(2,1)S(1)} %get-tuple-element.21.v_ref.refs_2_), channel_id=1, source_target_pairs={{0,1},{1,0},{2,3},{3,2},{4,5},{5,4},{6,7},{7,6},{8,9},{9,8},{10,11... | collective-permute-start | bytes 184328 | tf_op jit(solution)/shard_map/ppermute | solution.py:132
  20.2 0.9 %collective-permute-start.6 = (bf16[16,320]{1,0:T(8,128)(2,1)S(1)}, bf16[16,320]{1,0:T(8,128)(2,1)S(1)}, u32[]{:S(2)}, u32[]{:S(2)}) collective-permute-start(bf16[16,320]{1,0:T(8,128)(2,1)S(1)} %get-tuple-element.22), channel_id=1, source_target_pairs={{2,4},{4,2},{6,8},{8,6},{10,12},{12,10},{14,16},{16,14},{18,20},{2... | collective-permute-start | bytes 30728 | tf_op jit(solution)/shard_map/ppermute | solution.py:135
  21.1 0.2 collective-permute-start.7
  21.3 1.3 %inner.6.acc_ref = f32[6,16,320]{2,1,0:T(8,128)S(1)} custom-call(s32[1,6,3]{2,1,0:T(8,128)S(1)} %copy.19.offsets_ref, bf16[6,16,320]{2,1,0:T(8,128)(2,1)S(1)} %get-tuple-element.21.v_ref.refs_2_, bf16[6,3,320,320]{3,2,1,0:T(8,128)(2,1)S(1)} %bitcast.12), custom_call_target="tpu_custom_call" | custom-call | flops 58982400 | bytes 3686400 | tf_op jit(solution)/shard_map/inner/pallas_call | solution.py:153
  22.6 1.3 %collective-permute-done.6.side_ref = bf16[16,320]{1,0:T(8,128)(2,1)S(1)} collective-permute-done((bf16[16,320]{1,0:T(8,128)(2,1)S(1)}, bf16[16,320]{1,0:T(8,128)(2,1)S(1)}, u32[]{:S(2)}, u32[]{:S(2)}) %collective-permute-start.6) | collective-permute-done | bytes 10272 | tf_op jit(solution)/shard_map/ppermute | solution.py:135
  23.9 1.0 %outer.6 = (bf16[6,16,320]{2,1,0:T(8,128)(2,1)S(1)}, bf16[16,320]{1,0:T(8,128)(2,1)S(1)}, bf16[16,320]{1,0:T(8,128)(2,1)S(1)}) custom-call(s32[1,6,3]{2,1,0:T(8,128)S(1)} %copy.19.offsets_ref, s32[1,1,2,2]{3,2,1,0:T(2,128)S(1)} %copy-done.4, s32[1,1,2,2]{3,2,1,0:T(2,128)S(1)} %copy-done.5, f32[1,1,2,2]{3,2,1,0:T(2,128)S(1)} %copy-done.6, ...), custom_call_target="tpu_custom_call" | custom-call | tf_op jit(solution)/shard_map/outer/pallas_call | solution.py:158
  24.9 0.9 %collective-permute-start.11 = (bf16[6,16,320]{2,1,0:T(8,128)(2,1)S(1)}, bf16[6,16,320]{2,1,0:T(8,128)(2,1)S(1)}, u32[]{:S(2)}, u32[]{:S(2)}) collective-permute-start(bf16[6,16,320]{2,1,0:T(8,128)(2,1)S(1)} %get-tuple-element.24.v_ref.refs_3_), channel_id=1, source_target_pairs={{0,1},{1,0},{2,3},{3,2},{4,5},{5,4},{6,7},{7,6},{8,9},{9,8},{10,11... | collective-permute-start | bytes 184328 | tf_op jit(solution)/shard_map/ppermute | solution.py:132
  25.8 1.2 %collective-permute-start.9 = (bf16[16,320]{1,0:T(8,128)(2,1)S(1)}, bf16[16,320]{1,0:T(8,128)(2,1)S(1)}, u32[]{:S(2)}, u32[]{:S(2)}) collective-permute-start(bf16[16,320]{1,0:T(8,128)(2,1)S(1)} %get-tuple-element.25), channel_id=1, source_target_pairs={{2,4},{4,2},{6,8},{8,6},{10,12},{12,10},{14,16},{16,14},{18,20},{2... | collective-permute-start | bytes 30728 | tf_op jit(solution)/shard_map/ppermute | solution.py:135
  27.0 0.1 collective-permute-start.10
  27.1 1.3 %inner.7.acc_ref = f32[6,16,320]{2,1,0:T(8,128)S(1)} custom-call(s32[1,6,3]{2,1,0:T(8,128)S(1)} %copy.19.offsets_ref, bf16[6,16,320]{2,1,0:T(8,128)(2,1)S(1)} %get-tuple-element.24.v_ref.refs_3_, bf16[6,3,320,320]{3,2,1,0:T(8,128)(2,1)S(1)} %bitcast.14), custom_call_target="tpu_custom_call" | custom-call | flops 58982400 | bytes 3686400 | tf_op jit(solution)/shard_map/inner/pallas_call | solution.py:153
  28.5 1.0 %collective-permute-done.9.side_ref = bf16[16,320]{1,0:T(8,128)(2,1)S(1)} collective-permute-done((bf16[16,320]{1,0:T(8,128)(2,1)S(1)}, bf16[16,320]{1,0:T(8,128)(2,1)S(1)}, u32[]{:S(2)}, u32[]{:S(2)}) %collective-permute-start.9) | collective-permute-done | bytes 10272 | tf_op jit(solution)/shard_map/ppermute | solution.py:135
  29.5 1.6 %outer.7 = (bf16[6,16,320]{2,1,0:T(8,128)(2,1)S(1)}, bf16[16,320]{1,0:T(8,128)(2,1)}, bf16[16,320]{1,0:T(8,128)(2,1)}) custom-call(s32[1,6,3]{2,1,0:T(8,128)S(1)} %copy.19.offsets_ref, s32[1,1,2,2]{3,2,1,0:T(2,128)S(1)} %copy-done.4, s32[1,1,2,2]{3,2,1,0:T(2,128)S(1)} %copy-done.5, f32[1,1,2,2]{3,2,1,0:T(2,128)S(1)} %copy-done.6, s32[1,1,2]{2,1,0:T(1,128)S(1)} %copy-done.7, ...), custom_call_target="tpu_custom_call" | custom-call | tf_op jit(solution)/shard_map/outer/pallas_call | solution.py:158
  31.1 0.3 gram.1
  31.5 1.2 %collective-permute-done.12 = f32[16,128]{1,0:T(8,128)S(1)} collective-permute-done((f32[16,128]{1,0:T(8,128)S(1)}, f32[16,128]{1,0:T(8,128)S(1)}, u32[]{:S(2)}, u32[]{:S(2)}) %collective-permute-start.12) | collective-permute-done | bytes 8224 | tf_op jit(solution)/shard_map/ppermute | solution.py:171
  32.7 14.6 %all_to_all.5 = f32[16,16,128]{2,1,0:T(8,128)S(1)} all-to-all(f32[16,16,128]{2,1,0:T(8,128)S(1)} %broadcast_in_dim.10), channel_id=1, replica_groups=mesh['chip'=8,'core'=2,'grid'=2] {'chip','grid'}, dimensions={0} | all-to-all | bytes 262144 | tf_op jit(solution)/shard_map/all_to_all | solution.py:172
  47.5 0.7 %copy.26 = bf16[1,6,4,16,320]{4,3,2,1,0:T(8,128)(2,1)} copy(bf16[1,6,4,16,320]{4,3,1,2,0:T(8,128)(2,1)S(1)} %maximum_bitcast_fusion) | data formatting | bytes 491520
  48.2 0.3 collective-permute-done.13.other_ref
  48.6 7.4 %factor.1 = f32[80,80]{1,0:T(8,128)} custom-call(f32[16,128]{1,0:T(8,128)S(1)} %reduce_sum.9.mine_ref, f32[16,128]{1,0:T(8,128)S(1)} %collective-permute-done.13.other_ref), custom_call_target="tpu_custom_call" | custom-call | tf_op jit(solution)/shard_map/factor/pallas_call | solution.py:177
  (30 shorter events, 0.4 us)
Async XLA Ops:
  0.6 10.9 %copy-start.7 = (s32[1,1,2]{2,1,0:T(1,128)S(1)}, s32[1,1,2]{2,1,0:T(1,128)}, u32[]{:S(2)}) copy-start(s32[1,1,2]{2,1,0:T(1,128)} %live_ref.7) | copy-start | bytes 28
  0.6 10.9 %copy-start.4 = (s32[1,1,2,2]{3,2,1,0:T(2,128)S(1)}, s32[1,1,2,2]{3,2,1,0:T(2,128)}, u32[]{:S(2)}) copy-start(s32[1,1,2,2]{3,2,1,0:T(2,128)} %donor_ref.7) | copy-start | bytes 52
  0.7 10.9 %collective-permute-start.2 = (bf16[6,16,320]{2,1,0:T(8,128)(2,1)}, bf16[6,16,320]{2,1,0:T(8,128)(2,1)S(1)}, u32[]{:S(2)}, u32[]{:S(2)}) collective-permute-start(bf16[6,16,320]{2,1,0:T(8,128)(2,1)} %bitcast.19), channel_id=1, source_target_pairs={{0,1},{1,0},{2,3},{3,2},{4,5},{5,4},{6,7},{7,6},{8,9},{9,8},{10,11... | collective-permute-start | bytes 184328 | tf_op jit(solution)/shard_map/ppermute | solution.py:132
  3.7 0.9 %copy-start.2 = (bf16[1,6,16,320]{3,2,1,0:T(8,128)(2,1)S(1)}, bf16[1,6,16,320]{3,2,1,0:T(8,128)(2,1)}, u32[]{:S(2)}) copy-start(bf16[1,6,16,320]{3,2,1,0:T(8,128)(2,1)} %param.7) | copy-start | bytes 184324
  4.6 7.0 %copy-start.5 = (s32[1,1,2,2]{3,2,1,0:T(2,128)S(1)}, s32[1,1,2,2]{3,2,1,0:T(2,128)}, u32[]{:S(2)}) copy-start(s32[1,1,2,2]{3,2,1,0:T(2,128)} %fringe_ref.7) | copy-start | bytes 52
  4.6 7.0 %copy-start.6 = (f32[1,1,2,2]{3,2,1,0:T(2,128)S(1)}, f32[1,1,2,2]{3,2,1,0:T(2,128)}, u32[]{:S(2)}) copy-start(f32[1,1,2,2]{3,2,1,0:T(2,128)} %weight_ref.7) | copy-start | bytes 52
  4.6 6.9 %collective-permute-start = (bf16[16,320]{1,0:T(8,128)(2,1)S(1)}, bf16[16,320]{1,0:T(8,128)(2,1)S(1)}, u32[]{:S(2)}, u32[]{:S(2)}) collective-permute-start(bf16[16,320]{1,0:T(8,128)(2,1)S(1)} %get-tuple-element.16), channel_id=1, source_target_pairs={{2,4},{4,2},{6,8},{8,6},{10,12},{12,10},{14,16},{16,14},{18,20},{2... | collective-permute-start | bytes 30728 | tf_op jit(solution)/shard_map/ppermute | solution.py:135
  4.7 6.9 %collective-permute-start.1 = (bf16[16,320]{1,0:T(8,128)(2,1)S(1)}, bf16[16,320]{1,0:T(8,128)(2,1)S(1)}, u32[]{:S(2)}, u32[]{:S(2)}) collective-permute-start(bf16[16,320]{1,0:T(8,128)(2,1)S(1)} %get-tuple-element.17), channel_id=1, source_target_pairs={{0,2},{2,0},{1,3},{3,1},{4,6},{6,4},{5,7},{7,5},{8,10},{10,8},{9,1... | collective-permute-start | bytes 30728 | tf_op jit(solution)/shard_map/ppermute | solution.py:135
  7.1 2.3 %copy-start = (bf16[1,6,3,320,320]{4,3,2,1,0:T(8,128)(2,1)S(1)}, bf16[1,6,3,320,320]{4,3,2,1,0:T(8,128)(2,1)}, u32[]{:S(2)}) copy-start(bf16[1,6,3,320,320]{4,3,2,1,0:T(8,128)(2,1)} %param.8) | copy-start | bytes 11059204
  9.3 0.9 %copy-start.3 = (bf16[1,6,16,320]{3,2,1,0:T(8,128)(2,1)S(1)}, bf16[1,6,16,320]{3,2,1,0:T(8,128)(2,1)}, u32[]{:S(2)}) copy-start(bf16[1,6,16,320]{3,2,1,0:T(8,128)(2,1)} %param.7) | copy-start | bytes 184324
  10.2 2.3 %copy-start.1 = (bf16[1,6,3,320,320]{4,3,2,1,0:T(8,128)(2,1)S(1)}, bf16[1,6,3,320,320]{4,3,2,1,0:T(8,128)(2,1)}, u32[]{:S(2)}) copy-start(bf16[1,6,3,320,320]{4,3,2,1,0:T(8,128)(2,1)} %param.8) | copy-start | bytes 11059204
  13.5 4.6 %collective-permute-start.5 = (bf16[6,16,320]{2,1,0:T(8,128)(2,1)S(1)}, bf16[6,16,320]{2,1,0:T(8,128)(2,1)S(1)}, u32[]{:S(2)}, u32[]{:S(2)}) collective-permute-start(bf16[6,16,320]{2,1,0:T(8,128)(2,1)S(1)} %get-tuple-element.18.v_ref.refs_1_), channel_id=1, source_target_pairs={{0,1},{1,0},{2,3},{3,2},{4,5},{5,4},{6,7},{7,6},{8,9},{9,8},{10,11... | collective-permute-start | bytes 184328 | tf_op jit(solution)/shard_map/ppermute | solution.py:132
  13.9 4.1 %collective-permute-start.3 = (bf16[16,320]{1,0:T(8,128)(2,1)S(1)}, bf16[16,320]{1,0:T(8,128)(2,1)S(1)}, u32[]{:S(2)}, u32[]{:S(2)}) collective-permute-start(bf16[16,320]{1,0:T(8,128)(2,1)S(1)} %get-tuple-element.19), channel_id=1, source_target_pairs={{2,4},{4,2},{6,8},{8,6},{10,12},{12,10},{14,16},{16,14},{18,20},{2... | collective-permute-start | bytes 30728 | tf_op jit(solution)/shard_map/ppermute | solution.py:135
  15.5 2.5 %collective-permute-start.4 = (bf16[16,320]{1,0:T(8,128)(2,1)S(1)}, bf16[16,320]{1,0:T(8,128)(2,1)S(1)}, u32[]{:S(2)}, u32[]{:S(2)}) collective-permute-start(bf16[16,320]{1,0:T(8,128)(2,1)S(1)} %get-tuple-element.20), channel_id=1, source_target_pairs={{0,2},{2,0},{1,3},{3,1},{4,6},{6,4},{5,7},{7,5},{8,10},{10,8},{9,1... | collective-permute-start | bytes 30728 | tf_op jit(solution)/shard_map/ppermute | solution.py:135
  19.0 4.9 %collective-permute-start.8 = (bf16[6,16,320]{2,1,0:T(8,128)(2,1)S(1)}, bf16[6,16,320]{2,1,0:T(8,128)(2,1)S(1)}, u32[]{:S(2)}, u32[]{:S(2)}) collective-permute-start(bf16[6,16,320]{2,1,0:T(8,128)(2,1)S(1)} %get-tuple-element.21.v_ref.refs_2_), channel_id=1, source_target_pairs={{0,1},{1,0},{2,3},{3,2},{4,5},{5,4},{6,7},{7,6},{8,9},{9,8},{10,11... | collective-permute-start | bytes 184328 | tf_op jit(solution)/shard_map/ppermute | solution.py:132
  20.2 3.7 %collective-permute-start.6 = (bf16[16,320]{1,0:T(8,128)(2,1)S(1)}, bf16[16,320]{1,0:T(8,128)(2,1)S(1)}, u32[]{:S(2)}, u32[]{:S(2)}) collective-permute-start(bf16[16,320]{1,0:T(8,128)(2,1)S(1)} %get-tuple-element.22), channel_id=1, source_target_pairs={{2,4},{4,2},{6,8},{8,6},{10,12},{12,10},{14,16},{16,14},{18,20},{2... | collective-permute-start | bytes 30728 | tf_op jit(solution)/shard_map/ppermute | solution.py:135
  21.1 2.8 %collective-permute-start.7 = (bf16[16,320]{1,0:T(8,128)(2,1)S(1)}, bf16[16,320]{1,0:T(8,128)(2,1)S(1)}, u32[]{:S(2)}, u32[]{:S(2)}) collective-permute-start(bf16[16,320]{1,0:T(8,128)(2,1)S(1)} %get-tuple-element.23), channel_id=1, source_target_pairs={{0,2},{2,0},{1,3},{3,1},{4,6},{6,4},{5,7},{7,5},{8,10},{10,8},{9,1... | collective-permute-start | bytes 30728 | tf_op jit(solution)/shard_map/ppermute | solution.py:135
  24.9 4.6 %collective-permute-start.11 = (bf16[6,16,320]{2,1,0:T(8,128)(2,1)S(1)}, bf16[6,16,320]{2,1,0:T(8,128)(2,1)S(1)}, u32[]{:S(2)}, u32[]{:S(2)}) collective-permute-start(bf16[6,16,320]{2,1,0:T(8,128)(2,1)S(1)} %get-tuple-element.24.v_ref.refs_3_), channel_id=1, source_target_pairs={{0,1},{1,0},{2,3},{3,2},{4,5},{5,4},{6,7},{7,6},{8,9},{9,8},{10,11... | collective-permute-start | bytes 184328 | tf_op jit(solution)/shard_map/ppermute | solution.py:132
  25.8 3.7 %collective-permute-start.9 = (bf16[16,320]{1,0:T(8,128)(2,1)S(1)}, bf16[16,320]{1,0:T(8,128)(2,1)S(1)}, u32[]{:S(2)}, u32[]{:S(2)}) collective-permute-start(bf16[16,320]{1,0:T(8,128)(2,1)S(1)} %get-tuple-element.25), channel_id=1, source_target_pairs={{2,4},{4,2},{6,8},{8,6},{10,12},{12,10},{14,16},{16,14},{18,20},{2... | collective-permute-start | bytes 30728 | tf_op jit(solution)/shard_map/ppermute | solution.py:135
  27.0 2.5 %collective-permute-start.10 = (bf16[16,320]{1,0:T(8,128)(2,1)S(1)}, bf16[16,320]{1,0:T(8,128)(2,1)S(1)}, u32[]{:S(2)}, u32[]{:S(2)}) collective-permute-start(bf16[16,320]{1,0:T(8,128)(2,1)S(1)} %get-tuple-element.26), channel_id=1, source_target_pairs={{0,2},{2,0},{1,3},{3,1},{4,6},{6,4},{5,7},{7,5},{8,10},{10,8},{9,1... | collective-permute-start | bytes 30728 | tf_op jit(solution)/shard_map/ppermute | solution.py:135
  31.4 1.2 %collective-permute-start.12 = (f32[16,128]{1,0:T(8,128)S(1)}, f32[16,128]{1,0:T(8,128)S(1)}, u32[]{:S(2)}, u32[]{:S(2)}) collective-permute-start(f32[16,128]{1,0:T(8,128)S(1)} %get-tuple-element.29), channel_id=1, source_target_pairs={{0,2},{2,0},{1,3},{3,1},{4,6},{6,4},{5,7},{7,5},{8,10},{10,8},{9,1... | collective-permute-start | bytes 24584 | tf_op jit(solution)/shard_map/ppermute | solution.py:171
  47.3 1.2 %collective-permute-start.13 = (f32[16,128]{1,0:T(8,128)S(1)}, f32[16,128]{1,0:T(8,128)S(1)}, u32[]{:S(2)}, u32[]{:S(2)}) collective-permute-start(f32[16,128]{1,0:T(8,128)S(1)} %reduce_sum.9.mine_ref), channel_id=1, source_target_pairs={{0,2},{2,0},{1,3},{3,1},{4,6},{6,4},{5,7},{7,5},{8,10},{10,8},{9,1... | collective-permute-start | bytes 24584 | tf_op jit(solution)/shard_map/ppermute | solution.py:174

commit v2 on v1

v2 whole, which is shorter than its diff:
```python
import functools

import jax
import jax.numpy as jnp
from jax import lax
from jax.experimental import pallas as pl
from jax.experimental.pallas import tpu as pltpu
from jax.sharding import Mesh
from jax.sharding import PartitionSpec as P

S = 4
H = 1
CORES = 2

VMEM = pl.BlockSpec(memory_space=pltpu.VMEM)
HBM = pl.BlockSpec(memory_space=pltpu.HBM)
SMEM = pl.BlockSpec(memory_space=pltpu.SMEM)


def start_kernel(*refs):
    sources, rest = refs[:6], refs[6:]
    targets, side_ref, chip_ref, sems = rest[:6], rest[6], rest[7], rest[8]
    copies = [pltpu.make_async_copy(a, b, sems.at[i]) for i, (a, b) in enumerate(zip(sources, targets))]
    for copy in copies:
        copy.start()
    copies[0].wait()
    v_ref = targets[0]
    last = v_ref.shape[0] - 1
    core = lax.axis_index("core")
    side_ref[...] = v_ref[core * last]
    chip_ref[...] = v_ref[(1 - core) * last]
    for copy in copies[1:]:
        copy.wait()


def inner_products(offsets_ref, v_ref, chip_ref, acc_ref, block_of):
    count, kinds = v_ref.shape[0], offsets_ref.shape[0]
    core = lax.axis_index("core")
    for e in range(count):
        total = None
        get = block_of(e)
        for k in range(kinds):
            col = e + offsets_ref[k, 0, e]
            inside = jnp.logical_and(col >= 0, col < count)
            lhs = v_ref[jnp.clip(col, 0, count - 1)]
            if e == 0 or e == count - 1:
                halo = jnp.logical_or(
                    jnp.logical_and(col < 0, core == 1), jnp.logical_and(col >= count, core == 0)
                )
                lhs = jnp.where(inside, lhs, jnp.where(halo, chip_ref[...], jnp.zeros_like(lhs)))
            part = jnp.dot(lhs, get(k), preferred_element_type=jnp.float32)
            total = part if total is None else total + part
        acc_ref[e] = total


def first_inner_kernel(offsets_ref, v_ref, chip_ref, source_ref, acc_ref, blocks_ref, sems):
    count = v_ref.shape[0]
    copies = [pltpu.make_async_copy(source_ref.at[e], blocks_ref.at[e], sems.at[e]) for e in range(count)]
    for copy in copies:
        copy.start()

    def block_of(e):
        copies[e].wait()
        return lambda k: blocks_ref[e, k]

    inner_products(offsets_ref, v_ref, chip_ref, acc_ref, block_of)


def inner_kernel(offsets_ref, v_ref, chip_ref, blocks_ref, acc_ref):
    inner_products(offsets_ref, v_ref, chip_ref, acc_ref, lambda e: lambda k: blocks_ref[e, k])


def outer_kernel(
    grids, offsets_ref, donor_ref, fringe_ref, weight_ref, live_ref,
    acc_ref, blocks_ref, halo_ref, *rest
):
    others, (v_ref, *edges, total_ref) = rest[: grids - 1], rest[grids - 1 :]
    count, kinds = blocks_ref.shape[:2]
    last = count - 1
    chips = lax.axis_size("chip")
    chip, core, grid = (lax.axis_index(a) for a in ("chip", "core", "grid"))
    for e in range(count):
        total_ref[e] = acc_ref[e]
    there = jnp.where(core == 0, chip > 0, chip < chips - 1)
    edge = core * last
    total = total_ref[edge]
    for k in range(kinds):
        used = jnp.logical_and(offsets_ref[k, 0, edge] == jnp.where(core == 0, -H, H), there)
        lhs = jnp.where(used, halo_ref[...], jnp.zeros_like(halo_ref))
        total += jnp.dot(lhs, blocks_ref[edge, k], preferred_element_type=jnp.float32)
    total_ref[edge] = total
    for s, other in enumerate(others):
        g = lax.rem(grid + grids - 1 - s, grids)
        for c in range(donor_ref.shape[3]):
            f = fringe_ref[0, 0, g, c]
            weight = jnp.where(c < live_ref[0, 0, g], weight_ref[0, 0, g, c], 0.0)
            total_ref[f] += weight * other[donor_ref[0, 0, g, c]].astype(jnp.float32)
    for e in range(count):
        v_ref[e] = total_ref[e].astype(jnp.bfloat16)
    for edge_ref, edge in zip(edges, (core * last, (1 - core) * last)):
        edge_ref[...] = v_ref[edge]


def gram_kernel(*refs):
    fields, (keep_ref, send_ref) = refs[: S + 1], refs[S + 1 :]
    count, n = fields[0].shape[:2]
    total = None
    for e in range(count):
        rows = jnp.concatenate([f[e] for f in fields], axis=0)
        part = lax.dot_general(rows, rows, (((1,), (1,)), ((), ())), preferred_element_type=jnp.float32)
        total = part if total is None else total + part
    b = lambda i, j0, j1: total[i * n : (i + 1) * n, j0 * n : j1 * n]
    one = jnp.concatenate([b(4, 0, 5), b(3, 0, 3)], axis=1)
    two = jnp.concatenate([b(3, 3, 4), b(2, 0, 3), b(1, 0, 2), b(0, 0, 1), jnp.zeros((n, n), jnp.float32)], axis=1)
    first = lax.axis_index("core") == 0
    keep_ref[...] = jnp.where(first, one, two)
    send_ref[...] = jnp.where(first, two, one)


def cholesky_rows(panels, height, r_ref):
    size = len(panels) * height
    lane = lax.broadcasted_iota(jnp.int32, (1, size), 1)
    panels = list(panels)
    for q in range(len(panels)):
        later = range(q, len(panels))
        wide = lambda p, c: jnp.broadcast_to(panels[p][:, q * height + c : q * height + c + 1], (height, size))
        side = {(c, p): wide(p, c) for c in range(height) for p in later}
        for c in range(0, height, 2):
            one, two = panels[q][c : c + 1], panels[q][c + 1 : c + 2]
            a, b, d = side[c, q][c : c + 1], side[c + 1, q][c : c + 1], side[c + 1, q][c + 1 : c + 2]
            det = a * d - b * b
            inv_det = 1.0 / det
            root = lax.rsqrt(a)
            inv_a = root * root
            j = q * height + c
            r_ref[j : j + 1, :] = jnp.where(lane >= j, one * root, 0.0)
            second = (two - (b * inv_a) * one) * lax.rsqrt(det * inv_a)
            r_ref[j + 1 : j + 2, :] = jnp.where(lane >= j + 1, second, 0.0)
            if c + 2 == height and q + 1 == len(panels):
                break
            tops = [(side[e, q][c : c + 1], side[e, q][c + 1 : c + 2]) for e in range(c + 2, height)]
            for p in later:
                if p == q and c + 2 == height:
                    continue
                x, y = side[c, p], side[c + 1, p]
                w_one, w_two = (d * x - b * y) * inv_det, (a * y - b * x) * inv_det
                panels[p] = panels[p] - w_one * one - w_two * two
                for e, (t_one, t_two) in zip(range(c + 2, height), tops):
                    side[e, p] = side[e, p] - w_one * t_one - w_two * t_two


def factor_kernel(scale, mine_ref, other_ref, r_ref):
    first = lax.axis_index("core") == 0
    mine, other = mine_ref[...] * scale, other_ref[...] * scale
    one, two = jnp.where(first, mine, other), jnp.where(first, other, mine)
    n = one.shape[0]
    size = (S + 1) * n
    b = lambda x, j0, j1: x[:, j0 * n : j1 * n]
    wide = lambda x: jnp.concatenate([x, jnp.zeros((n, size - x.shape[1]), jnp.float32)], axis=1)
    low = jnp.concatenate([
        wide(b(two, 6, 7)),
        wide(b(two, 4, 6)),
        wide(b(two, 1, 4)),
        wide(jnp.concatenate([b(one, 5, 8), b(two, 0, 1)], axis=1)),
        b(one, 0, 5),
    ], axis=0)
    row = lax.broadcasted_iota(jnp.int32, (size, size), 0)
    col = lax.broadcasted_iota(jnp.int32, (size, size), 1)
    a = jnp.where(row >= col, low, low.T)
    height = 8
    cholesky_rows([a[i : i + height] for i in range(0, size, height)], height, r_ref)


def local(rhs, blocks, offsets, donor_elem, fringe_elem, donor_weight, fringe_count):
    _, elem_count, n, unknowns = rhs.shape
    chips, cores, grids = (lax.axis_size(a) for a in ("chip", "core", "grid"))
    axes = ("chip", "core", "grid")
    at = lambda chip, core, grid: (chip * cores + core) * grids + grid % grids
    side = []
    for g in range(grids):
        for chip in range(chips - 1):
            side += [(at(chip, 1, g), at(chip + 1, 0, g)), (at(chip + 1, 0, g), at(chip, 1, g))]
        side += [(at(0, 0, g), at(0, 0, g + 1)), (at(chips - 1, 1, g), at(chips - 1, 1, g + 1))]
    swap = [(0, 1), (1, 0)]

    def exchange(v, to_side, to_chip):
        from_chip = lax.ppermute(to_chip, "core", swap)
        others = [
            lax.ppermute(v, "grid", [(g, (g + s) % grids) for g in range(grids)])
            for s in range(1, grids)
        ]
        return lax.ppermute(to_side, axes, side), from_chip, others

    halo_type = jax.ShapeDtypeStruct((n, unknowns), jnp.bfloat16)
    field_type = jax.ShapeDtypeStruct((elem_count, n, unknowns), jnp.bfloat16)
    acc_type = jax.ShapeDtypeStruct((elem_count, n, unknowns), jnp.float32)
    half_type = jax.ShapeDtypeStruct((n, 8 * n), jnp.float32)
    limit = pltpu.CompilerParams(vmem_limit_bytes=24 << 20)
    flops = 2 * elem_count * n * unknowns * unknowns * blocks.shape[2]

    kinds = blocks.shape[2]
    by_kind = jnp.transpose(offsets, (2, 0, 1))
    small = (by_kind, donor_elem, fringe_elem, donor_weight, fringe_count)
    field, *small, side_edge, chip_edge = pl.pallas_call(
        start_kernel,
        out_shape=(field_type, *(pltpu.SMEM(x.shape, x.dtype) for x in small), halo_type, halo_type),
        in_specs=[HBM] * 6, out_specs=(VMEM, *[SMEM] * 5, VMEM, VMEM),
        scratch_shapes=[pltpu.SemaphoreType.DMA((6,))],
        compiler_params=limit, name="start",
    )(*(pltpu.with_memory_space_constraint(x, pltpu.HBM) for x in (rhs[0], *small)))
    edges = (side_edge, chip_edge)
    basis = [field]
    stored = None
    for level in range(S):
        from_side, from_chip, others = exchange(field, *edges)
        cost = pl.CostEstimate(flops=flops, bytes_accessed=blocks.size * 2, transcendentals=0)
        if level == 0:
            acc, stored = pl.pallas_call(
                first_inner_kernel,
                out_shape=(acc_type, pltpu.VMEM(blocks.shape[1:], blocks.dtype)),
                in_specs=[SMEM, VMEM, VMEM, HBM], out_specs=(VMEM, VMEM),
                scratch_shapes=[pltpu.SemaphoreType.DMA((elem_count,))],
                compiler_params=limit, name="first_inner", cost_estimate=cost,
            )(small[0], field, from_chip, pltpu.with_memory_space_constraint(blocks[0], pltpu.HBM))
        else:
            acc = pl.pallas_call(
                inner_kernel, out_shape=acc_type, in_specs=[SMEM, VMEM, VMEM, VMEM], out_specs=VMEM,
                compiler_params=limit, name="inner", cost_estimate=cost,
            )(small[0], field, from_chip, stored)
        edges = 2 if level + 1 < S else 0
        field, *edges = pl.pallas_call(
            functools.partial(outer_kernel, grids),
            out_shape=(field_type, *[halo_type] * edges),
            in_specs=[SMEM] * 5 + [VMEM] * (3 + grids - 1),
            out_specs=(VMEM, *[VMEM] * edges),
            scratch_shapes=[pltpu.VMEM((elem_count, n, unknowns), jnp.float32)],
            compiler_params=limit, name="outer",
        )(*small, acc, stored, from_side, *others)
        basis.append(field)
    keep, send = pl.pallas_call(
        gram_kernel, out_shape=(half_type, half_type), in_specs=[VMEM] * (S + 1), out_specs=(VMEM, VMEM),
        compiler_params=limit, name="gram",
    )(*basis)
    half = keep + lax.ppermute(send, "core", swap)
    parts = lax.all_to_all(jnp.broadcast_to(half[None], (chips * grids, n, 8 * n)), ("chip", "grid"), 0, 0, tiled=True)
    mine = parts.sum(axis=0)
    other = lax.ppermute(mine, "core", swap)
    columns = (S + 1) * n
    row_total = grids * chips * cores * elem_count * unknowns
    r_factor = pl.pallas_call(
        functools.partial(factor_kernel, 1.0 / row_total),
        out_shape=jax.ShapeDtypeStruct((columns, columns), jnp.float32),
        in_specs=[VMEM] * 2, out_specs=VMEM,
        compiler_params=limit, name="factor",
    )(mine, other)
    powers = jnp.stack(basis[1:], axis=1)[None]
    return (powers, r_factor)


def solution(mesh):
    dom, grids = mesh.shape["dom"], mesh.shape["grid"]
    split = Mesh(mesh.devices.reshape(dom // CORES, CORES, grids), ("chip", "core", "grid"))
    where = ("chip", "core")
    in_specs = (
        P("grid", where, None, None),
        P("grid", where, None, None, None),
        P("grid", where, None),
        P("grid", where, None, None),
        P("grid", where, None, None),
        P("grid", where, None, None),
        P("grid", where, None),
    )
    out_specs = (P("grid", where, None, None, None), P())
    return jax.shard_map(local, mesh=split, in_specs=in_specs, out_specs=out_specs, check_vma=False)
```

time: 56.5 us -> 44.2 us (0.78)
  Pallas kernels: 17.7 us -> 10.1 us
  local copies, waits for them, and re-layouts: 6.45 us -> 0.76 us
  waiting for transfers between devices: 4.95 us -> 8.16 us
  starting transfers between devices: 11.4 us -> 9.86 us
    unnamed x18 -> x1, local copies, waits for them, and re-layouts: 6.44 us -> 0.75 us
    pallas_call x1, Pallas kernels: 7.41 us -> 2.82 us  [local(): pl.pallas_call(functools.partial(factor_kernel, 1.0 / row_total), out_sha...]
    pallas_call x1 -> x2, Pallas kernels: 0.01 us -> 3.76 us  [the longest x1 2.78 us: local(): pl.pallas_call(first_inner_kernel, out_shape=(acc_type, pltpu.VMEM(blocks...]
    pallas_call x4, Pallas kernels: 4.65 us -> 0.98 us  [local(): pl.pallas_call(functools.partial(outer_kernel, grids), out_shape=(field_t...]
    ppermute x8, waiting for transfers between devices: 3.44 us -> 6.76 us  [the longest x4 5.41 us: exchange(): return (lax.ppermute(to_side, axes, side), from_chip, others)]
    pallas_call x4 -> x3, Pallas kernels: 5.3 us -> 2.18 us  [local(): pl.pallas_call(inner_kernel, out_shape=acc_type, in_specs=[SMEM, VMEM, VM...]
    ppermute x8, starting transfers between devices: 5.74 us -> 3.54 us  [the longest x4 3.53 us: exchange(): return (lax.ppermute(to_side, axes, side), from_chip, others)]
  transfers between devices with their start and end apart: 14 -> 14, of which waited for: 5 -> 7; matrix products, arithmetic and copies ran while one was open for 3% -> 2% of each run, Pallas kernels for 9% -> 11%
where the time goes in v2:
time: 44.2 us; the launch traced here: 44 us
  blocking collectives  14.3 us (32%)
  Pallas kernels  10.1 us (23%)
  starting transfers between devices  9.86 us (22%)
  waiting for transfers between devices  8.16 us (18%)
  local copies, waits for them, and re-layouts  0.76 us (2%)
  between operations  0.72 us (2%)
    all_to_all x1, blocking collectives, local(): lax.all_to_all(jnp.broadcast_to(half[None], (chips * grids, n, 8 * n)), (...  14.3 us
    ppermute x4, starting transfers between devices, exchange(): lax.ppermute(v, 'grid', [(g, (g + s) % grids) for g in range(grids)])  6.09 us
    ppermute x4, waiting for transfers between devices, exchange(): return (lax.ppermute(to_side, axes, side), from_chip, others)  5.41 us
    ppermute x4, starting transfers between devices, exchange(): return (lax.ppermute(to_side, axes, side), from_chip, others)  3.53 us
    pallas_call x1, Pallas kernels, local(): pl.pallas_call(functools.partial(factor_kernel, 1.0 / row_total), out_sha...  2.82 us
    pallas_call x1, Pallas kernels, local(): pl.pallas_call(first_inner_kernel, out_shape=(acc_type, pltpu.VMEM(blocks...  2.78 us
    pallas_call x3, Pallas kernels, local(): pl.pallas_call(inner_kernel, out_shape=acc_type, in_specs=[SMEM, VMEM, VM...  2.18 us
    ppermute x4, waiting for transfers between devices, exchange(): from_chip = lax.ppermute(to_chip, 'core', swap)  1.35 us
  transfers between devices with their start and end apart: 14, of which 7 were waited for; matrix products, arithmetic and copies ran while one was open for 2% of the time, Pallas kernels for 11%

profile of v2, /device:TPU:0, one launch (start us, length us, event | category | flops | bytes accessed | tf_op | source)
XLA Modules:
  0.0 44.0 jit_solution(3234428850989956306)
XLA Ops:
  0.6 1.0 %start.1 = (bf16[6,16,320]{2,1,0:T(8,128)(2,1)S(1)}, s32[3,1,6]{2,1,0:T(1,128)S(4)}, s32[1,1,2,2]{3,2,1,0:T(2,128)S(4)}, s32[1,1,2,2]{3,2,1,0:T(2,128)S(4)}, f32...) custom-call(bf16[6,16,320]{2,1,0:T(8,128)(2,1)} %bitcast.14, ...), custom_call_target="tpu_custom_call" | custom-call | tf_op jit(solution)/shard_map/start/pallas_call | solution.py:204
  1.6 3.0 %collective-permute-start.2 = (bf16[6,16,320]{2,1,0:T(8,128)(2,1)S(1)}, bf16[6,16,320]{2,1,0:T(8,128)(2,1)S(1)}, u32[]{:S(2)}, u32[]{:S(2)}) collective-permute-start(bf16[6,16,320]{2,1,0:T(8,128)(2,1)S(1)} %get-tuple-element.28.v_ref.refs_0_), channel_id=1, source_target_pairs={{0,1},{1,0},{2,3},{3,2},{4,5},{5,4},{6,7},{7,6},{8,9},{9,8},{10,11... | collective-permute-start | bytes 184328 | tf_op jit(solution)/shard_map/ppermute | solution.py:189
  4.6 0.2 collective-permute-start.1
  4.8 1.0 %collective-permute-done.chip_ref = bf16[16,320]{1,0:T(8,128)(2,1)S(1)} collective-permute-done((bf16[16,320]{1,0:T(8,128)(2,1)S(1)}, bf16[16,320]{1,0:T(8,128)(2,1)S(1)}, u32[]{:S(2)}, u32[]{:S(2)}) %collective-permute-start) | collective-permute-done | bytes 10272 | tf_op jit(solution)/shard_map/ppermute | solution.py:187
  5.8 2.8 %first_inner.1 = (f32[6,16,320]{2,1,0:T(8,128)S(1)}, bf16[6,3,320,320]{3,2,1,0:T(8,128)(2,1)S(1)}) custom-call(s32[3,1,6]{2,1,0:T(1,128)S(4)} %get-tuple-element.23.offsets_ref, bf16[6,16,320]{2,1,0:T(8,128)(2,1)S(1)} %get-tuple-element.28.v_ref.refs_0_, bf16[16,320]{1,0:T(8,128)(2,1)S(1)} %collective-permute-done.chip_ref, bf16[6,3,320,320]{3,2,1,0:T(8,128)(2,1)} %bitcast.13), custom_call_target="tpu_custom_call" | custom-call | flops 58982400 | bytes 3686400 | tf_op jit(solution)/shard_map/first_inner/pallas_call | solution.py:218
  8.6 0.3 outer.4
  8.9 0.9 %collective-permute-start.5 = (bf16[6,16,320]{2,1,0:T(8,128)(2,1)S(1)}, bf16[6,16,320]{2,1,0:T(8,128)(2,1)S(1)}, u32[]{:S(2)}, u32[]{:S(2)}) collective-permute-start(bf16[6,16,320]{2,1,0:T(8,128)(2,1)S(1)} %get-tuple-element.33.v_ref.refs_1_), channel_id=1, source_target_pairs={{0,1},{1,0},{2,3},{3,2},{4,5},{5,4},{6,7},{7,6},{8,9},{9,8},{10,11... | collective-permute-start | bytes 184328 | tf_op jit(solution)/shard_map/ppermute | solution.py:189
  9.8 1.4 %collective-permute-start.4 = (bf16[16,320]{1,0:T(8,128)(2,1)S(1)}, bf16[16,320]{1,0:T(8,128)(2,1)S(1)}, u32[]{:S(2)}, u32[]{:S(2)}) collective-permute-start(bf16[16,320]{1,0:T(8,128)(2,1)S(1)} %get-tuple-element.35), channel_id=1, source_target_pairs={{2,4},{4,2},{6,8},{8,6},{10,12},{12,10},{14,16},{16,14},{18,20},{2... | collective-permute-start | bytes 30728 | tf_op jit(solution)/shard_map/ppermute | solution.py:192
  11.2 0.7 %inner.3.acc_ref = f32[6,16,320]{2,1,0:T(8,128)S(1)} custom-call(s32[3,1,6]{2,1,0:T(1,128)S(4)} %get-tuple-element.23.offsets_ref, bf16[6,16,320]{2,1,0:T(8,128)(2,1)S(1)} %get-tuple-element.33.v_ref.refs_1_, bf16[16,320]{1,0:T(8,128)(2,1)S(1)} %collective-permute-done.3.chip_ref, bf16[6,3,320,320]{3,2,1,0:T(8,128)(2,1)S(1)} %get-tuple-element.31.blocks_ref), custom_call_target="tpu_custom_call" | custom-call | flops 58982400 | bytes 3686400 | tf_op jit(solution)/shard_map/inner/pallas_call | solution.py:226
  11.9 1.8 %collective-permute-done.4.halo_ref = bf16[16,320]{1,0:T(8,128)(2,1)S(1)} collective-permute-done((bf16[16,320]{1,0:T(8,128)(2,1)S(1)}, bf16[16,320]{1,0:T(8,128)(2,1)S(1)}, u32[]{:S(2)}, u32[]{:S(2)}) %collective-permute-start.4) | collective-permute-done | bytes 10272 | tf_op jit(solution)/shard_map/ppermute | solution.py:192
  13.7 0.2 outer.5
  14.0 1.2 %collective-permute-start.8 = (bf16[6,16,320]{2,1,0:T(8,128)(2,1)S(1)}, bf16[6,16,320]{2,1,0:T(8,128)(2,1)S(1)}, u32[]{:S(2)}, u32[]{:S(2)}) collective-permute-start(bf16[6,16,320]{2,1,0:T(8,128)(2,1)S(1)} %get-tuple-element.36.v_ref.refs_2_), channel_id=1, source_target_pairs={{0,1},{1,0},{2,3},{3,2},{4,5},{5,4},{6,7},{7,6},{8,9},{9,8},{10,11... | collective-permute-start | bytes 184328 | tf_op jit(solution)/shard_map/ppermute | solution.py:189
  15.2 0.9 %collective-permute-start.7 = (bf16[16,320]{1,0:T(8,128)(2,1)S(1)}, bf16[16,320]{1,0:T(8,128)(2,1)S(1)}, u32[]{:S(2)}, u32[]{:S(2)}) collective-permute-start(bf16[16,320]{1,0:T(8,128)(2,1)S(1)} %get-tuple-element.38), channel_id=1, source_target_pairs={{2,4},{4,2},{6,8},{8,6},{10,12},{12,10},{14,16},{16,14},{18,20},{2... | collective-permute-start | bytes 30728 | tf_op jit(solution)/shard_map/ppermute | solution.py:192
  16.1 0.3 collective-permute-done.6.chip_ref
  16.4 0.7 %inner.4.acc_ref = f32[6,16,320]{2,1,0:T(8,128)S(1)} custom-call(s32[3,1,6]{2,1,0:T(1,128)S(4)} %get-tuple-element.23.offsets_ref, bf16[6,16,320]{2,1,0:T(8,128)(2,1)S(1)} %get-tuple-element.36.v_ref.refs_2_, bf16[16,320]{1,0:T(8,128)(2,1)S(1)} %collective-permute-done.6.chip_ref, bf16[6,3,320,320]{3,2,1,0:T(8,128)(2,1)S(1)} %get-tuple-element.31.blocks_ref), custom_call_target="tpu_custom_call" | custom-call | flops 58982400 | bytes 3686400 | tf_op jit(solution)/shard_map/inner/pallas_call | solution.py:226
  17.1 1.8 %collective-permute-done.7.halo_ref = bf16[16,320]{1,0:T(8,128)(2,1)S(1)} collective-permute-done((bf16[16,320]{1,0:T(8,128)(2,1)S(1)}, bf16[16,320]{1,0:T(8,128)(2,1)S(1)}, u32[]{:S(2)}, u32[]{:S(2)}) %collective-permute-start.7) | collective-permute-done | bytes 10272 | tf_op jit(solution)/shard_map/ppermute | solution.py:192
  18.9 0.2 outer.6
  19.1 1.0 %collective-permute-start.11 = (bf16[6,16,320]{2,1,0:T(8,128)(2,1)S(1)}, bf16[6,16,320]{2,1,0:T(8,128)(2,1)S(1)}, u32[]{:S(2)}, u32[]{:S(2)}) collective-permute-start(bf16[6,16,320]{2,1,0:T(8,128)(2,1)S(1)} %get-tuple-element.39.v_ref.refs_3_), channel_id=1, source_target_pairs={{0,1},{1,0},{2,3},{3,2},{4,5},{5,4},{6,7},{7,6},{8,9},{9,8},{10,11... | collective-permute-start | bytes 184328 | tf_op jit(solution)/shard_map/ppermute | solution.py:189
  20.1 1.1 %collective-permute-start.10 = (bf16[16,320]{1,0:T(8,128)(2,1)S(1)}, bf16[16,320]{1,0:T(8,128)(2,1)S(1)}, u32[]{:S(2)}, u32[]{:S(2)}) collective-permute-start(bf16[16,320]{1,0:T(8,128)(2,1)S(1)} %get-tuple-element.41), channel_id=1, source_target_pairs={{2,4},{4,2},{6,8},{8,6},{10,12},{12,10},{14,16},{16,14},{18,20},{2... | collective-permute-start | bytes 30728 | tf_op jit(solution)/shard_map/ppermute | solution.py:192
  21.2 0.0 collective-permute-done.9.chip_ref
  21.3 0.7 %inner.5.acc_ref = f32[6,16,320]{2,1,0:T(8,128)S(1)} custom-call(s32[3,1,6]{2,1,0:T(1,128)S(4)} %get-tuple-element.23.offsets_ref, bf16[6,16,320]{2,1,0:T(8,128)(2,1)S(1)} %get-tuple-element.39.v_ref.refs_3_, bf16[16,320]{1,0:T(8,128)(2,1)S(1)} %collective-permute-done.9.chip_ref, bf16[6,3,320,320]{3,2,1,0:T(8,128)(2,1)S(1)} %get-tuple-element.31.blocks_ref), custom_call_target="tpu_custom_call" | custom-call | flops 58982400 | bytes 3686400 | tf_op jit(solution)/shard_map/inner/pallas_call | solution.py:226
  22.0 1.8 %collective-permute-done.10.halo_ref = bf16[16,320]{1,0:T(8,128)(2,1)S(1)} collective-permute-done((bf16[16,320]{1,0:T(8,128)(2,1)S(1)}, bf16[16,320]{1,0:T(8,128)(2,1)S(1)}, u32[]{:S(2)}, u32[]{:S(2)}) %collective-permute-start.10) | collective-permute-done | bytes 10272 | tf_op jit(solution)/shard_map/ppermute | solution.py:192
  23.8 0.2 outer.7.refs_4_
  24.0 0.3 gram.1
  24.4 0.2 collective-permute-start.12
  24.5 1.1 %collective-permute-done.12 = f32[16,128]{1,0:T(8,128)S(1)} collective-permute-done((f32[16,128]{1,0:T(8,128)S(1)}, f32[16,128]{1,0:T(8,128)S(1)}, u32[]{:S(2)}, u32[]{:S(2)}) %collective-permute-start.12) | collective-permute-done | bytes 8224 | tf_op jit(solution)/shard_map/ppermute | solution.py:244
  25.6 14.3 %all_to_all.5 = f32[16,16,128]{2,1,0:T(8,128)S(1)} all-to-all(f32[16,16,128]{2,1,0:T(8,128)S(1)} %broadcast_in_dim.10), channel_id=1, replica_groups=mesh['chip'=8,'core'=2,'grid'=2] {'chip','grid'}, dimensions={0} | all-to-all | bytes 262144 | tf_op jit(solution)/shard_map/all_to_all | solution.py:245
  39.9 0.1 collective-permute-start.13
  40.0 0.1 maximum_bitcast_fusion
  40.1 0.7 %copy.10 = bf16[1,6,4,16,320]{4,3,2,1,0:T(8,128)(2,1)} copy(bf16[1,6,4,16,320]{4,3,1,2,0:T(8,128)(2,1)S(1)} %maximum_bitcast_fusion) | data formatting | bytes 491520
  40.8 0.3 collective-permute-done.13.other_ref
  41.2 2.8 %factor.1 = f32[80,80]{1,0:T(8,128)} custom-call(f32[16,128]{1,0:T(8,128)S(1)} %reduce_sum.9.mine_ref, f32[16,128]{1,0:T(8,128)S(1)} %collective-permute-done.13.other_ref), custom_call_target="tpu_custom_call" | custom-call | tf_op jit(solution)/shard_map/factor/pallas_call | solution.py:250
  (13 shorter events, 0.1 us)
Async XLA Ops:
  1.6 7.0 %collective-permute-start.2 = (bf16[6,16,320]{2,1,0:T(8,128)(2,1)S(1)}, bf16[6,16,320]{2,1,0:T(8,128)(2,1)S(1)}, u32[]{:S(2)}, u32[]{:S(2)}) collective-permute-start(bf16[6,16,320]{2,1,0:T(8,128)(2,1)S(1)} %get-tuple-element.28.v_ref.refs_0_), channel_id=1, source_target_pairs={{0,1},{1,0},{2,3},{3,2},{4,5},{5,4},{6,7},{7,6},{8,9},{9,8},{10,11... | collective-permute-start | bytes 184328 | tf_op jit(solution)/shard_map/ppermute | solution.py:189
  4.6 1.2 %collective-permute-start = (bf16[16,320]{1,0:T(8,128)(2,1)S(1)}, bf16[16,320]{1,0:T(8,128)(2,1)S(1)}, u32[]{:S(2)}, u32[]{:S(2)}) collective-permute-start(bf16[16,320]{1,0:T(8,128)(2,1)S(1)} %get-tuple-element.29), channel_id=1, source_target_pairs={{0,2},{2,0},{1,3},{3,1},{4,6},{6,4},{5,7},{7,5},{8,10},{10,8},{9,1... | collective-permute-start | bytes 30728 | tf_op jit(solution)/shard_map/ppermute | solution.py:187
  4.6 4.0 %collective-permute-start.1 = (bf16[16,320]{1,0:T(8,128)(2,1)S(1)}, bf16[16,320]{1,0:T(8,128)(2,1)S(1)}, u32[]{:S(2)}, u32[]{:S(2)}) collective-permute-start(bf16[16,320]{1,0:T(8,128)(2,1)S(1)} %get-tuple-element.32), channel_id=1, source_target_pairs={{2,4},{4,2},{6,8},{8,6},{10,12},{12,10},{14,16},{16,14},{18,20},{2... | collective-permute-start | bytes 30728 | tf_op jit(solution)/shard_map/ppermute | solution.py:192
  8.9 4.8 %collective-permute-start.5 = (bf16[6,16,320]{2,1,0:T(8,128)(2,1)S(1)}, bf16[6,16,320]{2,1,0:T(8,128)(2,1)S(1)}, u32[]{:S(2)}, u32[]{:S(2)}) collective-permute-start(bf16[6,16,320]{2,1,0:T(8,128)(2,1)S(1)} %get-tuple-element.33.v_ref.refs_1_), channel_id=1, source_target_pairs={{0,1},{1,0},{2,3},{3,2},{4,5},{5,4},{6,7},{7,6},{8,9},{9,8},{10,11... | collective-permute-start | bytes 184328 | tf_op jit(solution)/shard_map/ppermute | solution.py:189
  9.8 1.4 %collective-permute-start.3 = (bf16[16,320]{1,0:T(8,128)(2,1)S(1)}, bf16[16,320]{1,0:T(8,128)(2,1)S(1)}, u32[]{:S(2)}, u32[]{:S(2)}) collective-permute-start(bf16[16,320]{1,0:T(8,128)(2,1)S(1)} %get-tuple-element.34), channel_id=1, source_target_pairs={{0,2},{2,0},{1,3},{3,1},{4,6},{6,4},{5,7},{7,5},{8,10},{10,8},{9,1... | collective-permute-start | bytes 30728 | tf_op jit(solution)/shard_map/ppermute | solution.py:187
  9.8 3.9 %collective-permute-start.4 = (bf16[16,320]{1,0:T(8,128)(2,1)S(1)}, bf16[16,320]{1,0:T(8,128)(2,1)S(1)}, u32[]{:S(2)}, u32[]{:S(2)}) collective-permute-start(bf16[16,320]{1,0:T(8,128)(2,1)S(1)} %get-tuple-element.35), channel_id=1, source_target_pairs={{2,4},{4,2},{6,8},{8,6},{10,12},{12,10},{14,16},{16,14},{18,20},{2... | collective-permute-start | bytes 30728 | tf_op jit(solution)/shard_map/ppermute | solution.py:192
  14.0 4.9 %collective-permute-start.8 = (bf16[6,16,320]{2,1,0:T(8,128)(2,1)S(1)}, bf16[6,16,320]{2,1,0:T(8,128)(2,1)S(1)}, u32[]{:S(2)}, u32[]{:S(2)}) collective-permute-start(bf16[6,16,320]{2,1,0:T(8,128)(2,1)S(1)} %get-tuple-element.36.v_ref.refs_2_), channel_id=1, source_target_pairs={{0,1},{1,0},{2,3},{3,2},{4,5},{5,4},{6,7},{7,6},{8,9},{9,8},{10,11... | collective-permute-start | bytes 184328 | tf_op jit(solution)/shard_map/ppermute | solution.py:189
  15.2 1.2 %collective-permute-start.6 = (bf16[16,320]{1,0:T(8,128)(2,1)S(1)}, bf16[16,320]{1,0:T(8,128)(2,1)S(1)}, u32[]{:S(2)}, u32[]{:S(2)}) collective-permute-start(bf16[16,320]{1,0:T(8,128)(2,1)S(1)} %get-tuple-element.37), channel_id=1, source_target_pairs={{0,2},{2,0},{1,3},{3,1},{4,6},{6,4},{5,7},{7,5},{8,10},{10,8},{9,1... | collective-permute-start | bytes 30728 | tf_op jit(solution)/shard_map/ppermute | solution.py:187
  15.2 3.7 %collective-permute-start.7 = (bf16[16,320]{1,0:T(8,128)(2,1)S(1)}, bf16[16,320]{1,0:T(8,128)(2,1)S(1)}, u32[]{:S(2)}, u32[]{:S(2)}) collective-permute-start(bf16[16,320]{1,0:T(8,128)(2,1)S(1)} %get-tuple-element.38), channel_id=1, source_target_pairs={{2,4},{4,2},{6,8},{8,6},{10,12},{12,10},{14,16},{16,14},{18,20},{2... | collective-permute-start | bytes 30728 | tf_op jit(solution)/shard_map/ppermute | solution.py:192
  19.1 4.7 %collective-permute-start.11 = (bf16[6,16,320]{2,1,0:T(8,128)(2,1)S(1)}, bf16[6,16,320]{2,1,0:T(8,128)(2,1)S(1)}, u32[]{:S(2)}, u32[]{:S(2)}) collective-permute-start(bf16[6,16,320]{2,1,0:T(8,128)(2,1)S(1)} %get-tuple-element.39.v_ref.refs_3_), channel_id=1, source_target_pairs={{0,1},{1,0},{2,3},{3,2},{4,5},{5,4},{6,7},{7,6},{8,9},{9,8},{10,11... | collective-permute-start | bytes 184328 | tf_op jit(solution)/shard_map/ppermute | solution.py:189
  20.1 1.2 %collective-permute-start.9 = (bf16[16,320]{1,0:T(8,128)(2,1)S(1)}, bf16[16,320]{1,0:T(8,128)(2,1)S(1)}, u32[]{:S(2)}, u32[]{:S(2)}) collective-permute-start(bf16[16,320]{1,0:T(8,128)(2,1)S(1)} %get-tuple-element.40), channel_id=1, source_target_pairs={{0,2},{2,0},{1,3},{3,1},{4,6},{6,4},{5,7},{7,5},{8,10},{10,8},{9,1... | collective-permute-start | bytes 30728 | tf_op jit(solution)/shard_map/ppermute | solution.py:187
  20.1 3.7 %collective-permute-start.10 = (bf16[16,320]{1,0:T(8,128)(2,1)S(1)}, bf16[16,320]{1,0:T(8,128)(2,1)S(1)}, u32[]{:S(2)}, u32[]{:S(2)}) collective-permute-start(bf16[16,320]{1,0:T(8,128)(2,1)S(1)} %get-tuple-element.41), channel_id=1, source_target_pairs={{2,4},{4,2},{6,8},{8,6},{10,12},{12,10},{14,16},{16,14},{18,20},{2... | collective-permute-start | bytes 30728 | tf_op jit(solution)/shard_map/ppermute | solution.py:192
  24.4 1.2 %collective-permute-start.12 = (f32[16,128]{1,0:T(8,128)S(1)}, f32[16,128]{1,0:T(8,128)S(1)}, u32[]{:S(2)}, u32[]{:S(2)}) collective-permute-start(f32[16,128]{1,0:T(8,128)S(1)} %get-tuple-element.43), channel_id=1, source_target_pairs={{0,2},{2,0},{1,3},{3,1},{4,6},{6,4},{5,7},{7,5},{8,10},{10,8},{9,1... | collective-permute-start | bytes 24584 | tf_op jit(solution)/shard_map/ppermute | solution.py:244
  39.9 1.2 %collective-permute-start.13 = (f32[16,128]{1,0:T(8,128)S(1)}, f32[16,128]{1,0:T(8,128)S(1)}, u32[]{:S(2)}, u32[]{:S(2)}) collective-permute-start(f32[16,128]{1,0:T(8,128)S(1)} %reduce_sum.9.mine_ref), channel_id=1, source_target_pairs={{0,2},{2,0},{1,3},{3,1},{4,6},{6,4},{5,7},{7,5},{8,10},{10,8},{9,1... | collective-permute-start | bytes 24584 | tf_op jit(solution)/shard_map/ppermute | solution.py:247

commit v3 on v2

v3 whole, which is shorter than its diff:
```python
import functools

import jax
import jax.numpy as jnp
from jax import lax
from jax.experimental import pallas as pl
from jax.experimental.pallas import tpu as pltpu
from jax.sharding import Mesh
from jax.sharding import PartitionSpec as P

S = 4
H = 1
CORES = 2

VMEM = pl.BlockSpec(memory_space=pltpu.VMEM)
HBM = pl.BlockSpec(memory_space=pltpu.HBM)
SMEM = pl.BlockSpec(memory_space=pltpu.SMEM)


def start_kernel(*refs):
    sources, rest = refs[:6], refs[6:]
    targets, side_ref, chip_ref, sems = rest[:6], rest[6], rest[7], rest[8]
    field_ref = targets[0]
    count = field_ref.shape[0] - 1
    targets = (field_ref.at[pl.ds(0, count)], *targets[1:])
    copies = [pltpu.make_async_copy(a, b, sems.at[i]) for i, (a, b) in enumerate(zip(sources, targets))]
    for copy in copies:
        copy.start()
    copies[0].wait()
    core = lax.axis_index("core")
    near, far = field_ref[core * (count - 1)], field_ref[(1 - core) * (count - 1)]
    side_ref[0] = near
    side_ref[1] = far
    chip_ref[...] = far
    for copy in copies[1:]:
        copy.wait()
    donor_ref = targets[2]
    _, _, grids, slots = donor_ref.shape
    row = lax.broadcasted_iota(jnp.int32, field_ref.shape[1:], 0)
    asked = jnp.zeros(field_ref.shape[1:], jnp.int32)
    for g in range(grids):
        for c in range(slots):
            asked = jnp.where(row == g * slots + c, donor_ref[0, 0, g, c], asked)
    field_ref[count] = asked.astype(jnp.float32).astype(jnp.bfloat16)


def inner_kernel(offsets_ref, v_ref, chip_ref, blocks_ref, acc_ref):
    count, kinds = acc_ref.shape[0], offsets_ref.shape[0]
    core = lax.axis_index("core")
    for e in range(count):
        total = None
        for k in range(kinds):
            col = e + offsets_ref[k, 0, e]
            inside = jnp.logical_and(col >= 0, col < count)
            lhs = v_ref[jnp.clip(col, 0, count - 1)]
            if e == 0 or e == count - 1:
                halo = jnp.logical_or(
                    jnp.logical_and(col < 0, core == 1), jnp.logical_and(col >= count, core == 0)
                )
                lhs = jnp.where(inside, lhs, jnp.where(halo, chip_ref[...], jnp.zeros_like(lhs)))
            part = jnp.dot(lhs, blocks_ref[e, k], preferred_element_type=jnp.float32)
            total = part if total is None else total + part
        acc_ref[e] = total


def outer_kernel(
    grids, first, last_level, offsets_ref, donor_ref, fringe_ref, weight_ref, live_ref,
    acc_ref, blocks_ref, halo_ref, *rest
):
    take = lambda m: (rest[:m], rest[m:])
    asked, rest = take(grids - 1)
    others, rest = (asked, rest) if first else take(grids - 1)
    v_ref, *sends, total_ref = rest
    count, kinds = blocks_ref.shape[:2]
    slots = donor_ref.shape[3]
    last = count - 1
    chips = lax.axis_size("chip")
    chip, core, grid = (lax.axis_index(a) for a in ("chip", "core", "grid"))
    for e in range(count):
        total_ref[e] = acc_ref[e]
    there = jnp.where(core == 0, chip > 0, chip < chips - 1)
    edge = core * last
    total = total_ref[edge]
    for k in range(kinds):
        used = jnp.logical_and(offsets_ref[k, 0, edge] == jnp.where(core == 0, -H, H), there)
        lhs = jnp.where(used, halo_ref[0], jnp.zeros(halo_ref.shape[1:], halo_ref.dtype))
        total += jnp.dot(lhs, blocks_ref[edge, k], preferred_element_type=jnp.float32)
    total_ref[edge] = total
    for s, other in enumerate(others):
        g = lax.rem(grid + grids - 1 - s, grids)
        for c in range(slots):
            f = fringe_ref[0, 0, g, c]
            weight = jnp.where(c < live_ref[0, 0, g], weight_ref[0, 0, g, c], 0.0)
            value = other[donor_ref[0, 0, g, c] if first else c].astype(jnp.float32)
            total_ref[f] += weight * value
    for e in range(count):
        v_ref[e] = total_ref[e].astype(jnp.bfloat16)
    if last_level:
        return
    sends[0][0] = v_ref[edge]
    sends[0][1] = v_ref[last - edge]
    sends[1][...] = v_ref[last - edge]
    row = lax.broadcasted_iota(jnp.int32, v_ref.shape[1:], 0)
    for s, send_ref in enumerate(sends[2:]):
        wish = asked[grids - 2 - s][count].astype(jnp.float32)
        for c in range(slots):
            index = jnp.sum(jnp.where(row == grid * slots + c, wish, 0.0), axis=0, keepdims=True)
            picked = total_ref[0]
            for e in range(1, count):
                picked = jnp.where(index == e, total_ref[e], picked)
            send_ref[c] = picked.astype(jnp.bfloat16)


def stripe(fields, upto):
    count = fields[1].shape[0]
    total = None
    for e in range(count):
        rows = jnp.concatenate([f[e] for f in fields[: upto + 1]], axis=0)
        part = lax.dot_general(
            fields[upto][e], rows, (((1,), (1,)), ((), ())), preferred_element_type=jnp.float32
        )
        total = part if total is None else total + part
    return total


def early_gram_kernel(*refs):
    fields, (early_ref,) = refs[:S], refs[S:]
    n = early_ref.shape[0]
    total = None
    for e in range(fields[1].shape[0]):
        rows = jnp.concatenate([f[e] for f in fields], axis=0)
        part = lax.dot_general(rows, rows, (((1,), (1,)), ((), ())), preferred_element_type=jnp.float32)
        total = part if total is None else total + part
    b = lambda i, j0, j1: total[i * n : (i + 1) * n, j0 * n : j1 * n]
    blank = jnp.zeros((n, n), jnp.float32)
    early_ref[...] = jnp.concatenate(
        [b(3, 0, 3), b(3, 3, 4), b(2, 0, 3), b(1, 0, 2), b(0, 0, 1), blank], axis=1
    )


def late_gram_kernel(*refs):
    fields, (early_ref, keep_ref, send_ref) = refs[: S + 1], refs[S + 1 :]
    n = early_ref.shape[0]
    one = jnp.concatenate([stripe(fields, S), early_ref[:, : 3 * n]], axis=1)
    two = early_ref[:, 3 * n :]
    first = lax.axis_index("core") == 0
    keep_ref[...] = jnp.where(first, one, two)
    send_ref[...] = jnp.where(first, two, one)


def cholesky_rows(panels, height, r_ref):
    size = len(panels) * height
    count = len(panels)
    lane = lax.broadcasted_iota(jnp.int32, (height, size), 1)
    sub = lax.broadcasted_iota(jnp.int32, (height, size), 0)
    panels = list(panels)
    row = lambda x, c: jnp.broadcast_to(x[c : c + 1], (height, size))
    wide = lambda p, j: jnp.broadcast_to(panels[p][:, j : j + 1], (height, size))
    ahead = {c: wide(0, c) for c in range(height)}
    for q in range(count):
        base = q * height
        more = 2 * height if q + 1 < count else height
        side = {(c, p): wide(p, base + c) for c in range(height) for p in range(q + 1, count)}
        side.update({(c, q): ahead[c] for c in range(height)})
        if q + 1 < count:
            side.update({(c, p): wide(p, base + c) for c in range(height, more) for p in (q, q + 1)})
        out = jnp.zeros((height, size), jnp.float32)
        for c in range(height):
            one = row(panels[q], c)
            a = row(side[c, q], c)
            inv = 1.0 / a
            out = jnp.where(sub == c, one * lax.rsqrt(a), out)
            if c + 1 == height and q + 1 == count:
                break
            tops = {e: row(side[e, q], c) for e in range(c + 1, more)}
            scaled = one * inv
            for p in range(q, count):
                if p == q and c + 1 == height:
                    continue
                x = side[c, p] * inv
                panels[p] = panels[p] - x * one
                for e in range(c + 1, more):
                    if (e, p) in side:
                        side[e, p] = side[e, p] - x * tops[e]
        ahead = {c: side[height + c, q + 1] for c in range(height)} if q + 1 < count else {}
        r_ref[base : base + height, :] = jnp.where(lane >= sub + base, out, 0.0)


def factor_kernel(scale, mine_ref, other_ref, r_ref):
    first = lax.axis_index("core") == 0
    mine, other = mine_ref[...] * scale, other_ref[...] * scale
    one, two = jnp.where(first, mine, other), jnp.where(first, other, mine)
    n = one.shape[0]
    size = (S + 1) * n
    b = lambda x, j0, j1: x[:, j0 * n : j1 * n]
    wide = lambda x: jnp.concatenate([x, jnp.zeros((n, size - x.shape[1]), jnp.float32)], axis=1)
    low = jnp.concatenate([
        wide(b(two, 6, 7)),
        wide(b(two, 4, 6)),
        wide(b(two, 1, 4)),
        wide(jnp.concatenate([b(one, 5, 8), b(two, 0, 1)], axis=1)),
        b(one, 0, 5),
    ], axis=0)
    row = lax.broadcasted_iota(jnp.int32, (size, size), 0)
    col = lax.broadcasted_iota(jnp.int32, (size, size), 1)
    a = jnp.where(row >= col, low, low.T)
    height = 8
    cholesky_rows([a[i : i + height] for i in range(0, size, height)], height, r_ref)


def local(rhs, blocks, offsets, donor_elem, fringe_elem, donor_weight, fringe_count):
    _, elem_count, n, unknowns = rhs.shape
    chips, cores, grids = (lax.axis_size(a) for a in ("chip", "core", "grid"))
    axes = ("chip", "core", "grid")
    at = lambda chip, core, grid: (chip * cores + core) * grids + grid % grids
    side = []
    for g in range(grids):
        for chip in range(chips - 1):
            side += [(at(chip, 1, g), at(chip + 1, 0, g)), (at(chip + 1, 0, g), at(chip, 1, g))]
        side += [(at(0, 0, g), at(0, 0, g + 1)), (at(chips - 1, 1, g), at(chips - 1, 1, g + 1))]
    swap = [(0, 1), (1, 0)]

    def exchange(to_side, to_chip, *donors):
        from_side = lax.ppermute(to_side, axes, side)
        others = [
            lax.ppermute(v, "grid", [(g, (g + s) % grids) for g in range(grids)])
            for s, v in enumerate(donors, 1)
        ]
        return from_side, lax.ppermute(to_chip, "core", swap), others

    halo_type = jax.ShapeDtypeStruct((n, unknowns), jnp.bfloat16)
    side_type = jax.ShapeDtypeStruct((2, n, unknowns), jnp.bfloat16)
    field_type = jax.ShapeDtypeStruct((elem_count, n, unknowns), jnp.bfloat16)
    acc_type = jax.ShapeDtypeStruct((elem_count, n, unknowns), jnp.float32)
    half_type = jax.ShapeDtypeStruct((n, 8 * n), jnp.float32)
    limit = pltpu.CompilerParams(vmem_limit_bytes=24 << 20)
    flops = 2 * elem_count * n * unknowns * unknowns * blocks.shape[2]

    kinds = blocks.shape[2]
    by_kind = jnp.transpose(offsets, (2, 0, 1))
    small = (by_kind, donor_elem, fringe_elem, donor_weight, fringe_count)
    field, *small, side_edge, chip_edge = pl.pallas_call(
        start_kernel,
        out_shape=(
            jax.ShapeDtypeStruct((elem_count + 1, n, unknowns), jnp.bfloat16),
            *(pltpu.SMEM(x.shape, x.dtype) for x in small), side_type, halo_type,
        ),
        in_specs=[HBM] * 6, out_specs=(VMEM, *[SMEM] * 5, VMEM, VMEM),
        scratch_shapes=[pltpu.SemaphoreType.DMA((6,))],
        compiler_params=limit, name="start",
        cost_estimate=pl.CostEstimate(flops=4 * 10**9, bytes_accessed=10**7, transcendentals=0),
    )(*(pltpu.with_memory_space_constraint(x, pltpu.HBM) for x in (rhs[0], *small)))
    sends = (side_edge, chip_edge, *[field] * (grids - 1))
    donor_type = jax.ShapeDtypeStruct((donor_elem.shape[3], n, unknowns), jnp.bfloat16)
    asked = []
    basis = [field]
    blocks = blocks[0]
    for level in range(S):
        from_side, from_chip, others = exchange(*sends)
        cost = pl.CostEstimate(flops=flops, bytes_accessed=blocks.size * 2, transcendentals=0)
        acc = pl.pallas_call(
            inner_kernel, out_shape=acc_type, in_specs=[SMEM, VMEM, VMEM, VMEM], out_specs=VMEM,
            compiler_params=limit, name="inner", cost_estimate=cost,
        )(small[0], field, from_chip, blocks)
        if level + 1 == S:
            early = pl.pallas_call(
                early_gram_kernel, out_shape=jax.ShapeDtypeStruct((n, 11 * n), jnp.float32),
                in_specs=[VMEM] * S, out_specs=VMEM, compiler_params=limit, name="early_gram", cost_estimate=cost,
            )(*basis)
        types = () if level + 1 == S else (side_type, halo_type, *[donor_type] * (grids - 1))
        messages = [*asked, *others]
        field, *sends = pl.pallas_call(
            functools.partial(outer_kernel, grids, level == 0, level + 1 == S),
            out_shape=(field_type, *types),
            in_specs=[SMEM] * 5 + [VMEM] * (3 + len(messages)),
            out_specs=(VMEM, *[VMEM] * len(types)),
            scratch_shapes=[pltpu.VMEM((elem_count, n, unknowns), jnp.float32)],
            compiler_params=limit, name="outer",
        )(*small, acc, blocks, from_side, *messages)
        asked = asked or others
        basis.append(field)
    keep, send = pl.pallas_call(
        late_gram_kernel, out_shape=(half_type, half_type), in_specs=[VMEM] * (S + 2), out_specs=(VMEM, VMEM),
        compiler_params=limit, name="late_gram",
    )(*basis, early)
    half = keep + lax.ppermute(send, "core", swap)
    parts = lax.all_to_all(jnp.broadcast_to(half[None], (chips * grids, n, 8 * n)), ("chip", "grid"), 0, 0, tiled=True)
    mine = parts.sum(axis=0)
    other = lax.ppermute(mine, "core", swap)
    columns = (S + 1) * n
    row_total = grids * chips * cores * elem_count * unknowns
    r_factor = pl.pallas_call(
        functools.partial(factor_kernel, 1.0 / row_total),
        out_shape=jax.ShapeDtypeStruct((columns, columns), jnp.float32),
        in_specs=[VMEM] * 2, out_specs=VMEM,
        compiler_params=limit, name="factor",
    )(mine, other)
    powers = jnp.stack(basis[1:], axis=1)[None]
    return (powers, r_factor)


def solution(mesh):
    dom, grids = mesh.shape["dom"], mesh.shape["grid"]
    split = Mesh(mesh.devices.reshape(dom // CORES, CORES, grids), ("chip", "core", "grid"))
    where = ("chip", "core")
    in_specs = (
        P("grid", where, None, None),
        P("grid", where, None, None, None),
        P("grid", where, None),
        P("grid", where, None, None),
        P("grid", where, None, None),
        P("grid", where, None, None),
        P("grid", where, None),
    )
    out_specs = (P("grid", where, None, None, None), P())
    return jax.shard_map(local, mesh=split, in_specs=in_specs, out_specs=out_specs, check_vma=False)
```

time: 44.2 us -> 42.3 us (0.957)
  Pallas kernels: 10.1 us -> 8.26 us
  blocking collectives: 14.3 us -> 12.5 us
  starting transfers between devices: 9.86 us -> 11 us
  waiting for transfers between devices: 8.16 us -> 8.81 us
    ppermute x4, waiting for transfers between devices: 0.01 us -> 2.53 us  [exchange(): lax.ppermute(v, 'grid', [(g, (g + s) % grids) for g in range(grids)])]
    pallas_call x7, Pallas kernels: 5.08 us -> 2.81 us  [the longest x1 1.15 us: local(): pl.pallas_call(start_kernel, out_shape=(jax.ShapeDtypeStruct((elem_count...]
    ppermute x8, waiting for transfers between devices: 6.76 us -> 4.75 us  [the longest x4 4.06 us: exchange(): return (from_side, lax.ppermute(to_chip, 'core', swap), others)]
    all_to_all x1, blocking collectives: 14.3 us -> 12.5 us  [local(): lax.all_to_all(jnp.broadcast_to(half[None], (chips * grids, n, 8 * n)), (...]
    ppermute x8, starting transfers between devices: 3.54 us -> 4.78 us  [the longest x4 3.21 us: exchange(): from_side = lax.ppermute(to_side, axes, side)]
    pallas_call x3 -> x4, Pallas kernels: 2.18 us -> 2.91 us  [local(): pl.pallas_call(inner_kernel, out_shape=acc_type, in_specs=[SMEM, VMEM, VM...]
  transfers between devices with their start and end apart: 14 -> 14, of which waited for: 7 -> 11; matrix products, arithmetic and copies ran while one was open for 2% -> 2% of each run, Pallas kernels for 11% -> 8%
where the time goes in v3:
time: 42.3 us; the launch traced here: 42.1 us
  blocking collectives  12.5 us (30%)
  starting transfers between devices  11 us (26%)
  waiting for transfers between devices  8.81 us (21%)
  Pallas kernels  8.26 us (20%)
  local copies, waits for them, and re-layouts  0.76 us (2%)
  between operations  0.74 us (2%)
    all_to_all x1, blocking collectives, local(): lax.all_to_all(jnp.broadcast_to(half[None], (chips * grids, n, 8 * n)), (...  12.5 us
    ppermute x4, starting transfers between devices, exchange(): lax.ppermute(v, 'grid', [(g, (g + s) % grids) for g in range(grids)])  6.14 us
    ppermute x4, waiting for transfers between devices, exchange(): return (from_side, lax.ppermute(to_chip, 'core', swap), others)  4.06 us
    ppermute x4, starting transfers between devices, exchange(): from_side = lax.ppermute(to_side, axes, side)  3.21 us
    pallas_call x4, Pallas kernels, local(): pl.pallas_call(inner_kernel, out_shape=acc_type, in_specs=[SMEM, VMEM, VM...  2.91 us
    pallas_call x1, Pallas kernels, local(): pl.pallas_call(functools.partial(factor_kernel, 1.0 / row_total), out_sha...  2.54 us
    ppermute x4, waiting for transfers between devices, exchange(): lax.ppermute(v, 'grid', [(g, (g + s) % grids) for g in range(grids)])  2.53 us
    ppermute x4, starting transfers between devices, exchange(): return (from_side, lax.ppermute(to_chip, 'core', swap), others)  1.56 us
  transfers between devices with their start and end apart: 14, of which 11 were waited for; matrix products, arithmetic and copies ran while one was open for 2% of the time, Pallas kernels for 8%

profile of v3, /device:TPU:0, one launch (start us, length us, event | category | flops | bytes accessed | tf_op | source)
XLA Modules:
  0.0 42.1 jit_solution(7601621621509198126)
XLA Ops:
  0.6 1.1 %start.1 = (bf16[7,16,320]{2,1,0:T(8,128)(2,1)S(1)}, s32[3,1,6]{2,1,0:T(1,128)S(4)}, s32[1,1,2,2]{3,2,1,0:T(2,128)S(4)}, s32[1,1,2,2]{3,2,1,0:T(2,128)S(4)}, f32...) custom-call(bf16[6,16,320]{2,1,0:T(8,128)(2,1)} %bitcast.21, ...), custom_call_target="tpu_custom_call" | custom-call | flops 4000000000 | bytes 10000000 | tf_op jit(solution)/shard_map/start/pallas_call | solution.py:242
  1.8 3.0 %collective-permute-start.2 = (bf16[7,16,320]{2,1,0:T(8,128)(2,1)S(1)}, bf16[7,16,320]{2,1,0:T(8,128)(2,1)S(1)}, u32[]{:S(2)}, u32[]{:S(2)}) collective-permute-start(bf16[7,16,320]{2,1,0:T(8,128)(2,1)S(1)} %get-tuple-element.29.v_ref.refs_0_), channel_id=1, source_target_pairs={{0,1},{1,0},{2,3},{3,2},{4,5},{5,4},{6,7},{7,6},{8,9},{9,8},{10,11... | collective-permute-start | bytes 215048 | tf_op jit(solution)/shard_map/ppermute | solution.py:226
  4.9 1.6 %collective-permute-start = (bf16[16,320]{1,0:T(8,128)(2,1)S(1)}, bf16[16,320]{1,0:T(8,128)(2,1)S(1)}, u32[]{:S(2)}, u32[]{:S(2)}) collective-permute-start(bf16[16,320]{1,0:T(8,128)(2,1)S(1)} %get-tuple-element.30), channel_id=1, source_target_pairs={{0,2},{2,0},{1,3},{3,1},{4,6},{6,4},{5,7},{7,5},{8,10},{10,8},{9,1... | collective-permute-start | bytes 30728 | tf_op jit(solution)/shard_map/ppermute | solution.py:229
  6.4 0.8 %collective-permute-done.chip_ref = bf16[16,320]{1,0:T(8,128)(2,1)S(1)} collective-permute-done((bf16[16,320]{1,0:T(8,128)(2,1)S(1)}, bf16[16,320]{1,0:T(8,128)(2,1)S(1)}, u32[]{:S(2)}, u32[]{:S(2)}) %collective-permute-start) | collective-permute-done | bytes 10272 | tf_op jit(solution)/shard_map/ppermute | solution.py:229
  7.3 0.7 %inner.4.acc_ref = f32[6,16,320]{2,1,0:T(8,128)S(1)} custom-call(s32[3,1,6]{2,1,0:T(1,128)S(4)} %get-tuple-element.24.offsets_ref, bf16[7,16,320]{2,1,0:T(8,128)(2,1)S(1)} %get-tuple-element.29.v_ref.refs_0_, bf16[16,320]{1,0:T(8,128)(2,1)S(1)} %collective-permute-done.chip_ref, bf16[6,3,320,320]{3,2,1,0:T(8,128)(2,1)S(1)} %bitcast.9), custom_call_target="tpu_custom_call" | custom-call | flops 58982400 | bytes 3686400 | tf_op jit(solution)/shard_map/inner/pallas_call | solution.py:261
  8.0 0.6 %collective-permute-done.1.halo_ref = bf16[2,16,320]{2,1,0:T(8,128)(2,1)S(1)} collective-permute-done((bf16[2,16,320]{2,1,0:T(8,128)(2,1)S(1)}, bf16[2,16,320]{2,1,0:T(8,128)(2,1)S(1)}, u32[]{:S(2)}, u32[]{:S(2)}) %collective-permute-start.1) | collective-permute-done | bytes 20512 | tf_op jit(solution)/shard_map/ppermute | solution.py:224
  8.6 0.3 outer.4
  8.9 1.0 %collective-permute-start.4 = (bf16[2,16,320]{2,1,0:T(8,128)(2,1)S(1)}, bf16[2,16,320]{2,1,0:T(8,128)(2,1)S(1)}, u32[]{:S(2)}, u32[]{:S(2)}) collective-permute-start(bf16[2,16,320]{2,1,0:T(8,128)(2,1)S(1)} %get-tuple-element.34), channel_id=1, source_target_pairs={{2,4},{4,2},{6,8},{8,6},{10,12},{12,10},{14,16},{16,14},{18,20},{2... | collective-permute-start | bytes 61448 | tf_op jit(solution)/shard_map/ppermute | solution.py:224
  9.9 1.1 %collective-permute-start.5 = (bf16[2,16,320]{2,1,0:T(8,128)(2,1)S(1)}, bf16[2,16,320]{2,1,0:T(8,128)(2,1)S(1)}, u32[]{:S(2)}, u32[]{:S(2)}) collective-permute-start(bf16[2,16,320]{2,1,0:T(8,128)(2,1)S(1)} %get-tuple-element.35), channel_id=1, source_target_pairs={{0,1},{1,0},{2,3},{3,2},{4,5},{5,4},{6,7},{7,6},{8,9},{9,8},{10,11... | collective-permute-start | bytes 61448 | tf_op jit(solution)/shard_map/ppermute | solution.py:226
  11.0 1.2 %collective-permute-done.3.chip_ref = bf16[16,320]{1,0:T(8,128)(2,1)S(1)} collective-permute-done((bf16[16,320]{1,0:T(8,128)(2,1)S(1)}, bf16[16,320]{1,0:T(8,128)(2,1)S(1)}, u32[]{:S(2)}, u32[]{:S(2)}) %collective-permute-start.3) | collective-permute-done | bytes 10272 | tf_op jit(solution)/shard_map/ppermute | solution.py:229
  12.2 0.7 %inner.5.acc_ref = f32[6,16,320]{2,1,0:T(8,128)S(1)} custom-call(s32[3,1,6]{2,1,0:T(1,128)S(4)} %get-tuple-element.24.offsets_ref, bf16[6,16,320]{2,1,0:T(8,128)(2,1)S(1)} %get-tuple-element.32.v_ref.refs_1_, bf16[16,320]{1,0:T(8,128)(2,1)S(1)} %collective-permute-done.3.chip_ref, bf16[6,3,320,320]{3,2,1,0:T(8,128)(2,1)S(1)} %bitcast.11), custom_call_target="tpu_custom_call" | custom-call | flops 58982400 | bytes 3686400 | tf_op jit(solution)/shard_map/inner/pallas_call | solution.py:261
  13.0 0.7 %collective-permute-done.5.rest_1_ = bf16[2,16,320]{2,1,0:T(8,128)(2,1)S(1)} collective-permute-done((bf16[2,16,320]{2,1,0:T(8,128)(2,1)S(1)}, bf16[2,16,320]{2,1,0:T(8,128)(2,1)S(1)}, u32[]{:S(2)}, u32[]{:S(2)}) %collective-permute-start.5) | collective-permute-done | bytes 20512 | tf_op jit(solution)/shard_map/ppermute | solution.py:226
  13.7 0.3 outer.5
  14.0 1.2 %collective-permute-start.7 = (bf16[2,16,320]{2,1,0:T(8,128)(2,1)S(1)}, bf16[2,16,320]{2,1,0:T(8,128)(2,1)S(1)}, u32[]{:S(2)}, u32[]{:S(2)}) collective-permute-start(bf16[2,16,320]{2,1,0:T(8,128)(2,1)S(1)} %get-tuple-element.38), channel_id=1, source_target_pairs={{2,4},{4,2},{6,8},{8,6},{10,12},{12,10},{14,16},{16,14},{18,20},{2... | collective-permute-start | bytes 61448 | tf_op jit(solution)/shard_map/ppermute | solution.py:224
  15.1 0.9 %collective-permute-start.8 = (bf16[2,16,320]{2,1,0:T(8,128)(2,1)S(1)}, bf16[2,16,320]{2,1,0:T(8,128)(2,1)S(1)}, u32[]{:S(2)}, u32[]{:S(2)}) collective-permute-start(bf16[2,16,320]{2,1,0:T(8,128)(2,1)S(1)} %get-tuple-element.39), channel_id=1, source_target_pairs={{0,1},{1,0},{2,3},{3,2},{4,5},{5,4},{6,7},{7,6},{8,9},{9,8},{10,11... | collective-permute-start | bytes 61448 | tf_op jit(solution)/shard_map/ppermute | solution.py:226
  16.1 1.2 %collective-permute-done.6.chip_ref = bf16[16,320]{1,0:T(8,128)(2,1)S(1)} collective-permute-done((bf16[16,320]{1,0:T(8,128)(2,1)S(1)}, bf16[16,320]{1,0:T(8,128)(2,1)S(1)}, u32[]{:S(2)}, u32[]{:S(2)}) %collective-permute-start.6) | collective-permute-done | bytes 10272 | tf_op jit(solution)/shard_map/ppermute | solution.py:229
  17.2 0.7 %inner.6.acc_ref = f32[6,16,320]{2,1,0:T(8,128)S(1)} custom-call(s32[3,1,6]{2,1,0:T(1,128)S(4)} %get-tuple-element.24.offsets_ref, bf16[6,16,320]{2,1,0:T(8,128)(2,1)S(1)} %get-tuple-element.36.v_ref.refs_2_, bf16[16,320]{1,0:T(8,128)(2,1)S(1)} %collective-permute-done.6.chip_ref, bf16[6,3,320,320]{3,2,1,0:T(8,128)(2,1)S(1)} %bitcast.13), custom_call_target="tpu_custom_call" | custom-call | flops 58982400 | bytes 3686400 | tf_op jit(solution)/shard_map/inner/pallas_call | solution.py:261
  18.0 1.0 %collective-permute-done.8.rest_1_ = bf16[2,16,320]{2,1,0:T(8,128)(2,1)S(1)} collective-permute-done((bf16[2,16,320]{2,1,0:T(8,128)(2,1)S(1)}, bf16[2,16,320]{2,1,0:T(8,128)(2,1)S(1)}, u32[]{:S(2)}, u32[]{:S(2)}) %collective-permute-start.8) | collective-permute-done | bytes 20512 | tf_op jit(solution)/shard_map/ppermute | solution.py:226
  19.0 0.3 outer.6
  19.2 1.0 %collective-permute-start.10 = (bf16[2,16,320]{2,1,0:T(8,128)(2,1)S(1)}, bf16[2,16,320]{2,1,0:T(8,128)(2,1)S(1)}, u32[]{:S(2)}, u32[]{:S(2)}) collective-permute-start(bf16[2,16,320]{2,1,0:T(8,128)(2,1)S(1)} %get-tuple-element.42), channel_id=1, source_target_pairs={{2,4},{4,2},{6,8},{8,6},{10,12},{12,10},{14,16},{16,14},{18,20},{2... | collective-permute-start | bytes 61448 | tf_op jit(solution)/shard_map/ppermute | solution.py:224
  20.2 1.1 %collective-permute-start.11 = (bf16[2,16,320]{2,1,0:T(8,128)(2,1)S(1)}, bf16[2,16,320]{2,1,0:T(8,128)(2,1)S(1)}, u32[]{:S(2)}, u32[]{:S(2)}) collective-permute-start(bf16[2,16,320]{2,1,0:T(8,128)(2,1)S(1)} %get-tuple-element.43), channel_id=1, source_target_pairs={{0,1},{1,0},{2,3},{3,2},{4,5},{5,4},{6,7},{7,6},{8,9},{9,8},{10,11... | collective-permute-start | bytes 61448 | tf_op jit(solution)/shard_map/ppermute | solution.py:226
  21.3 0.3 early_gram.1.refs_5_
  21.6 0.9 %collective-permute-done.9.chip_ref = bf16[16,320]{1,0:T(8,128)(2,1)S(1)} collective-permute-done((bf16[16,320]{1,0:T(8,128)(2,1)S(1)}, bf16[16,320]{1,0:T(8,128)(2,1)S(1)}, u32[]{:S(2)}, u32[]{:S(2)}) %collective-permute-start.9) | collective-permute-done | bytes 10272 | tf_op jit(solution)/shard_map/ppermute | solution.py:229
  22.5 0.7 %inner.7.acc_ref = f32[6,16,320]{2,1,0:T(8,128)S(1)} custom-call(s32[3,1,6]{2,1,0:T(1,128)S(4)} %get-tuple-element.24.offsets_ref, bf16[6,16,320]{2,1,0:T(8,128)(2,1)S(1)} %get-tuple-element.40.v_ref.refs_3_, bf16[16,320]{1,0:T(8,128)(2,1)S(1)} %collective-permute-done.9.chip_ref, bf16[6,3,320,320]{3,2,1,0:T(8,128)(2,1)S(1)} %bitcast.15), custom_call_target="tpu_custom_call" | custom-call | flops 58982400 | bytes 3686400 | tf_op jit(solution)/shard_map/inner/pallas_call | solution.py:261
  23.2 0.8 %collective-permute-done.11.rest_1_ = bf16[2,16,320]{2,1,0:T(8,128)(2,1)S(1)} collective-permute-done((bf16[2,16,320]{2,1,0:T(8,128)(2,1)S(1)}, bf16[2,16,320]{2,1,0:T(8,128)(2,1)S(1)}, u32[]{:S(2)}, u32[]{:S(2)}) %collective-permute-start.11) | collective-permute-done | bytes 20512 | tf_op jit(solution)/shard_map/ppermute | solution.py:226
  24.0 0.2 outer.7.refs_4_
  24.3 0.4 late_gram.1
  24.6 1.2 %collective-permute-done.12 = f32[16,128]{1,0:T(8,128)S(1)} collective-permute-done((f32[16,128]{1,0:T(8,128)S(1)}, f32[16,128]{1,0:T(8,128)S(1)}, u32[]{:S(2)}, u32[]{:S(2)}) %collective-permute-start.12) | collective-permute-done | bytes 8224 | tf_op jit(solution)/shard_map/ppermute | solution.py:286
  25.9 12.5 %all_to_all.5 = f32[16,16,128]{2,1,0:T(8,128)S(1)} all-to-all(f32[16,16,128]{2,1,0:T(8,128)S(1)} %broadcast_in_dim.10), channel_id=1, replica_groups=mesh['chip'=8,'core'=2,'grid'=2] {'chip','grid'}, dimensions={0} | all-to-all | bytes 262144 | tf_op jit(solution)/shard_map/all_to_all | solution.py:287
  38.5 0.7 %copy.10 = bf16[1,6,4,16,320]{4,3,2,1,0:T(8,128)(2,1)} copy(bf16[1,6,4,16,320]{4,3,1,2,0:T(8,128)(2,1)S(1)} %maximum_bitcast_fusion) | data formatting | bytes 491520
  39.3 0.3 collective-permute-done.13.other_ref
  39.6 2.5 %factor.1 = f32[80,80]{1,0:T(8,128)} custom-call(f32[16,128]{1,0:T(8,128)S(1)} %reduce_sum.9.mine_ref, f32[16,128]{1,0:T(8,128)S(1)} %collective-permute-done.13.other_ref), custom_call_target="tpu_custom_call" | custom-call | tf_op jit(solution)/shard_map/factor/pallas_call | solution.py:292
  (16 shorter events, 0.3 us)
Async XLA Ops:
  0.6 6.6 %copy-start = (bf16[1,6,3,320,320]{4,3,2,1,0:T(8,128)(2,1)S(1)}, bf16[1,6,3,320,320]{4,3,2,1,0:T(8,128)(2,1)}, u32[]{:S(2)}) copy-start(bf16[1,6,3,320,320]{4,3,2,1,0:T(8,128)(2,1)} %param.8) | copy-start | bytes 11059204
  1.8 6.8 %collective-permute-start.2 = (bf16[7,16,320]{2,1,0:T(8,128)(2,1)S(1)}, bf16[7,16,320]{2,1,0:T(8,128)(2,1)S(1)}, u32[]{:S(2)}, u32[]{:S(2)}) collective-permute-start(bf16[7,16,320]{2,1,0:T(8,128)(2,1)S(1)} %get-tuple-element.29.v_ref.refs_0_), channel_id=1, source_target_pairs={{0,1},{1,0},{2,3},{3,2},{4,5},{5,4},{6,7},{7,6},{8,9},{9,8},{10,11... | collective-permute-start | bytes 215048 | tf_op jit(solution)/shard_map/ppermute | solution.py:226
  4.8 3.8 %collective-permute-start.1 = (bf16[2,16,320]{2,1,0:T(8,128)(2,1)S(1)}, bf16[2,16,320]{2,1,0:T(8,128)(2,1)S(1)}, u32[]{:S(2)}, u32[]{:S(2)}) collective-permute-start(bf16[2,16,320]{2,1,0:T(8,128)(2,1)S(1)} %get-tuple-element.31), channel_id=1, source_target_pairs={{2,4},{4,2},{6,8},{8,6},{10,12},{12,10},{14,16},{16,14},{18,20},{2... | collective-permute-start | bytes 61448 | tf_op jit(solution)/shard_map/ppermute | solution.py:224
  4.9 2.4 %collective-permute-start = (bf16[16,320]{1,0:T(8,128)(2,1)S(1)}, bf16[16,320]{1,0:T(8,128)(2,1)S(1)}, u32[]{:S(2)}, u32[]{:S(2)}) collective-permute-start(bf16[16,320]{1,0:T(8,128)(2,1)S(1)} %get-tuple-element.30), channel_id=1, source_target_pairs={{0,2},{2,0},{1,3},{3,1},{4,6},{6,4},{5,7},{7,5},{8,10},{10,8},{9,1... | collective-permute-start | bytes 30728 | tf_op jit(solution)/shard_map/ppermute | solution.py:229
  8.9 4.1 %collective-permute-start.4 = (bf16[2,16,320]{2,1,0:T(8,128)(2,1)S(1)}, bf16[2,16,320]{2,1,0:T(8,128)(2,1)S(1)}, u32[]{:S(2)}, u32[]{:S(2)}) collective-permute-start(bf16[2,16,320]{2,1,0:T(8,128)(2,1)S(1)} %get-tuple-element.34), channel_id=1, source_target_pairs={{2,4},{4,2},{6,8},{8,6},{10,12},{12,10},{14,16},{16,14},{18,20},{2... | collective-permute-start | bytes 61448 | tf_op jit(solution)/shard_map/ppermute | solution.py:224
  9.9 3.8 %collective-permute-start.5 = (bf16[2,16,320]{2,1,0:T(8,128)(2,1)S(1)}, bf16[2,16,320]{2,1,0:T(8,128)(2,1)S(1)}, u32[]{:S(2)}, u32[]{:S(2)}) collective-permute-start(bf16[2,16,320]{2,1,0:T(8,128)(2,1)S(1)} %get-tuple-element.35), channel_id=1, source_target_pairs={{0,1},{1,0},{2,3},{3,2},{4,5},{5,4},{6,7},{7,6},{8,9},{9,8},{10,11... | collective-permute-start | bytes 61448 | tf_op jit(solution)/shard_map/ppermute | solution.py:226
  11.0 1.2 %collective-permute-start.3 = (bf16[16,320]{1,0:T(8,128)(2,1)S(1)}, bf16[16,320]{1,0:T(8,128)(2,1)S(1)}, u32[]{:S(2)}, u32[]{:S(2)}) collective-permute-start(bf16[16,320]{1,0:T(8,128)(2,1)S(1)} %get-tuple-element.33), channel_id=1, source_target_pairs={{0,2},{2,0},{1,3},{3,1},{4,6},{6,4},{5,7},{7,5},{8,10},{10,8},{9,1... | collective-permute-start | bytes 30728 | tf_op jit(solution)/shard_map/ppermute | solution.py:229
  14.0 4.0 %collective-permute-start.7 = (bf16[2,16,320]{2,1,0:T(8,128)(2,1)S(1)}, bf16[2,16,320]{2,1,0:T(8,128)(2,1)S(1)}, u32[]{:S(2)}, u32[]{:S(2)}) collective-permute-start(bf16[2,16,320]{2,1,0:T(8,128)(2,1)S(1)} %get-tuple-element.38), channel_id=1, source_target_pairs={{2,4},{4,2},{6,8},{8,6},{10,12},{12,10},{14,16},{16,14},{18,20},{2... | collective-permute-start | bytes 61448 | tf_op jit(solution)/shard_map/ppermute | solution.py:224
  15.1 3.8 %collective-permute-start.8 = (bf16[2,16,320]{2,1,0:T(8,128)(2,1)S(1)}, bf16[2,16,320]{2,1,0:T(8,128)(2,1)S(1)}, u32[]{:S(2)}, u32[]{:S(2)}) collective-permute-start(bf16[2,16,320]{2,1,0:T(8,128)(2,1)S(1)} %get-tuple-element.39), channel_id=1, source_target_pairs={{0,1},{1,0},{2,3},{3,2},{4,5},{5,4},{6,7},{7,6},{8,9},{9,8},{10,11... | collective-permute-start | bytes 61448 | tf_op jit(solution)/shard_map/ppermute | solution.py:226
  16.1 1.2 %collective-permute-start.6 = (bf16[16,320]{1,0:T(8,128)(2,1)S(1)}, bf16[16,320]{1,0:T(8,128)(2,1)S(1)}, u32[]{:S(2)}, u32[]{:S(2)}) collective-permute-start(bf16[16,320]{1,0:T(8,128)(2,1)S(1)} %get-tuple-element.37), channel_id=1, source_target_pairs={{0,2},{2,0},{1,3},{3,1},{4,6},{6,4},{5,7},{7,5},{8,10},{10,8},{9,1... | collective-permute-start | bytes 30728 | tf_op jit(solution)/shard_map/ppermute | solution.py:229
  19.2 4.0 %collective-permute-start.10 = (bf16[2,16,320]{2,1,0:T(8,128)(2,1)S(1)}, bf16[2,16,320]{2,1,0:T(8,128)(2,1)S(1)}, u32[]{:S(2)}, u32[]{:S(2)}) collective-permute-start(bf16[2,16,320]{2,1,0:T(8,128)(2,1)S(1)} %get-tuple-element.42), channel_id=1, source_target_pairs={{2,4},{4,2},{6,8},{8,6},{10,12},{12,10},{14,16},{16,14},{18,20},{2... | collective-permute-start | bytes 61448 | tf_op jit(solution)/shard_map/ppermute | solution.py:224
  20.2 3.8 %collective-permute-start.11 = (bf16[2,16,320]{2,1,0:T(8,128)(2,1)S(1)}, bf16[2,16,320]{2,1,0:T(8,128)(2,1)S(1)}, u32[]{:S(2)}, u32[]{:S(2)}) collective-permute-start(bf16[2,16,320]{2,1,0:T(8,128)(2,1)S(1)} %get-tuple-element.43), channel_id=1, source_target_pairs={{0,1},{1,0},{2,3},{3,2},{4,5},{5,4},{6,7},{7,6},{8,9},{9,8},{10,11... | collective-permute-start | bytes 61448 | tf_op jit(solution)/shard_map/ppermute | solution.py:226
  21.3 1.2 %collective-permute-start.9 = (bf16[16,320]{1,0:T(8,128)(2,1)S(1)}, bf16[16,320]{1,0:T(8,128)(2,1)S(1)}, u32[]{:S(2)}, u32[]{:S(2)}) collective-permute-start(bf16[16,320]{1,0:T(8,128)(2,1)S(1)} %get-tuple-element.41), channel_id=1, source_target_pairs={{0,2},{2,0},{1,3},{3,1},{4,6},{6,4},{5,7},{7,5},{8,10},{10,8},{9,1... | collective-permute-start | bytes 30728 | tf_op jit(solution)/shard_map/ppermute | solution.py:229
  24.6 1.2 %collective-permute-start.12 = (f32[16,128]{1,0:T(8,128)S(1)}, f32[16,128]{1,0:T(8,128)S(1)}, u32[]{:S(2)}, u32[]{:S(2)}) collective-permute-start(f32[16,128]{1,0:T(8,128)S(1)} %get-tuple-element.45), channel_id=1, source_target_pairs={{0,2},{2,0},{1,3},{3,1},{4,6},{6,4},{5,7},{7,5},{8,10},{10,8},{9,1... | collective-permute-start | bytes 24584 | tf_op jit(solution)/shard_map/ppermute | solution.py:286
  38.3 1.2 %collective-permute-start.13 = (f32[16,128]{1,0:T(8,128)S(1)}, f32[16,128]{1,0:T(8,128)S(1)}, u32[]{:S(2)}, u32[]{:S(2)}) collective-permute-start(f32[16,128]{1,0:T(8,128)S(1)} %reduce_sum.9.mine_ref), channel_id=1, source_target_pairs={{0,2},{2,0},{1,3},{3,1},{4,6},{6,4},{5,7},{7,5},{8,10},{10,8},{9,1... | collective-permute-start | bytes 24584 | tf_op jit(solution)/shard_map/ppermute | solution.py:289

commit v4 on v3

v4 whole, which is shorter than its diff:
```python
import functools

import jax
import jax.numpy as jnp
from jax import lax
from jax.experimental import pallas as pl
from jax.experimental.pallas import tpu as pltpu
from jax.sharding import Mesh
from jax.sharding import PartitionSpec as P

S = 4
H = 1
CORES = 2

VMEM = pl.BlockSpec(memory_space=pltpu.VMEM)
HBM = pl.BlockSpec(memory_space=pltpu.HBM)
SMEM = pl.BlockSpec(memory_space=pltpu.SMEM)


def start_kernel(*refs):
    half = len(refs) // 2
    sems = refs[-1]
    copies = [pltpu.make_async_copy(a, b, sems.at[i]) for i, (a, b) in enumerate(zip(refs[:half], refs[half:-1]))]
    for copy in copies:
        copy.start()
    for copy in copies:
        copy.wait()


def inner_kernel(offsets_ref, v_ref, chip_ref, blocks_ref, acc_ref):
    count, kinds = blocks_ref.shape[:2]
    core = lax.axis_index("core")
    halo = chip_ref[core * (count - 1)] if len(chip_ref.shape) == 3 else chip_ref[...]
    for e in range(count):
        total = None
        for k in range(kinds):
            col = e + offsets_ref[k, 0, e]
            inside = jnp.logical_and(col >= 0, col < count)
            lhs = v_ref[jnp.clip(col, 0, count - 1)]
            if e == 0 or e == count - 1:
                near = jnp.logical_or(
                    jnp.logical_and(col < 0, core == 1), jnp.logical_and(col >= count, core == 0)
                )
                lhs = jnp.where(inside, lhs, jnp.where(near, halo, jnp.zeros_like(lhs)))
            part = jnp.dot(lhs, blocks_ref[e, k], preferred_element_type=jnp.float32)
            total = part if total is None else total + part
        acc_ref[e] = total


def next_field(
    grids, first, offsets_ref, donor_ref, fringe_ref, weight_ref, live_ref, acc_ref, blocks_ref, halo_ref, others
):
    count, kinds = blocks_ref.shape[:2]
    last = count - 1
    chips = lax.axis_size("chip")
    chip, core, grid = (lax.axis_index(a) for a in ("chip", "core", "grid"))
    there = jnp.where(core == 0, chip > 0, chip < chips - 1)
    edge = core * last
    halo = halo_ref[last - edge] if first else halo_ref[0]
    product = None
    for k in range(kinds):
        used = jnp.logical_and(offsets_ref[k, 0, edge] == jnp.where(core == 0, -H, H), there)
        lhs = jnp.where(used, halo, jnp.zeros_like(halo))
        part = jnp.dot(lhs, blocks_ref[edge, k], preferred_element_type=jnp.float32)
        product = part if product is None else product + part
    totals = [acc_ref[e] for e in range(count)]
    for s, other in enumerate(others):
        g = lax.rem(grid + grids - 1 - s, grids)
        for c in range(donor_ref.shape[3]):
            target = jnp.where(c < live_ref[0, 0, g], fringe_ref[0, 0, g, c], -1)
            weight = weight_ref[0, 0, g, c]
            value = other[donor_ref[0, 0, g, c] if first else c].astype(jnp.float32)
            for e in range(count):
                totals[e] = totals[e] + jnp.where(target == e, weight, 0.0) * value
    for e in {0, last}:
        totals[e] = totals[e] + jnp.where(edge == e, product, jnp.zeros_like(product))
    return totals


def outer_kernel(grids, first, *refs):
    take = lambda refs, m: (refs[:m], refs[m:])
    shared, rest = take(refs, 7)
    halo, rest = ((), rest) if first else take(rest, 1)
    asked, rest = take(rest, grids - 1)
    others, rest = take(rest, grids - 1)
    halo, rest = take(rest, 1) if first else (halo, rest)
    v_ref, side_ref, chip_ref, *sends = rest
    totals = next_field(grids, first, *shared, *halo, others)
    count = len(totals)
    fields = [t.astype(jnp.bfloat16) for t in totals]
    for e in range(count):
        v_ref[e] = fields[e]
    start = lax.axis_index("core") == 0
    near, far = (jnp.where(start, *pair) for pair in ((fields[0], fields[-1]), (fields[-1], fields[0])))
    side_ref[0] = near
    side_ref[1] = far
    chip_ref[...] = far
    row = lax.broadcasted_iota(jnp.int32, asked[0].shape[2:], 0) if asked else None
    for s, send_ref in enumerate(sends):
        wish = jnp.where(row == lax.axis_index("grid"), asked[grids - 2 - s][0, 0], 0)
        wish = jnp.sum(wish.astype(jnp.float32), axis=0, keepdims=True)
        for c in range(send_ref.shape[0]):
            index = jnp.broadcast_to(wish[:, c : c + 1], totals[0].shape)
            picked = totals[0]
            for e in range(1, count):
                picked = jnp.where(index == e, totals[e], picked)
            send_ref[c] = picked.astype(jnp.bfloat16)


def early_gram_kernel(*refs):
    fields, (one_ref, two_ref) = refs[:S], refs[S:]
    count, n = fields[0].shape[:2]
    total = None
    for e in range(count):
        rows = jnp.concatenate([f[e] for f in fields], axis=0)
        part = lax.dot_general(rows, rows, (((1,), (1,)), ((), ())), preferred_element_type=jnp.float32)
        total = part if total is None else total + part
    b = lambda i, j0, j1: total[i * n : (i + 1) * n, j0 * n : j1 * n]
    blank = jnp.zeros((n, n), jnp.float32)
    one_ref[...] = jnp.concatenate([*[blank] * (S + 1), b(3, 0, 3)], axis=1)
    two_ref[...] = jnp.concatenate([b(3, 3, 4), b(2, 0, 3), b(1, 0, 2), b(0, 0, 1), blank], axis=1)


def last_kernel(grids, *refs):
    shared, rest = refs[:8], refs[8:]
    others, rest = rest[: grids - 1], rest[grids - 1 :]
    fields, (one_ref, two_ref, v_ref, keep_ref, send_ref) = rest[:S], rest[S:]
    n, width = one_ref.shape
    total = None
    for e, values in enumerate(next_field(grids, False, *shared, others)):
        power = values.astype(jnp.bfloat16)
        v_ref[e] = power
        blank = jnp.zeros((width - (S + 1) * n, power.shape[1]), power.dtype)
        rows = jnp.concatenate([*[f[e] for f in fields], power, blank], axis=0)
        part = lax.dot_general(power, rows, (((1,), (1,)), ((), ())), preferred_element_type=jnp.float32)
        total = part if total is None else total + part
    one, two = total + one_ref[...], two_ref[...]
    first = lax.axis_index("core") == 0
    keep_ref[...] = jnp.where(first, one, two)
    send_ref[...] = jnp.where(first, two, one)


def cholesky_rows(panels, height, r_ref):
    size = len(panels) * height
    count = len(panels)
    lane = lax.broadcasted_iota(jnp.int32, (height, size), 1)
    sub = lax.broadcasted_iota(jnp.int32, (height, size), 0)
    panels = list(panels)
    row = lambda x, c: jnp.broadcast_to(x[c : c + 1], (height, size))
    wide = lambda p, j: jnp.broadcast_to(panels[p][:, j : j + 1], (height, size))
    ahead = {c: wide(0, c) for c in range(height)}
    for q in range(count):
        base = q * height
        more = 2 * height if q + 1 < count else height
        side = {(c, p): wide(p, base + c) for c in range(height) for p in range(q + 1, count)}
        side.update({(c, q): ahead[c] for c in range(height)})
        if q + 1 < count:
            side.update({(c, p): wide(p, base + c) for c in range(height, more) for p in (q, q + 1)})
        out = jnp.zeros((height, size), jnp.float32)
        for c in range(height):
            one = row(panels[q], c)
            a = row(side[c, q], c)
            inv = 1.0 / a
            out = jnp.where(sub == c, one * lax.rsqrt(a), out)
            if c + 1 == height and q + 1 == count:
                break
            tops = {e: row(side[e, q], c) for e in range(c + 1, more)}
            scaled = one * inv
            for p in range(q, count):
                if p == q and c + 1 == height:
                    continue
                x = side[c, p] * inv
                panels[p] = panels[p] - x * one
                for e in range(c + 1, more):
                    if (e, p) in side:
                        side[e, p] = side[e, p] - x * tops[e]
        ahead = {c: side[height + c, q + 1] for c in range(height)} if q + 1 < count else {}
        r_ref[base : base + height, :] = jnp.where(lane >= sub + base, out, 0.0)


def factor_kernel(scale, mine_ref, other_ref, r_ref):
    first = lax.axis_index("core") == 0
    mine, other = mine_ref[...] * scale, other_ref[...] * scale
    one, two = jnp.where(first, mine, other), jnp.where(first, other, mine)
    n = one.shape[0]
    size = (S + 1) * n
    b = lambda x, j0, j1: x[:, j0 * n : j1 * n]
    wide = lambda x: jnp.concatenate([x, jnp.zeros((n, size - x.shape[1]), jnp.float32)], axis=1)
    low = jnp.concatenate([
        wide(b(two, 6, 7)),
        wide(b(two, 4, 6)),
        wide(b(two, 1, 4)),
        wide(jnp.concatenate([b(one, 5, 8), b(two, 0, 1)], axis=1)),
        b(one, 0, 5),
    ], axis=0)
    row = lax.broadcasted_iota(jnp.int32, (size, size), 0)
    col = lax.broadcasted_iota(jnp.int32, (size, size), 1)
    a = jnp.where(row >= col, low, low.T)
    height = 8
    cholesky_rows([a[i : i + height] for i in range(0, size, height)], height, r_ref)


def local(rhs, blocks, offsets, donor_elem, fringe_elem, donor_weight, fringe_count):
    _, elem_count, n, unknowns = rhs.shape
    chips, cores, grids = (lax.axis_size(a) for a in ("chip", "core", "grid"))
    axes = ("chip", "core", "grid")
    at = lambda chip, core, grid: (chip * cores + core) * grids + grid % grids
    side = []
    for g in range(grids):
        for chip in range(chips - 1):
            side += [(at(chip, 1, g), at(chip + 1, 0, g)), (at(chip + 1, 0, g), at(chip, 1, g))]
        side += [(at(0, 0, g), at(0, 0, g + 1)), (at(chips - 1, 1, g), at(chips - 1, 1, g + 1))]
    swap = [(0, 1), (1, 0)]

    around = [[(g, (g + s) % grids) for g in range(grids)] for s in range(1, grids)]

    def exchange(to_side, to_chip, *to_grids):
        from_side = lax.ppermute(to_side, axes, side)
        others = [lax.ppermute(v, "grid", pairs) for v, pairs in zip(to_grids, around)]
        return from_side, lax.ppermute(to_chip, "core", swap), others

    slots = donor_elem.shape[3]
    halo_type = jax.ShapeDtypeStruct((n, unknowns), jnp.bfloat16)
    side_type = jax.ShapeDtypeStruct((2, n, unknowns), jnp.bfloat16)
    donor_type = jax.ShapeDtypeStruct((slots, n, unknowns), jnp.bfloat16)
    field_type = jax.ShapeDtypeStruct((elem_count, n, unknowns), jnp.bfloat16)
    acc_type = jax.ShapeDtypeStruct((elem_count, n, unknowns), jnp.float32)
    half_type = jax.ShapeDtypeStruct((n, 8 * n), jnp.float32)
    limit = pltpu.CompilerParams(vmem_limit_bytes=24 << 20)
    rhs, blocks = rhs[0], blocks[0]
    flops = 2 * blocks.size * n
    cost = pl.CostEstimate(flops=flops, bytes_accessed=blocks.size * 2, transcendentals=0)

    small = (jnp.transpose(offsets, (2, 0, 1)), donor_elem, fringe_elem, donor_weight, fringe_count)
    messages = exchange(rhs, rhs, *[rhs] * (grids - 1))
    asked = [lax.ppermute(donor_elem, "grid", pairs) for pairs in around]
    field, *small = pl.pallas_call(
        start_kernel,
        out_shape=(field_type, *(pltpu.SMEM(x.shape, x.dtype) for x in small)),
        in_specs=[HBM] * 6, out_specs=(VMEM, *[SMEM] * 5),
        scratch_shapes=[pltpu.SemaphoreType.DMA((6,))],
        compiler_params=limit, name="start",
        cost_estimate=pl.CostEstimate(flops=2 * 10**9, bytes_accessed=10**6, transcendentals=0),
    )(*(pltpu.with_memory_space_constraint(x, pltpu.HBM) for x in (rhs, *small)))
    basis = [field]
    for level in range(S):
        from_side, from_chip, others = messages
        acc = pl.pallas_call(
            inner_kernel, out_shape=acc_type, in_specs=[SMEM, VMEM, VMEM, VMEM], out_specs=VMEM,
            compiler_params=limit, name="inner", cost_estimate=cost,
        )(small[0], field, from_chip, blocks)
        shared = (*small, acc, blocks)
        if level + 1 < S:
            field, *sends = pl.pallas_call(
                functools.partial(outer_kernel, grids, level == 0),
                out_shape=(field_type, side_type, halo_type, *[donor_type] * (grids - 1)),
                in_specs=[SMEM] * 5 + [VMEM] * (3 + 2 * (grids - 1)),
                out_specs=(VMEM,) * (3 + grids - 1),
                compiler_params=limit, name="outer",
            )(*shared, *((*asked, *others, from_side) if level == 0 else (from_side, *asked, *others)))
            messages = exchange(*sends)
        else:
            early = pl.pallas_call(
                early_gram_kernel, out_shape=(half_type, half_type),
                in_specs=[VMEM] * S, out_specs=(VMEM, VMEM), compiler_params=limit, name="early_gram", cost_estimate=cost,
            )(*basis)
            field, keep, send = pl.pallas_call(
                functools.partial(last_kernel, grids), out_shape=(field_type, half_type, half_type),
                in_specs=[SMEM] * 5 + [VMEM] * (3 + grids - 1 + S + 2), out_specs=(VMEM,) * 3,
                compiler_params=limit, name="last",
            )(*shared, from_side, *others, *basis, *early)
        basis.append(field)
    half = keep + lax.ppermute(send, "core", swap)
    parts = lax.all_to_all(jnp.broadcast_to(half[None], (chips * grids, n, 8 * n)), ("chip", "grid"), 0, 0, tiled=True)
    mine = parts.sum(axis=0)
    other = lax.ppermute(mine, "core", swap)
    columns = (S + 1) * n
    row_total = grids * chips * cores * elem_count * unknowns
    r_factor = pl.pallas_call(
        functools.partial(factor_kernel, 1.0 / row_total),
        out_shape=jax.ShapeDtypeStruct((columns, columns), jnp.float32),
        in_specs=[VMEM] * 2, out_specs=VMEM,
        compiler_params=limit, name="factor",
    )(mine, other)
    powers = jnp.stack(basis[1:], axis=1)[None]
    return (powers, r_factor)


def solution(mesh):
    dom, grids = mesh.shape["dom"], mesh.shape["grid"]
    split = Mesh(mesh.devices.reshape(dom // CORES, CORES, grids), ("chip", "core", "grid"))
    where = ("chip", "core")
    in_specs = (
        P("grid", where, None, None),
        P("grid", where, None, None, None),
        P("grid", where, None),
        P("grid", where, None, None),
        P("grid", where, None, None),
        P("grid", where, None, None),
        P("grid", where, None),
    )
    out_specs = (P("grid", where, None, None, None), P())
    return jax.shard_map(local, mesh=split, in_specs=in_specs, out_specs=out_specs, check_vma=False)
```

time: 42.3 us -> 41.7 us (0.986)
  blocking collectives: 12.5 us -> 11.8 us
  starting transfers between devices: 11 us -> 11.5 us
    ppermute x4, starting transfers between devices: 3.21 us -> 6.29 us  [exchange(): from_side = lax.ppermute(to_side, axes, side)]
    ppermute x4 -> x5, starting transfers between devices: 6.14 us -> 3.74 us  [the longest x4 3.06 us: exchange(): lax.ppermute(v, 'grid', pairs)]
    ppermute x4 -> x5, waiting for transfers between devices: 2.53 us -> 4.1 us  [the longest x4 2.73 us: exchange(): lax.ppermute(v, 'grid', pairs)]
    ppermute x4, waiting for transfers between devices: 4.06 us -> 3.23 us  [exchange(): return (from_side, lax.ppermute(to_chip, 'core', swap), others)]
    ppermute x4, waiting for transfers between devices: 0.7 us -> 0.02 us  [exchange(): from_side = lax.ppermute(to_side, axes, side)]
    all_to_all x1, blocking collectives: 12.5 us -> 11.8 us  [local(): lax.all_to_all(jnp.broadcast_to(half[None], (chips * grids, n, 8 * n)), (...]
    pallas_call x7 -> x6, Pallas kernels: 2.81 us -> 2.4 us  [the longest x1 0.98 us: local(): pl.pallas_call(start_kernel, out_shape=(field_type, *(pltpu.SMEM(x.shape,...]
  transfers between devices with their start and end apart: 14 -> 15, of which waited for: 11 -> 9; matrix products, arithmetic and copies ran while one was open for 2% -> 2% of each run, Pallas kernels for 8% -> 10%
where the time goes in v4:
time: 41.7 us; the launch traced here: 41.6 us
  blocking collectives  11.8 us (28%)
  starting transfers between devices  11.5 us (28%)
  waiting for transfers between devices  8.84 us (21%)
  Pallas kernels  7.85 us (19%)
  local copies, waits for them, and re-layouts  0.76 us (2%)
  between operations  0.76 us (2%)
    all_to_all x1, blocking collectives, local(): lax.all_to_all(jnp.broadcast_to(half[None], (chips * grids, n, 8 * n)), (...  11.8 us
    ppermute x4, starting transfers between devices, exchange(): from_side = lax.ppermute(to_side, axes, side)  6.29 us
    ppermute x4, waiting for transfers between devices, exchange(): return (from_side, lax.ppermute(to_chip, 'core', swap), others)  3.23 us
    ppermute x4, starting transfers between devices, exchange(): lax.ppermute(v, 'grid', pairs)  3.06 us
    pallas_call x4, Pallas kernels, local(): pl.pallas_call(inner_kernel, out_shape=acc_type, in_specs=[SMEM, VMEM, VM...  2.91 us
    ppermute x4, waiting for transfers between devices, exchange(): lax.ppermute(v, 'grid', pairs)  2.73 us
    pallas_call x1, Pallas kernels, local(): pl.pallas_call(functools.partial(factor_kernel, 1.0 / row_total), out_sha...  2.54 us
    ppermute x1, waiting for transfers between devices, local(): asked = [lax.ppermute(donor_elem, 'grid', pairs) for pairs in around]  1.37 us
  transfers between devices with their start and end apart: 15, of which 9 were waited for; matrix products, arithmetic and copies ran while one was open for 2% of the time, Pallas kernels for 10%

profile of v4, /device:TPU:0, one launch (start us, length us, event | category | flops | bytes accessed | tf_op | source)
XLA Modules:
  0.0 41.6 jit_solution(5220552705167276387)
XLA Ops:
  0.6 3.0 %collective-permute-start.3 = (bf16[6,16,320]{2,1,0:T(8,128)(2,1)}, bf16[6,16,320]{2,1,0:T(8,128)(2,1)S(1)}, u32[]{:S(2)}, u32[]{:S(2)}) collective-permute-start(bf16[6,16,320]{2,1,0:T(8,128)(2,1)} %bitcast.21), channel_id=1, source_target_pairs={{2,4},{4,2},{6,8},{8,6},{10,12},{12,10},{14,16},{16,14},{18,20},{2... | collective-permute-start | bytes 184328 | tf_op jit(solution)/shard_map/ppermute | solution.py:218
  3.6 0.1 collective-permute-start.2
  3.7 1.3 %collective-permute-start = (bf16[6,16,320]{2,1,0:T(8,128)(2,1)}, bf16[6,16,320]{2,1,0:T(8,128)(2,1)S(1)}, u32[]{:S(2)}, u32[]{:S(2)}) collective-permute-start(bf16[6,16,320]{2,1,0:T(8,128)(2,1)} %bitcast.23), channel_id=1, source_target_pairs={{0,2},{2,0},{1,3},{3,1},{4,6},{6,4},{5,7},{7,5},{8,10},{10,8},{9,1... | collective-permute-start | bytes 184328 | tf_op jit(solution)/shard_map/ppermute | solution.py:220
  5.0 0.7 %collective-permute-start.1 = (s32[1,1,2,2]{3,2,1,0:T(2,128)}, s32[1,1,2,2]{3,2,1,0:T(2,128)S(1)}, u32[]{:S(2)}, u32[]{:S(2)}) collective-permute-start(s32[1,1,2,2]{3,2,1,0:T(2,128)} %refs_2_.1), channel_id=1, source_target_pairs={{0,1},{1,0},{2,3},{3,2},{4,5},{5,4},{6,7},{7,6},{8,9},{9,8},{10,11... | collective-permute-start | bytes 56 | tf_op jit(solution)/shard_map/ppermute | solution.py:236
  5.7 1.0 %start.1 = (bf16[6,16,320]{2,1,0:T(8,128)(2,1)S(1)}, s32[3,1,6]{2,1,0:T(1,128)S(4)}, s32[1,1,2,2]{3,2,1,0:T(2,128)S(4)}, s32[1,1,2,2]{3,2,1,0:T(2,128)S(4)}, f32...) custom-call(bf16[6,16,320]{2,1,0:T(8,128)(2,1)} %bitcast.24, s32[3,1,6]{2,1,0:T(1,128)} %bitcast.25, ...), custom_call_target="tpu_custom_call" | custom-call | flops 2000000000 | bytes 1000000 | tf_op jit(solution)/shard_map/start/pallas_call | solution.py:237
  6.7 0.7 %inner.4.refs_5_ = f32[6,16,320]{2,1,0:T(8,128)S(1)} custom-call(s32[3,1,6]{2,1,0:T(1,128)S(4)} %get-tuple-element.25.offsets_ref.refs_0_, bf16[6,16,320]{2,1,0:T(8,128)(2,1)S(1)} %get-tuple-element.30.v_ref.refs_0_.refs_9_, bf16[6,16,320]{2,1,0:T(8,128)(2,1)S(1)} %collective-permute-done.chip_ref, bf16[6,3,320,320]{3,2,1,0:T(8,128)(2,1)S(1)} %bitcast.9), custom_call_target="tpu_custom_call" | custom-call | flops 58982400 | bytes 3686400 | tf_op jit(solution)/shard_map/inner/pallas_call | solution.py:248
  7.4 1.4 %collective-permute-done.1.refs_7_.refs_8_ = s32[1,1,2,2]{3,2,1,0:T(2,128)S(1)} collective-permute-done((s32[1,1,2,2]{3,2,1,0:T(2,128)}, s32[1,1,2,2]{3,2,1,0:T(2,128)S(1)}, u32[]{:S(2)}, u32[]{:S(2)}) %collective-permute-start.1) | collective-permute-done | bytes 48 | tf_op jit(solution)/shard_map/ppermute | solution.py:236
  8.8 0.2 outer.3
  9.0 1.1 %collective-permute-start.5 = (bf16[2,16,320]{2,1,0:T(8,128)(2,1)S(1)}, bf16[2,16,320]{2,1,0:T(8,128)(2,1)S(1)}, u32[]{:S(2)}, u32[]{:S(2)}) collective-permute-start(bf16[2,16,320]{2,1,0:T(8,128)(2,1)S(1)} %get-tuple-element.33), channel_id=1, source_target_pairs={{2,4},{4,2},{6,8},{8,6},{10,12},{12,10},{14,16},{16,14},{18,20},{2... | collective-permute-start | bytes 61448 | tf_op jit(solution)/shard_map/ppermute | solution.py:218
  10.2 1.0 %collective-permute-start.6 = (bf16[2,16,320]{2,1,0:T(8,128)(2,1)S(1)}, bf16[2,16,320]{2,1,0:T(8,128)(2,1)S(1)}, u32[]{:S(2)}, u32[]{:S(2)}) collective-permute-start(bf16[2,16,320]{2,1,0:T(8,128)(2,1)S(1)} %get-tuple-element.34), channel_id=1, source_target_pairs={{0,1},{1,0},{2,3},{3,2},{4,5},{5,4},{6,7},{7,6},{8,9},{9,8},{10,11... | collective-permute-start | bytes 61448 | tf_op jit(solution)/shard_map/ppermute | solution.py:219
  11.1 1.2 %collective-permute-done.4.chip_ref = bf16[16,320]{1,0:T(8,128)(2,1)S(1)} collective-permute-done((bf16[16,320]{1,0:T(8,128)(2,1)S(1)}, bf16[16,320]{1,0:T(8,128)(2,1)S(1)}, u32[]{:S(2)}, u32[]{:S(2)}) %collective-permute-start.4) | collective-permute-done | bytes 10272 | tf_op jit(solution)/shard_map/ppermute | solution.py:220
  12.3 0.7 %inner.5.refs_5_ = f32[6,16,320]{2,1,0:T(8,128)S(1)} custom-call(s32[3,1,6]{2,1,0:T(1,128)S(4)} %get-tuple-element.25.offsets_ref.refs_0_, bf16[6,16,320]{2,1,0:T(8,128)(2,1)S(1)} %get-tuple-element.31.v_ref.refs_1_.refs_10_, bf16[16,320]{1,0:T(8,128)(2,1)S(1)} %collective-permute-done.4.chip_ref, bf16[6,3,320,320]{3,2,1,0:T(8,128)(2,1)S(1)} %bitcast.11), custom_call_target="tpu_custom_call" | custom-call | flops 58982400 | bytes 3686400 | tf_op jit(solution)/shard_map/inner/pallas_call | solution.py:248
  13.0 0.9 %collective-permute-done.6.refs_9_ = bf16[2,16,320]{2,1,0:T(8,128)(2,1)S(1)} collective-permute-done((bf16[2,16,320]{2,1,0:T(8,128)(2,1)S(1)}, bf16[2,16,320]{2,1,0:T(8,128)(2,1)S(1)}, u32[]{:S(2)}, u32[]{:S(2)}) %collective-permute-start.6) | collective-permute-done | bytes 20512 | tf_op jit(solution)/shard_map/ppermute | solution.py:219
  14.0 0.2 outer.4
  14.2 1.0 %collective-permute-start.8 = (bf16[2,16,320]{2,1,0:T(8,128)(2,1)S(1)}, bf16[2,16,320]{2,1,0:T(8,128)(2,1)S(1)}, u32[]{:S(2)}, u32[]{:S(2)}) collective-permute-start(bf16[2,16,320]{2,1,0:T(8,128)(2,1)S(1)} %get-tuple-element.37), channel_id=1, source_target_pairs={{2,4},{4,2},{6,8},{8,6},{10,12},{12,10},{14,16},{16,14},{18,20},{2... | collective-permute-start | bytes 61448 | tf_op jit(solution)/shard_map/ppermute | solution.py:218
  15.3 1.1 %collective-permute-start.9 = (bf16[2,16,320]{2,1,0:T(8,128)(2,1)S(1)}, bf16[2,16,320]{2,1,0:T(8,128)(2,1)S(1)}, u32[]{:S(2)}, u32[]{:S(2)}) collective-permute-start(bf16[2,16,320]{2,1,0:T(8,128)(2,1)S(1)} %get-tuple-element.38), channel_id=1, source_target_pairs={{0,1},{1,0},{2,3},{3,2},{4,5},{5,4},{6,7},{7,6},{8,9},{9,8},{10,11... | collective-permute-start | bytes 61448 | tf_op jit(solution)/shard_map/ppermute | solution.py:219
  16.3 1.2 %collective-permute-done.7.chip_ref = bf16[16,320]{1,0:T(8,128)(2,1)S(1)} collective-permute-done((bf16[16,320]{1,0:T(8,128)(2,1)S(1)}, bf16[16,320]{1,0:T(8,128)(2,1)S(1)}, u32[]{:S(2)}, u32[]{:S(2)}) %collective-permute-start.7) | collective-permute-done | bytes 10272 | tf_op jit(solution)/shard_map/ppermute | solution.py:220
  17.5 0.7 %inner.6.refs_5_ = f32[6,16,320]{2,1,0:T(8,128)S(1)} custom-call(s32[3,1,6]{2,1,0:T(1,128)S(4)} %get-tuple-element.25.offsets_ref.refs_0_, bf16[6,16,320]{2,1,0:T(8,128)(2,1)S(1)} %get-tuple-element.35.v_ref.refs_2_.refs_11_, bf16[16,320]{1,0:T(8,128)(2,1)S(1)} %collective-permute-done.7.chip_ref, bf16[6,3,320,320]{3,2,1,0:T(8,128)(2,1)S(1)} %bitcast.13), custom_call_target="tpu_custom_call" | custom-call | flops 58982400 | bytes 3686400 | tf_op jit(solution)/shard_map/inner/pallas_call | solution.py:248
  18.2 0.8 %collective-permute-done.9.refs_9_ = bf16[2,16,320]{2,1,0:T(8,128)(2,1)S(1)} collective-permute-done((bf16[2,16,320]{2,1,0:T(8,128)(2,1)S(1)}, bf16[2,16,320]{2,1,0:T(8,128)(2,1)S(1)}, u32[]{:S(2)}, u32[]{:S(2)}) %collective-permute-start.9) | collective-permute-done | bytes 20512 | tf_op jit(solution)/shard_map/ppermute | solution.py:219
  19.1 0.2 outer.5
  19.3 1.1 %collective-permute-start.11 = (bf16[2,16,320]{2,1,0:T(8,128)(2,1)S(1)}, bf16[2,16,320]{2,1,0:T(8,128)(2,1)S(1)}, u32[]{:S(2)}, u32[]{:S(2)}) collective-permute-start(bf16[2,16,320]{2,1,0:T(8,128)(2,1)S(1)} %get-tuple-element.41), channel_id=1, source_target_pairs={{2,4},{4,2},{6,8},{8,6},{10,12},{12,10},{14,16},{16,14},{18,20},{2... | collective-permute-start | bytes 61448 | tf_op jit(solution)/shard_map/ppermute | solution.py:218
  20.5 1.0 %collective-permute-start.12 = (bf16[2,16,320]{2,1,0:T(8,128)(2,1)S(1)}, bf16[2,16,320]{2,1,0:T(8,128)(2,1)S(1)}, u32[]{:S(2)}, u32[]{:S(2)}) collective-permute-start(bf16[2,16,320]{2,1,0:T(8,128)(2,1)S(1)} %get-tuple-element.42), channel_id=1, source_target_pairs={{0,1},{1,0},{2,3},{3,2},{4,5},{5,4},{6,7},{7,6},{8,9},{9,8},{10,11... | collective-permute-start | bytes 61448 | tf_op jit(solution)/shard_map/ppermute | solution.py:219
  21.4 0.3 early_gram.1
  21.7 0.9 %collective-permute-done.10.chip_ref = bf16[16,320]{1,0:T(8,128)(2,1)S(1)} collective-permute-done((bf16[16,320]{1,0:T(8,128)(2,1)S(1)}, bf16[16,320]{1,0:T(8,128)(2,1)S(1)}, u32[]{:S(2)}, u32[]{:S(2)}) %collective-permute-start.10) | collective-permute-done | bytes 10272 | tf_op jit(solution)/shard_map/ppermute | solution.py:220
  22.6 0.7 %inner.7.refs_5_ = f32[6,16,320]{2,1,0:T(8,128)S(1)} custom-call(s32[3,1,6]{2,1,0:T(1,128)S(4)} %get-tuple-element.25.offsets_ref.refs_0_, bf16[6,16,320]{2,1,0:T(8,128)(2,1)S(1)} %get-tuple-element.39.v_ref.refs_3_.refs_12_, bf16[16,320]{1,0:T(8,128)(2,1)S(1)} %collective-permute-done.10.chip_ref, bf16[6,3,320,320]{3,2,1,0:T(8,128)(2,1)S(1)} %bitcast.15), custom_call_target="tpu_custom_call" | custom-call | flops 58982400 | bytes 3686400 | tf_op jit(solution)/shard_map/inner/pallas_call | solution.py:248
  23.3 0.9 %collective-permute-done.12.refs_8_ = bf16[2,16,320]{2,1,0:T(8,128)(2,1)S(1)} collective-permute-done((bf16[2,16,320]{2,1,0:T(8,128)(2,1)S(1)}, bf16[2,16,320]{2,1,0:T(8,128)(2,1)S(1)}, u32[]{:S(2)}, u32[]{:S(2)}) %collective-permute-start.12) | collective-permute-done | bytes 20512 | tf_op jit(solution)/shard_map/ppermute | solution.py:219
  24.3 0.4 %last.1 = (bf16[6,16,320]{2,1,0:T(8,128)(2,1)S(1)}, f32[16,128]{1,0:T(8,128)S(1)}, f32[16,128]{1,0:T(8,128)S(1)}) custom-call(s32[3,1,6]{2,1,0:T(1,128)S(4)} %get-tuple-element.25.offsets_ref.refs_0_, s32[1,1,2,2]{3,2,1,0:T(2,128)S(4)} %get-tuple-element.26.refs_1_, s32[1,1,2,2]{3,2,1,0:T(2,128)S(4)} %get-tuple-element.27.refs_2_, ...), custom_call_target="tpu_custom_call" | custom-call | tf_op jit(solution)/shard_map/last/pallas_call | solution.py:267
  24.8 1.2 %collective-permute-done.13 = f32[16,128]{1,0:T(8,128)S(1)} collective-permute-done((f32[16,128]{1,0:T(8,128)S(1)}, f32[16,128]{1,0:T(8,128)S(1)}, u32[]{:S(2)}, u32[]{:S(2)}) %collective-permute-start.13) | collective-permute-done | bytes 8224 | tf_op jit(solution)/shard_map/ppermute | solution.py:273
  26.0 11.8 %all_to_all.5 = f32[16,16,128]{2,1,0:T(8,128)S(1)} all-to-all(f32[16,16,128]{2,1,0:T(8,128)S(1)} %broadcast_in_dim.10), channel_id=1, replica_groups=mesh['chip'=8,'core'=2,'grid'=2] {'chip','grid'}, dimensions={0} | all-to-all | bytes 262144 | tf_op jit(solution)/shard_map/all_to_all | solution.py:274
  37.9 0.7 %copy.10 = bf16[1,6,4,16,320]{4,3,2,1,0:T(8,128)(2,1)} copy(bf16[1,6,4,16,320]{4,3,1,2,0:T(8,128)(2,1)S(1)} %maximum_bitcast_fusion) | data formatting | bytes 491520
  38.7 0.3 collective-permute-done.14.other_ref
  39.0 2.5 %factor.1 = f32[80,80]{1,0:T(8,128)} custom-call(f32[16,128]{1,0:T(8,128)S(1)} %reduce_sum.9.mine_ref, f32[16,128]{1,0:T(8,128)S(1)} %collective-permute-done.14.other_ref), custom_call_target="tpu_custom_call" | custom-call | tf_op jit(solution)/shard_map/factor/pallas_call | solution.py:279
  (17 shorter events, 0.3 us)
Async XLA Ops:
  0.6 6.0 %copy-start = (bf16[1,6,3,320,320]{4,3,2,1,0:T(8,128)(2,1)S(1)}, bf16[1,6,3,320,320]{4,3,2,1,0:T(8,128)(2,1)}, u32[]{:S(2)}) copy-start(bf16[1,6,3,320,320]{4,3,2,1,0:T(8,128)(2,1)} %param.8) | copy-start | bytes 11059204
  0.6 8.1 %collective-permute-start.3 = (bf16[6,16,320]{2,1,0:T(8,128)(2,1)}, bf16[6,16,320]{2,1,0:T(8,128)(2,1)S(1)}, u32[]{:S(2)}, u32[]{:S(2)}) collective-permute-start(bf16[6,16,320]{2,1,0:T(8,128)(2,1)} %bitcast.21), channel_id=1, source_target_pairs={{2,4},{4,2},{6,8},{8,6},{10,12},{12,10},{14,16},{16,14},{18,20},{2... | collective-permute-start | bytes 184328 | tf_op jit(solution)/shard_map/ppermute | solution.py:218
  3.6 5.1 %collective-permute-start.2 = (bf16[6,16,320]{2,1,0:T(8,128)(2,1)}, bf16[6,16,320]{2,1,0:T(8,128)(2,1)S(1)}, u32[]{:S(2)}, u32[]{:S(2)}) collective-permute-start(bf16[6,16,320]{2,1,0:T(8,128)(2,1)} %bitcast.22), channel_id=1, source_target_pairs={{0,1},{1,0},{2,3},{3,2},{4,5},{5,4},{6,7},{7,6},{8,9},{9,8},{10,11... | collective-permute-start | bytes 184328 | tf_op jit(solution)/shard_map/ppermute | solution.py:219
  3.7 2.9 %collective-permute-start = (bf16[6,16,320]{2,1,0:T(8,128)(2,1)}, bf16[6,16,320]{2,1,0:T(8,128)(2,1)S(1)}, u32[]{:S(2)}, u32[]{:S(2)}) collective-permute-start(bf16[6,16,320]{2,1,0:T(8,128)(2,1)} %bitcast.23), channel_id=1, source_target_pairs={{0,2},{2,0},{1,3},{3,1},{4,6},{6,4},{5,7},{7,5},{8,10},{10,8},{9,1... | collective-permute-start | bytes 184328 | tf_op jit(solution)/shard_map/ppermute | solution.py:220
  5.0 3.8 %collective-permute-start.1 = (s32[1,1,2,2]{3,2,1,0:T(2,128)}, s32[1,1,2,2]{3,2,1,0:T(2,128)S(1)}, u32[]{:S(2)}, u32[]{:S(2)}) collective-permute-start(s32[1,1,2,2]{3,2,1,0:T(2,128)} %refs_2_.1), channel_id=1, source_target_pairs={{0,1},{1,0},{2,3},{3,2},{4,5},{5,4},{6,7},{7,6},{8,9},{9,8},{10,11... | collective-permute-start | bytes 56 | tf_op jit(solution)/shard_map/ppermute | solution.py:236
  9.0 4.0 %collective-permute-start.5 = (bf16[2,16,320]{2,1,0:T(8,128)(2,1)S(1)}, bf16[2,16,320]{2,1,0:T(8,128)(2,1)S(1)}, u32[]{:S(2)}, u32[]{:S(2)}) collective-permute-start(bf16[2,16,320]{2,1,0:T(8,128)(2,1)S(1)} %get-tuple-element.33), channel_id=1, source_target_pairs={{2,4},{4,2},{6,8},{8,6},{10,12},{12,10},{14,16},{16,14},{18,20},{2... | collective-permute-start | bytes 61448 | tf_op jit(solution)/shard_map/ppermute | solution.py:218
  10.2 3.8 %collective-permute-start.6 = (bf16[2,16,320]{2,1,0:T(8,128)(2,1)S(1)}, bf16[2,16,320]{2,1,0:T(8,128)(2,1)S(1)}, u32[]{:S(2)}, u32[]{:S(2)}) collective-permute-start(bf16[2,16,320]{2,1,0:T(8,128)(2,1)S(1)} %get-tuple-element.34), channel_id=1, source_target_pairs={{0,1},{1,0},{2,3},{3,2},{4,5},{5,4},{6,7},{7,6},{8,9},{9,8},{10,11... | collective-permute-start | bytes 61448 | tf_op jit(solution)/shard_map/ppermute | solution.py:219
  11.1 1.2 %collective-permute-start.4 = (bf16[16,320]{1,0:T(8,128)(2,1)S(1)}, bf16[16,320]{1,0:T(8,128)(2,1)S(1)}, u32[]{:S(2)}, u32[]{:S(2)}) collective-permute-start(bf16[16,320]{1,0:T(8,128)(2,1)S(1)} %get-tuple-element.32), channel_id=1, source_target_pairs={{0,2},{2,0},{1,3},{3,1},{4,6},{6,4},{5,7},{7,5},{8,10},{10,8},{9,1... | collective-permute-start | bytes 30728 | tf_op jit(solution)/shard_map/ppermute | solution.py:220
  14.2 4.0 %collective-permute-start.8 = (bf16[2,16,320]{2,1,0:T(8,128)(2,1)S(1)}, bf16[2,16,320]{2,1,0:T(8,128)(2,1)S(1)}, u32[]{:S(2)}, u32[]{:S(2)}) collective-permute-start(bf16[2,16,320]{2,1,0:T(8,128)(2,1)S(1)} %get-tuple-element.37), channel_id=1, source_target_pairs={{2,4},{4,2},{6,8},{8,6},{10,12},{12,10},{14,16},{16,14},{18,20},{2... | collective-permute-start | bytes 61448 | tf_op jit(solution)/shard_map/ppermute | solution.py:218
  15.3 3.8 %collective-permute-start.9 = (bf16[2,16,320]{2,1,0:T(8,128)(2,1)S(1)}, bf16[2,16,320]{2,1,0:T(8,128)(2,1)S(1)}, u32[]{:S(2)}, u32[]{:S(2)}) collective-permute-start(bf16[2,16,320]{2,1,0:T(8,128)(2,1)S(1)} %get-tuple-element.38), channel_id=1, source_target_pairs={{0,1},{1,0},{2,3},{3,2},{4,5},{5,4},{6,7},{7,6},{8,9},{9,8},{10,11... | collective-permute-start | bytes 61448 | tf_op jit(solution)/shard_map/ppermute | solution.py:219
  16.3 1.2 %collective-permute-start.7 = (bf16[16,320]{1,0:T(8,128)(2,1)S(1)}, bf16[16,320]{1,0:T(8,128)(2,1)S(1)}, u32[]{:S(2)}, u32[]{:S(2)}) collective-permute-start(bf16[16,320]{1,0:T(8,128)(2,1)S(1)} %get-tuple-element.36), channel_id=1, source_target_pairs={{0,2},{2,0},{1,3},{3,1},{4,6},{6,4},{5,7},{7,5},{8,10},{10,8},{9,1... | collective-permute-start | bytes 30728 | tf_op jit(solution)/shard_map/ppermute | solution.py:220
  19.3 4.0 %collective-permute-start.11 = (bf16[2,16,320]{2,1,0:T(8,128)(2,1)S(1)}, bf16[2,16,320]{2,1,0:T(8,128)(2,1)S(1)}, u32[]{:S(2)}, u32[]{:S(2)}) collective-permute-start(bf16[2,16,320]{2,1,0:T(8,128)(2,1)S(1)} %get-tuple-element.41), channel_id=1, source_target_pairs={{2,4},{4,2},{6,8},{8,6},{10,12},{12,10},{14,16},{16,14},{18,20},{2... | collective-permute-start | bytes 61448 | tf_op jit(solution)/shard_map/ppermute | solution.py:218
  20.5 3.8 %collective-permute-start.12 = (bf16[2,16,320]{2,1,0:T(8,128)(2,1)S(1)}, bf16[2,16,320]{2,1,0:T(8,128)(2,1)S(1)}, u32[]{:S(2)}, u32[]{:S(2)}) collective-permute-start(bf16[2,16,320]{2,1,0:T(8,128)(2,1)S(1)} %get-tuple-element.42), channel_id=1, source_target_pairs={{0,1},{1,0},{2,3},{3,2},{4,5},{5,4},{6,7},{7,6},{8,9},{9,8},{10,11... | collective-permute-start | bytes 61448 | tf_op jit(solution)/shard_map/ppermute | solution.py:219
  21.4 1.2 %collective-permute-start.10 = (bf16[16,320]{1,0:T(8,128)(2,1)S(1)}, bf16[16,320]{1,0:T(8,128)(2,1)S(1)}, u32[]{:S(2)}, u32[]{:S(2)}) collective-permute-start(bf16[16,320]{1,0:T(8,128)(2,1)S(1)} %get-tuple-element.40), channel_id=1, source_target_pairs={{0,2},{2,0},{1,3},{3,1},{4,6},{6,4},{5,7},{7,5},{8,10},{10,8},{9,1... | collective-permute-start | bytes 30728 | tf_op jit(solution)/shard_map/ppermute | solution.py:220
  24.7 1.2 %collective-permute-start.13 = (f32[16,128]{1,0:T(8,128)S(1)}, f32[16,128]{1,0:T(8,128)S(1)}, u32[]{:S(2)}, u32[]{:S(2)}) collective-permute-start(f32[16,128]{1,0:T(8,128)S(1)} %get-tuple-element.47), channel_id=1, source_target_pairs={{0,2},{2,0},{1,3},{3,1},{4,6},{6,4},{5,7},{7,5},{8,10},{10,8},{9,1... | collective-permute-start | bytes 24584 | tf_op jit(solution)/shard_map/ppermute | solution.py:273
  37.8 1.2 %collective-permute-start.14 = (f32[16,128]{1,0:T(8,128)S(1)}, f32[16,128]{1,0:T(8,128)S(1)}, u32[]{:S(2)}, u32[]{:S(2)}) collective-permute-start(f32[16,128]{1,0:T(8,128)S(1)} %reduce_sum.9.mine_ref), channel_id=1, source_target_pairs={{0,2},{2,0},{1,3},{3,1},{4,6},{6,4},{5,7},{7,5},{8,10},{10,8},{9,1... | collective-permute-start | bytes 24584 | tf_op jit(solution)/shard_map/ppermute | solution.py:276

commit v5 on v4

--- a/solution.py
+++ b/solution.py
@@ -27,43 +27,50 @@
         copy.wait()
 
 
-def inner_kernel(offsets_ref, v_ref, chip_ref, blocks_ref, acc_ref):
+def inner_kernel(offsets_ref, v_ref, blocks_ref, acc_ref):
     count, kinds = blocks_ref.shape[:2]
-    core = lax.axis_index("core")
-    halo = chip_ref[core * (count - 1)] if len(chip_ref.shape) == 3 else chip_ref[...]
     for e in range(count):
         total = None
         for k in range(kinds):
             col = e + offsets_ref[k, 0, e]
             inside = jnp.logical_and(col >= 0, col < count)
             lhs = v_ref[jnp.clip(col, 0, count - 1)]
-            if e == 0 or e == count - 1:
-                near = jnp.logical_or(
-                    jnp.logical_and(col < 0, core == 1), jnp.logical_and(col >= count, core == 0)
-                )
-                lhs = jnp.where(inside, lhs, jnp.where(near, halo, jnp.zeros_like(lhs)))
+            lhs = jnp.where(inside, lhs, jnp.zeros_like(lhs))
             part = jnp.dot(lhs, blocks_ref[e, k], preferred_element_type=jnp.float32)
             total = part if total is None else total + part
         acc_ref[e] = total
 
 
-def next_field(
-    grids, first, offsets_ref, donor_ref, fringe_ref, weight_ref, live_ref, acc_ref, blocks_ref, halo_ref, others
-):
+def edge_product(in_chip, offsets_ref, halo_ref, blocks_ref):
     count, kinds = blocks_ref.shape[:2]
     last = count - 1
-    chips = lax.axis_size("chip")
-    chip, core, grid = (lax.axis_index(a) for a in ("chip", "core", "grid"))
-    there = jnp.where(core == 0, chip > 0, chip < chips - 1)
-    edge = core * last
-    halo = halo_ref[last - edge] if first else halo_ref[0]
-    product = None
+    chip, core = lax.axis_index("chip"), lax.axis_index("core")
+    upper = core == 0 if in_chip else core == 1
+    edge = jnp.where(upper, last, 0)
+    there = True if in_chip else jnp.where(core == 0, chip > 0, chip < lax.axis_size("chip") - 1)
+    halo = halo_ref[...]
+    if len(halo_ref.shape) == 3:
+        halo = halo_ref[last - edge] if halo_ref.shape[0] == count else halo_ref[0]
+    total = None
     for k in range(kinds):
-        used = jnp.logical_and(offsets_ref[k, 0, edge] == jnp.where(core == 0, -H, H), there)
+        used = jnp.logical_and(offsets_ref[k, 0, edge] == jnp.where(upper, H, -H), there)
         lhs = jnp.where(used, halo, jnp.zeros_like(halo))
         part = jnp.dot(lhs, blocks_ref[edge, k], preferred_element_type=jnp.float32)
-        product = part if product is None else product + part
+        total = part if total is None else total + part
+    return total
+
+
+def edge_kernel(in_chip, offsets_ref, halo_ref, blocks_ref, out_ref):
+    out_ref[...] = edge_product(in_chip, offsets_ref, halo_ref, blocks_ref)
+
+
+def next_field(grids, first, donor_ref, fringe_ref, weight_ref, live_ref, acc_ref, chip_ref, side, others):
+    count = acc_ref.shape[0]
+    core, grid = lax.axis_index("core"), lax.axis_index("grid")
     totals = [acc_ref[e] for e in range(count)]
+    chip = chip_ref[...]
+    totals[0] = totals[0] + jnp.where(core == 0, side, chip)
+    totals[-1] = totals[-1] + jnp.where(core == 0, chip, side)
     for s, other in enumerate(others):
         g = lax.rem(grid + grids - 1 - s, grids)
         for c in range(donor_ref.shape[3]):
@@ -72,20 +79,18 @@
             value = other[donor_ref[0, 0, g, c] if first else c].astype(jnp.float32)
             for e in range(count):
                 totals[e] = totals[e] + jnp.where(target == e, weight, 0.0) * value
-    for e in {0, last}:
-        totals[e] = totals[e] + jnp.where(edge == e, product, jnp.zeros_like(product))
     return totals
 
 
 def outer_kernel(grids, first, *refs):
     take = lambda refs, m: (refs[:m], refs[m:])
-    shared, rest = take(refs, 7)
-    halo, rest = ((), rest) if first else take(rest, 1)
+    shared, rest = take(refs, 6)
     asked, rest = take(rest, grids - 1)
     others, rest = take(rest, grids - 1)
-    halo, rest = take(rest, 1) if first else (halo, rest)
+    side, rest = take(rest, 3 if first else 1)
     v_ref, side_ref, chip_ref, *sends = rest
-    totals = next_field(grids, first, *shared, *halo, others)
+    side = edge_product(False, *side) if first else side[0][...]
+    totals = next_field(grids, first, *shared, side, others)
     count = len(totals)
     fields = [t.astype(jnp.bfloat16) for t in totals]
     for e in range(count):
@@ -122,12 +127,13 @@
 
 
 def last_kernel(grids, *refs):
-    shared, rest = refs[:8], refs[8:]
+    shared, rest = refs[:6], refs[6:]
     others, rest = rest[: grids - 1], rest[grids - 1 :]
+    side_ref, *rest = rest
     fields, (one_ref, two_ref, v_ref, keep_ref, send_ref) = rest[:S], rest[S:]
     n, width = one_ref.shape
     total = None
-    for e, values in enumerate(next_field(grids, False, *shared, others)):
+    for e, values in enumerate(next_field(grids, False, *shared, side_ref[...], others)):
         power = values.astype(jnp.bfloat16)
         v_ref[e] = power
         blank = jnp.zeros((width - (S + 1) * n, power.shape[1]), power.dtype)
@@ -224,17 +230,19 @@
     side_type = jax.ShapeDtypeStruct((2, n, unknowns), jnp.bfloat16)
     donor_type = jax.ShapeDtypeStruct((slots, n, unknowns), jnp.bfloat16)
     field_type = jax.ShapeDtypeStruct((elem_count, n, unknowns), jnp.bfloat16)
+    edge_type = jax.ShapeDtypeStruct((n, unknowns), jnp.float32)
     acc_type = jax.ShapeDtypeStruct((elem_count, n, unknowns), jnp.float32)
     half_type = jax.ShapeDtypeStruct((n, 8 * n), jnp.float32)
     limit = pltpu.CompilerParams(vmem_limit_bytes=24 << 20)
     rhs, blocks = rhs[0], blocks[0]
     flops = 2 * blocks.size * n
     cost = pl.CostEstimate(flops=flops, bytes_accessed=blocks.size * 2, transcendentals=0)
+    edge_cost = pl.CostEstimate(flops=flops // elem_count, bytes_accessed=blocks.size * 2 // elem_count, transcendentals=0)
 
     small = (jnp.transpose(offsets, (2, 0, 1)), donor_elem, fringe_elem, donor_weight, fringe_count)
     messages = exchange(rhs, rhs, *[rhs] * (grids - 1))
     asked = [lax.ppermute(donor_elem, "grid", pairs) for pairs in around]
-    field, *small = pl.pallas_call(
+    field, offset, *small = pl.pallas_call(
         start_kernel,
         out_shape=(field_type, *(pltpu.SMEM(x.shape, x.dtype) for x in small)),
         in_specs=[HBM] * 6, out_specs=(VMEM, *[SMEM] * 5),
@@ -246,18 +254,23 @@
     for level in range(S):
         from_side, from_chip, others = messages
         acc = pl.pallas_call(
-            inner_kernel, out_shape=acc_type, in_specs=[SMEM, VMEM, VMEM, VMEM], out_specs=VMEM,
+            inner_kernel, out_shape=acc_type, in_specs=[SMEM, VMEM, VMEM], out_specs=VMEM,
             compiler_params=limit, name="inner", cost_estimate=cost,
-        )(small[0], field, from_chip, blocks)
-        shared = (*small, acc, blocks)
+        )(offset, field, blocks)
+        edge = lambda in_chip, halo: pl.pallas_call(
+            functools.partial(edge_kernel, in_chip), out_shape=edge_type, in_specs=[SMEM, VMEM, VMEM], out_specs=VMEM,
+            compiler_params=limit, name="chip_edge" if in_chip else "side_edge", cost_estimate=edge_cost,
+        )(offset, halo, blocks)
+        shared = (*small, acc, edge(True, from_chip))
+        side_in = (offset, from_side, blocks) if level == 0 else (edge(False, from_side),)
         if level + 1 < S:
             field, *sends = pl.pallas_call(
                 functools.partial(outer_kernel, grids, level == 0),
                 out_shape=(field_type, side_type, halo_type, *[donor_type] * (grids - 1)),
-                in_specs=[SMEM] * 5 + [VMEM] * (3 + 2 * (grids - 1)),
+                in_specs=[SMEM] * 4 + [VMEM] * (2 + 2 * (grids - 1)) + ([SMEM] if level == 0 else []) + [VMEM] * len(side_in[-2:]),
                 out_specs=(VMEM,) * (3 + grids - 1),
                 compiler_params=limit, name="outer",
-            )(*shared, *((*asked, *others, from_side) if level == 0 else (from_side, *asked, *others)))
+            )(*shared, *asked, *others, *side_in)
             messages = exchange(*sends)
         else:
             early = pl.pallas_call(
@@ -266,9 +279,9 @@
             )(*basis)
             field, keep, send = pl.pallas_call(
                 functools.partial(last_kernel, grids), out_shape=(field_type, half_type, half_type),
-                in_specs=[SMEM] * 5 + [VMEM] * (3 + grids - 1 + S + 2), out_specs=(VMEM,) * 3,
+                in_specs=[SMEM] * 4 + [VMEM] * (3 + grids - 1 + S + 2), out_specs=(VMEM,) * 3,
                 compiler_params=limit, name="last",
-            )(*shared, from_side, *others, *basis, *early)
+            )(*shared, *others, *side_in, *basis, *early)
         basis.append(field)
     half = keep + lax.ppermute(send, "core", swap)
     parts = lax.all_to_all(jnp.broadcast_to(half[None], (chips * grids, n, 8 * n)), ("chip", "grid"), 0, 0, tiled=True)

time: 41.7 us -> 41.4 us (level)
  waiting for transfers between devices: 8.84 us -> 7.46 us
  Pallas kernels: 7.85 us -> 8.75 us
    ppermute x4, waiting for transfers between devices: 3.23 us -> 1.03 us  [exchange(): return (from_side, lax.ppermute(to_chip, 'core', swap), others)]
    pallas_call x0 -> x7, Pallas kernels: none -> 1.34 us  [local(): pl.pallas_call(functools.partial(edge_kernel, in_chip), out_shape=edge_ty...]
    ppermute x4, waiting for transfers between devices: 0.02 us -> 1.28 us  [exchange(): from_side = lax.ppermute(to_side, axes, side)]
  transfers between devices with their start and end apart: 15 -> 15, of which waited for: 9 -> 12; matrix products, arithmetic and copies ran while one was open for 2% -> 2% of each run, Pallas kernels for 10% -> 13%
where the time goes in v5:
time: 41.4 us; the launch traced here: 41.2 us
  blocking collectives  11.9 us (29%)
  starting transfers between devices  11.5 us (28%)
  Pallas kernels  8.75 us (21%)
  waiting for transfers between devices  7.46 us (18%)
  between operations  0.79 us (2%)
  local copies, waits for them, and re-layouts  0.76 us (2%)
    all_to_all x1, blocking collectives, local(): lax.all_to_all(jnp.broadcast_to(half[None], (chips * grids, n, 8 * n)), (...  11.9 us
    ppermute x4, starting transfers between devices, exchange(): from_side = lax.ppermute(to_side, axes, side)  6.29 us
    ppermute x4, starting transfers between devices, exchange(): lax.ppermute(v, 'grid', pairs)  3.06 us
    pallas_call x4, Pallas kernels, local(): pl.pallas_call(inner_kernel, out_shape=acc_type, in_specs=[SMEM, VMEM, VM...  2.93 us
    pallas_call x1, Pallas kernels, local(): pl.pallas_call(functools.partial(factor_kernel, 1.0 / row_total), out_sha...  2.54 us
    ppermute x4, waiting for transfers between devices, exchange(): lax.ppermute(v, 'grid', pairs)  2.5 us
    pallas_call x7, Pallas kernels, local(): pl.pallas_call(functools.partial(edge_kernel, in_chip), out_shape=edge_ty...  1.34 us
    ppermute x4, starting transfers between devices, exchange(): return (from_side, lax.ppermute(to_chip, 'core', swap), others)  1.28 us
  transfers between devices with their start and end apart: 15, of which 12 were waited for; matrix products, arithmetic and copies ran while one was open for 2% of the time, Pallas kernels for 13%

profile of v5, /device:TPU:0, one launch (start us, length us, event | category | flops | bytes accessed | tf_op | source)
XLA Modules:
  0.0 41.2 jit_solution(13892879610022913977)
XLA Ops:
  0.6 3.0 %collective-permute-start.3 = (bf16[6,16,320]{2,1,0:T(8,128)(2,1)}, bf16[6,16,320]{2,1,0:T(8,128)(2,1)S(1)}, u32[]{:S(2)}, u32[]{:S(2)}) collective-permute-start(bf16[6,16,320]{2,1,0:T(8,128)(2,1)} %bitcast.25), channel_id=1, source_target_pairs={{2,4},{4,2},{6,8},{8,6},{10,12},{12,10},{14,16},{16,14},{18,20},{2... | collective-permute-start | bytes 184328 | tf_op jit(solution)/shard_map/ppermute | solution.py:224
  3.7 1.3 %collective-permute-start = (bf16[6,16,320]{2,1,0:T(8,128)(2,1)}, bf16[6,16,320]{2,1,0:T(8,128)(2,1)S(1)}, u32[]{:S(2)}, u32[]{:S(2)}) collective-permute-start(bf16[6,16,320]{2,1,0:T(8,128)(2,1)} %bitcast.27), channel_id=1, source_target_pairs={{0,2},{2,0},{1,3},{3,1},{4,6},{6,4},{5,7},{7,5},{8,10},{10,8},{9,1... | collective-permute-start | bytes 184328 | tf_op jit(solution)/shard_map/ppermute | solution.py:226
  5.0 0.7 %collective-permute-start.1 = (s32[1,1,2,2]{3,2,1,0:T(2,128)}, s32[1,1,2,2]{3,2,1,0:T(2,128)S(1)}, u32[]{:S(2)}, u32[]{:S(2)}) collective-permute-start(s32[1,1,2,2]{3,2,1,0:T(2,128)} %refs_2_.1), channel_id=1, source_target_pairs={{0,1},{1,0},{2,3},{3,2},{4,5},{5,4},{6,7},{7,6},{8,9},{9,8},{10,11... | collective-permute-start | bytes 56 | tf_op jit(solution)/shard_map/ppermute | solution.py:244
  5.7 1.0 %start.1 = (bf16[6,16,320]{2,1,0:T(8,128)(2,1)S(1)}, s32[3,1,6]{2,1,0:T(1,128)S(4)}, s32[1,1,2,2]{3,2,1,0:T(2,128)S(4)}, s32[1,1,2,2]{3,2,1,0:T(2,128)S(4)}, f32...) custom-call(bf16[6,16,320]{2,1,0:T(8,128)(2,1)} %bitcast.28, s32[3,1,6]{2,1,0:T(1,128)} %bitcast.29, ...), custom_call_target="tpu_custom_call" | custom-call | flops 2000000000 | bytes 1000000 | tf_op jit(solution)/shard_map/start/pallas_call | solution.py:245
  6.7 0.7 %inner.4.refs_4_ = f32[6,16,320]{2,1,0:T(8,128)S(1)} custom-call(s32[3,1,6]{2,1,0:T(1,128)S(4)} %get-tuple-element.29.offsets_ref.refs_8_, bf16[6,16,320]{2,1,0:T(8,128)(2,1)S(1)} %get-tuple-element.30.v_ref.refs_0_.refs_8_, bf16[6,3,320,320]{3,2,1,0:T(8,128)(2,1)S(1)} %bitcast.9), custom_call_target="tpu_custom_call" | custom-call | flops 58982400 | bytes 3686400 | tf_op jit(solution)/shard_map/inner/pallas_call | solution.py:256
  7.4 0.2 chip_edge.4.refs_5_
  7.6 1.2 %collective-permute-done.1.refs_6_ = s32[1,1,2,2]{3,2,1,0:T(2,128)S(1)} collective-permute-done((s32[1,1,2,2]{3,2,1,0:T(2,128)}, s32[1,1,2,2]{3,2,1,0:T(2,128)S(1)}, u32[]{:S(2)}, u32[]{:S(2)}) %collective-permute-start.1) | collective-permute-done | bytes 48 | tf_op jit(solution)/shard_map/ppermute | solution.py:244
  8.8 0.2 outer.3
  9.0 1.1 %collective-permute-start.6 = (bf16[2,16,320]{2,1,0:T(8,128)(2,1)S(1)}, bf16[2,16,320]{2,1,0:T(8,128)(2,1)S(1)}, u32[]{:S(2)}, u32[]{:S(2)}) collective-permute-start(bf16[2,16,320]{2,1,0:T(8,128)(2,1)S(1)} %get-tuple-element.34), channel_id=1, source_target_pairs={{2,4},{4,2},{6,8},{8,6},{10,12},{12,10},{14,16},{16,14},{18,20},{2... | collective-permute-start | bytes 61448 | tf_op jit(solution)/shard_map/ppermute | solution.py:224
  10.2 1.0 %collective-permute-start.5 = (bf16[2,16,320]{2,1,0:T(8,128)(2,1)S(1)}, bf16[2,16,320]{2,1,0:T(8,128)(2,1)S(1)}, u32[]{:S(2)}, u32[]{:S(2)}) collective-permute-start(bf16[2,16,320]{2,1,0:T(8,128)(2,1)S(1)} %get-tuple-element.33), channel_id=1, source_target_pairs={{0,1},{1,0},{2,3},{3,2},{4,5},{5,4},{6,7},{7,6},{8,9},{9,8},{10,11... | collective-permute-start | bytes 61448 | tf_op jit(solution)/shard_map/ppermute | solution.py:225
  11.1 0.7 %inner.5.refs_4_ = f32[6,16,320]{2,1,0:T(8,128)S(1)} custom-call(s32[3,1,6]{2,1,0:T(1,128)S(4)} %get-tuple-element.29.offsets_ref.refs_8_, bf16[6,16,320]{2,1,0:T(8,128)(2,1)S(1)} %get-tuple-element.31.v_ref.refs_1_.refs_9_, bf16[6,3,320,320]{3,2,1,0:T(8,128)(2,1)S(1)} %bitcast.12), custom_call_target="tpu_custom_call" | custom-call | flops 58982400 | bytes 3686400 | tf_op jit(solution)/shard_map/inner/pallas_call | solution.py:256
  11.9 0.4 %collective-permute-done.4.halo_ref = bf16[16,320]{1,0:T(8,128)(2,1)S(1)} collective-permute-done((bf16[16,320]{1,0:T(8,128)(2,1)S(1)}, bf16[16,320]{1,0:T(8,128)(2,1)S(1)}, u32[]{:S(2)}, u32[]{:S(2)}) %collective-permute-start.4) | collective-permute-done | bytes 10272 | tf_op jit(solution)/shard_map/ppermute | solution.py:226
  12.5 0.4 %collective-permute-done.6.halo_ref = bf16[2,16,320]{2,1,0:T(8,128)(2,1)S(1)} collective-permute-done((bf16[2,16,320]{2,1,0:T(8,128)(2,1)S(1)}, bf16[2,16,320]{2,1,0:T(8,128)(2,1)S(1)}, u32[]{:S(2)}, u32[]{:S(2)}) %collective-permute-start.6) | collective-permute-done | bytes 20512 | tf_op jit(solution)/shard_map/ppermute | solution.py:224
  13.1 0.9 %collective-permute-done.5.refs_7_ = bf16[2,16,320]{2,1,0:T(8,128)(2,1)S(1)} collective-permute-done((bf16[2,16,320]{2,1,0:T(8,128)(2,1)S(1)}, bf16[2,16,320]{2,1,0:T(8,128)(2,1)S(1)}, u32[]{:S(2)}, u32[]{:S(2)}) %collective-permute-start.5) | collective-permute-done | bytes 20512 | tf_op jit(solution)/shard_map/ppermute | solution.py:225
  14.1 1.0 %collective-permute-start.9 = (bf16[2,16,320]{2,1,0:T(8,128)(2,1)S(1)}, bf16[2,16,320]{2,1,0:T(8,128)(2,1)S(1)}, u32[]{:S(2)}, u32[]{:S(2)}) collective-permute-start(bf16[2,16,320]{2,1,0:T(8,128)(2,1)S(1)} %get-tuple-element.38), channel_id=1, source_target_pairs={{2,4},{4,2},{6,8},{8,6},{10,12},{12,10},{14,16},{16,14},{18,20},{2... | collective-permute-start | bytes 61448 | tf_op jit(solution)/shard_map/ppermute | solution.py:224
  15.1 1.1 %collective-permute-start.8 = (bf16[2,16,320]{2,1,0:T(8,128)(2,1)S(1)}, bf16[2,16,320]{2,1,0:T(8,128)(2,1)S(1)}, u32[]{:S(2)}, u32[]{:S(2)}) collective-permute-start(bf16[2,16,320]{2,1,0:T(8,128)(2,1)S(1)} %get-tuple-element.37), channel_id=1, source_target_pairs={{0,1},{1,0},{2,3},{3,2},{4,5},{5,4},{6,7},{7,6},{8,9},{9,8},{10,11... | collective-permute-start | bytes 61448 | tf_op jit(solution)/shard_map/ppermute | solution.py:225
  16.2 0.7 %inner.6.refs_4_ = f32[6,16,320]{2,1,0:T(8,128)S(1)} custom-call(s32[3,1,6]{2,1,0:T(1,128)S(4)} %get-tuple-element.29.offsets_ref.refs_8_, bf16[6,16,320]{2,1,0:T(8,128)(2,1)S(1)} %get-tuple-element.35.v_ref.refs_2_.refs_10_, bf16[6,3,320,320]{3,2,1,0:T(8,128)(2,1)S(1)} %bitcast.15), custom_call_target="tpu_custom_call" | custom-call | flops 58982400 | bytes 3686400 | tf_op jit(solution)/shard_map/inner/pallas_call | solution.py:256
  16.9 0.4 %collective-permute-done.7.halo_ref = bf16[16,320]{1,0:T(8,128)(2,1)S(1)} collective-permute-done((bf16[16,320]{1,0:T(8,128)(2,1)S(1)}, bf16[16,320]{1,0:T(8,128)(2,1)S(1)}, u32[]{:S(2)}, u32[]{:S(2)}) %collective-permute-start.7) | collective-permute-done | bytes 10272 | tf_op jit(solution)/shard_map/ppermute | solution.py:226
  17.6 0.4 %collective-permute-done.9.halo_ref = bf16[2,16,320]{2,1,0:T(8,128)(2,1)S(1)} collective-permute-done((bf16[2,16,320]{2,1,0:T(8,128)(2,1)S(1)}, bf16[2,16,320]{2,1,0:T(8,128)(2,1)S(1)}, u32[]{:S(2)}, u32[]{:S(2)}) %collective-permute-start.9) | collective-permute-done | bytes 20512 | tf_op jit(solution)/shard_map/ppermute | solution.py:224
  18.2 0.8 %collective-permute-done.8.refs_7_ = bf16[2,16,320]{2,1,0:T(8,128)(2,1)S(1)} collective-permute-done((bf16[2,16,320]{2,1,0:T(8,128)(2,1)S(1)}, bf16[2,16,320]{2,1,0:T(8,128)(2,1)S(1)}, u32[]{:S(2)}, u32[]{:S(2)}) %collective-permute-start.8) | collective-permute-done | bytes 20512 | tf_op jit(solution)/shard_map/ppermute | solution.py:225
  19.0 1.1 %collective-permute-start.12 = (bf16[2,16,320]{2,1,0:T(8,128)(2,1)S(1)}, bf16[2,16,320]{2,1,0:T(8,128)(2,1)S(1)}, u32[]{:S(2)}, u32[]{:S(2)}) collective-permute-start(bf16[2,16,320]{2,1,0:T(8,128)(2,1)S(1)} %get-tuple-element.42), channel_id=1, source_target_pairs={{2,4},{4,2},{6,8},{8,6},{10,12},{12,10},{14,16},{16,14},{18,20},{2... | collective-permute-start | bytes 61448 | tf_op jit(solution)/shard_map/ppermute | solution.py:224
  20.2 1.0 %collective-permute-start.11 = (bf16[2,16,320]{2,1,0:T(8,128)(2,1)S(1)}, bf16[2,16,320]{2,1,0:T(8,128)(2,1)S(1)}, u32[]{:S(2)}, u32[]{:S(2)}) collective-permute-start(bf16[2,16,320]{2,1,0:T(8,128)(2,1)S(1)} %get-tuple-element.41), channel_id=1, source_target_pairs={{0,1},{1,0},{2,3},{3,2},{4,5},{5,4},{6,7},{7,6},{8,9},{9,8},{10,11... | collective-permute-start | bytes 61448 | tf_op jit(solution)/shard_map/ppermute | solution.py:225
  21.1 0.3 early_gram.1
  21.4 0.7 %inner.7.refs_4_ = f32[6,16,320]{2,1,0:T(8,128)S(1)} custom-call(s32[3,1,6]{2,1,0:T(1,128)S(4)} %get-tuple-element.29.offsets_ref.refs_8_, bf16[6,16,320]{2,1,0:T(8,128)(2,1)S(1)} %get-tuple-element.39.v_ref.refs_3_.refs_11_, bf16[6,3,320,320]{3,2,1,0:T(8,128)(2,1)S(1)} %bitcast.18), custom_call_target="tpu_custom_call" | custom-call | flops 58982400 | bytes 3686400 | tf_op jit(solution)/shard_map/inner/pallas_call | solution.py:256
  22.5 0.4 %collective-permute-done.12.halo_ref = bf16[2,16,320]{2,1,0:T(8,128)(2,1)S(1)} collective-permute-done((bf16[2,16,320]{2,1,0:T(8,128)(2,1)S(1)}, bf16[2,16,320]{2,1,0:T(8,128)(2,1)S(1)}, u32[]{:S(2)}, u32[]{:S(2)}) %collective-permute-start.12) | collective-permute-done | bytes 20512 | tf_op jit(solution)/shard_map/ppermute | solution.py:224
  23.1 0.9 %collective-permute-done.11.refs_6_ = bf16[2,16,320]{2,1,0:T(8,128)(2,1)S(1)} collective-permute-done((bf16[2,16,320]{2,1,0:T(8,128)(2,1)S(1)}, bf16[2,16,320]{2,1,0:T(8,128)(2,1)S(1)}, u32[]{:S(2)}, u32[]{:S(2)}) %collective-permute-start.11) | collective-permute-done | bytes 20512 | tf_op jit(solution)/shard_map/ppermute | solution.py:225
  24.0 0.2 last.1
  24.3 1.2 %collective-permute-done.13 = f32[16,128]{1,0:T(8,128)S(1)} collective-permute-done((f32[16,128]{1,0:T(8,128)S(1)}, f32[16,128]{1,0:T(8,128)S(1)}, u32[]{:S(2)}, u32[]{:S(2)}) %collective-permute-start.13) | collective-permute-done | bytes 8224 | tf_op jit(solution)/shard_map/ppermute | solution.py:286
  25.5 11.9 %all_to_all.5 = f32[16,16,128]{2,1,0:T(8,128)S(1)} all-to-all(f32[16,16,128]{2,1,0:T(8,128)S(1)} %broadcast_in_dim.10), channel_id=1, replica_groups=mesh['chip'=8,'core'=2,'grid'=2] {'chip','grid'}, dimensions={0} | all-to-all | bytes 262144 | tf_op jit(solution)/shard_map/all_to_all | solution.py:287
  37.6 0.7 %copy.10 = bf16[1,6,4,16,320]{4,3,2,1,0:T(8,128)(2,1)} copy(bf16[1,6,4,16,320]{4,3,1,2,0:T(8,128)(2,1)S(1)} %maximum_bitcast_fusion) | data formatting | bytes 491520
  38.3 0.3 collective-permute-done.14.other_ref
  38.7 2.5 %factor.1 = f32[80,80]{1,0:T(8,128)} custom-call(f32[16,128]{1,0:T(8,128)S(1)} %reduce_sum.9.mine_ref, f32[16,128]{1,0:T(8,128)S(1)} %collective-permute-done.14.other_ref), custom_call_target="tpu_custom_call" | custom-call | tf_op jit(solution)/shard_map/factor/pallas_call | solution.py:292
  (24 shorter events, 1.8 us)
Async XLA Ops:
  0.6 6.0 %copy-start = (bf16[1,6,3,320,320]{4,3,2,1,0:T(8,128)(2,1)S(1)}, bf16[1,6,3,320,320]{4,3,2,1,0:T(8,128)(2,1)}, u32[]{:S(2)}) copy-start(bf16[1,6,3,320,320]{4,3,2,1,0:T(8,128)(2,1)} %param.8) | copy-start | bytes 11059204
  0.6 8.1 %collective-permute-start.3 = (bf16[6,16,320]{2,1,0:T(8,128)(2,1)}, bf16[6,16,320]{2,1,0:T(8,128)(2,1)S(1)}, u32[]{:S(2)}, u32[]{:S(2)}) collective-permute-start(bf16[6,16,320]{2,1,0:T(8,128)(2,1)} %bitcast.25), channel_id=1, source_target_pairs={{2,4},{4,2},{6,8},{8,6},{10,12},{12,10},{14,16},{16,14},{18,20},{2... | collective-permute-start | bytes 184328 | tf_op jit(solution)/shard_map/ppermute | solution.py:224
  3.6 5.1 %collective-permute-start.2 = (bf16[6,16,320]{2,1,0:T(8,128)(2,1)}, bf16[6,16,320]{2,1,0:T(8,128)(2,1)S(1)}, u32[]{:S(2)}, u32[]{:S(2)}) collective-permute-start(bf16[6,16,320]{2,1,0:T(8,128)(2,1)} %bitcast.26), channel_id=1, source_target_pairs={{0,1},{1,0},{2,3},{3,2},{4,5},{5,4},{6,7},{7,6},{8,9},{9,8},{10,11... | collective-permute-start | bytes 184328 | tf_op jit(solution)/shard_map/ppermute | solution.py:225
  3.7 3.7 %collective-permute-start = (bf16[6,16,320]{2,1,0:T(8,128)(2,1)}, bf16[6,16,320]{2,1,0:T(8,128)(2,1)S(1)}, u32[]{:S(2)}, u32[]{:S(2)}) collective-permute-start(bf16[6,16,320]{2,1,0:T(8,128)(2,1)} %bitcast.27), channel_id=1, source_target_pairs={{0,2},{2,0},{1,3},{3,1},{4,6},{6,4},{5,7},{7,5},{8,10},{10,8},{9,1... | collective-permute-start | bytes 184328 | tf_op jit(solution)/shard_map/ppermute | solution.py:226
  5.0 3.8 %collective-permute-start.1 = (s32[1,1,2,2]{3,2,1,0:T(2,128)}, s32[1,1,2,2]{3,2,1,0:T(2,128)S(1)}, u32[]{:S(2)}, u32[]{:S(2)}) collective-permute-start(s32[1,1,2,2]{3,2,1,0:T(2,128)} %refs_2_.1), channel_id=1, source_target_pairs={{0,1},{1,0},{2,3},{3,2},{4,5},{5,4},{6,7},{7,6},{8,9},{9,8},{10,11... | collective-permute-start | bytes 56 | tf_op jit(solution)/shard_map/ppermute | solution.py:244
  9.0 3.9 %collective-permute-start.6 = (bf16[2,16,320]{2,1,0:T(8,128)(2,1)S(1)}, bf16[2,16,320]{2,1,0:T(8,128)(2,1)S(1)}, u32[]{:S(2)}, u32[]{:S(2)}) collective-permute-start(bf16[2,16,320]{2,1,0:T(8,128)(2,1)S(1)} %get-tuple-element.34), channel_id=1, source_target_pairs={{2,4},{4,2},{6,8},{8,6},{10,12},{12,10},{14,16},{16,14},{18,20},{2... | collective-permute-start | bytes 61448 | tf_op jit(solution)/shard_map/ppermute | solution.py:224
  10.2 3.8 %collective-permute-start.5 = (bf16[2,16,320]{2,1,0:T(8,128)(2,1)S(1)}, bf16[2,16,320]{2,1,0:T(8,128)(2,1)S(1)}, u32[]{:S(2)}, u32[]{:S(2)}) collective-permute-start(bf16[2,16,320]{2,1,0:T(8,128)(2,1)S(1)} %get-tuple-element.33), channel_id=1, source_target_pairs={{0,1},{1,0},{2,3},{3,2},{4,5},{5,4},{6,7},{7,6},{8,9},{9,8},{10,11... | collective-permute-start | bytes 61448 | tf_op jit(solution)/shard_map/ppermute | solution.py:225
  11.1 1.2 %collective-permute-start.4 = (bf16[16,320]{1,0:T(8,128)(2,1)S(1)}, bf16[16,320]{1,0:T(8,128)(2,1)S(1)}, u32[]{:S(2)}, u32[]{:S(2)}) collective-permute-start(bf16[16,320]{1,0:T(8,128)(2,1)S(1)} %get-tuple-element.32), channel_id=1, source_target_pairs={{0,2},{2,0},{1,3},{3,1},{4,6},{6,4},{5,7},{7,5},{8,10},{10,8},{9,1... | collective-permute-start | bytes 30728 | tf_op jit(solution)/shard_map/ppermute | solution.py:226
  14.1 3.9 %collective-permute-start.9 = (bf16[2,16,320]{2,1,0:T(8,128)(2,1)S(1)}, bf16[2,16,320]{2,1,0:T(8,128)(2,1)S(1)}, u32[]{:S(2)}, u32[]{:S(2)}) collective-permute-start(bf16[2,16,320]{2,1,0:T(8,128)(2,1)S(1)} %get-tuple-element.38), channel_id=1, source_target_pairs={{2,4},{4,2},{6,8},{8,6},{10,12},{12,10},{14,16},{16,14},{18,20},{2... | collective-permute-start | bytes 61448 | tf_op jit(solution)/shard_map/ppermute | solution.py:224
  15.1 3.8 %collective-permute-start.8 = (bf16[2,16,320]{2,1,0:T(8,128)(2,1)S(1)}, bf16[2,16,320]{2,1,0:T(8,128)(2,1)S(1)}, u32[]{:S(2)}, u32[]{:S(2)}) collective-permute-start(bf16[2,16,320]{2,1,0:T(8,128)(2,1)S(1)} %get-tuple-element.37), channel_id=1, source_target_pairs={{0,1},{1,0},{2,3},{3,2},{4,5},{5,4},{6,7},{7,6},{8,9},{9,8},{10,11... | collective-permute-start | bytes 61448 | tf_op jit(solution)/shard_map/ppermute | solution.py:225
  16.2 1.2 %collective-permute-start.7 = (bf16[16,320]{1,0:T(8,128)(2,1)S(1)}, bf16[16,320]{1,0:T(8,128)(2,1)S(1)}, u32[]{:S(2)}, u32[]{:S(2)}) collective-permute-start(bf16[16,320]{1,0:T(8,128)(2,1)S(1)} %get-tuple-element.36), channel_id=1, source_target_pairs={{0,2},{2,0},{1,3},{3,1},{4,6},{6,4},{5,7},{7,5},{8,10},{10,8},{9,1... | collective-permute-start | bytes 30728 | tf_op jit(solution)/shard_map/ppermute | solution.py:226
  19.0 3.9 %collective-permute-start.12 = (bf16[2,16,320]{2,1,0:T(8,128)(2,1)S(1)}, bf16[2,16,320]{2,1,0:T(8,128)(2,1)S(1)}, u32[]{:S(2)}, u32[]{:S(2)}) collective-permute-start(bf16[2,16,320]{2,1,0:T(8,128)(2,1)S(1)} %get-tuple-element.42), channel_id=1, source_target_pairs={{2,4},{4,2},{6,8},{8,6},{10,12},{12,10},{14,16},{16,14},{18,20},{2... | collective-permute-start | bytes 61448 | tf_op jit(solution)/shard_map/ppermute | solution.py:224
  20.2 3.8 %collective-permute-start.11 = (bf16[2,16,320]{2,1,0:T(8,128)(2,1)S(1)}, bf16[2,16,320]{2,1,0:T(8,128)(2,1)S(1)}, u32[]{:S(2)}, u32[]{:S(2)}) collective-permute-start(bf16[2,16,320]{2,1,0:T(8,128)(2,1)S(1)} %get-tuple-element.41), channel_id=1, source_target_pairs={{0,1},{1,0},{2,3},{3,2},{4,5},{5,4},{6,7},{7,6},{8,9},{9,8},{10,11... | collective-permute-start | bytes 61448 | tf_op jit(solution)/shard_map/ppermute | solution.py:225
  21.1 1.2 %collective-permute-start.10 = (bf16[16,320]{1,0:T(8,128)(2,1)S(1)}, bf16[16,320]{1,0:T(8,128)(2,1)S(1)}, u32[]{:S(2)}, u32[]{:S(2)}) collective-permute-start(bf16[16,320]{1,0:T(8,128)(2,1)S(1)} %get-tuple-element.40), channel_id=1, source_target_pairs={{0,2},{2,0},{1,3},{3,1},{4,6},{6,4},{5,7},{7,5},{8,10},{10,8},{9,1... | collective-permute-start | bytes 30728 | tf_op jit(solution)/shard_map/ppermute | solution.py:226
  24.3 1.2 %collective-permute-start.13 = (f32[16,128]{1,0:T(8,128)S(1)}, f32[16,128]{1,0:T(8,128)S(1)}, u32[]{:S(2)}, u32[]{:S(2)}) collective-permute-start(f32[16,128]{1,0:T(8,128)S(1)} %get-tuple-element.47), channel_id=1, source_target_pairs={{0,2},{2,0},{1,3},{3,1},{4,6},{6,4},{5,7},{7,5},{8,10},{10,8},{9,1... | collective-permute-start | bytes 24584 | tf_op jit(solution)/shard_map/ppermute | solution.py:286
  37.4 1.2 %collective-permute-start.14 = (f32[16,128]{1,0:T(8,128)S(1)}, f32[16,128]{1,0:T(8,128)S(1)}, u32[]{:S(2)}, u32[]{:S(2)}) collective-permute-start(f32[16,128]{1,0:T(8,128)S(1)} %reduce_sum.9.mine_ref), channel_id=1, source_target_pairs={{0,2},{2,0},{1,3},{3,1},{4,6},{6,4},{5,7},{7,5},{8,10},{10,8},{9,1... | collective-permute-start | bytes 24584 | tf_op jit(solution)/shard_map/ppermute | solution.py:289

commit v6 on v5

--- a/solution.py
+++ b/solution.py
@@ -1,4 +1,5 @@
 import functools
+import math
 
 import jax
 import jax.numpy as jnp
@@ -130,7 +131,7 @@
     shared, rest = refs[:6], refs[6:]
     others, rest = rest[: grids - 1], rest[grids - 1 :]
     side_ref, *rest = rest
-    fields, (one_ref, two_ref, v_ref, keep_ref, send_ref) = rest[:S], rest[S:]
+    fields, (one_ref, two_ref, v_ref, part_ref) = rest[:S], rest[S:]
     n, width = one_ref.shape
     total = None
     for e, values in enumerate(next_field(grids, False, *shared, side_ref[...], others)):
@@ -140,10 +141,8 @@
         rows = jnp.concatenate([*[f[e] for f in fields], power, blank], axis=0)
         part = lax.dot_general(power, rows, (((1,), (1,)), ((), ())), preferred_element_type=jnp.float32)
         total = part if total is None else total + part
-    one, two = total + one_ref[...], two_ref[...]
-    first = lax.axis_index("core") == 0
-    keep_ref[...] = jnp.where(first, one, two)
-    send_ref[...] = jnp.where(first, two, one)
+    part_ref[0] = total + one_ref[...]
+    part_ref[1] = two_ref[...]
 
 
 def cholesky_rows(panels, height, r_ref):
@@ -184,10 +183,8 @@
         r_ref[base : base + height, :] = jnp.where(lane >= sub + base, out, 0.0)
 
 
-def factor_kernel(scale, mine_ref, other_ref, r_ref):
-    first = lax.axis_index("core") == 0
-    mine, other = mine_ref[...] * scale, other_ref[...] * scale
-    one, two = jnp.where(first, mine, other), jnp.where(first, other, mine)
+def factor_kernel(scale, gram_ref, r_ref):
+    one, two = gram_ref[0] * scale, gram_ref[1] * scale
     n = one.shape[0]
     size = (S + 1) * n
     b = lambda x, j0, j1: x[:, j0 * n : j1 * n]
@@ -206,6 +203,49 @@
     cholesky_rows([a[i : i + height] for i in range(0, size, height)], height, r_ref)
 
 
+def primes(value):
+    found, p = [], 2
+    while value > 1:
+        while value % p == 0:
+            found.append(p)
+            value //= p
+        p += 1
+    return found
+
+
+def sum_stages(chips, grids):
+    digits, step = [], 1
+    for size in primes(chips):
+        digits.append((0, step, size))
+        step *= size
+    step, places = 1, []
+    for size in primes(grids):
+        places.append((1, step, size))
+        step *= size
+    digits[1:1] = places
+
+    def moved(place, digit, by):
+        axis, step, size = digit
+        now = place[axis] // step % size
+        place[axis] += ((now + by) % size - now) * step
+
+    stages = []
+    for i in range(0, len(digits), 2):
+        pair, group = digits[i : i + 2], []
+        for shift in range(1, math.prod(d[2] for d in pair)):
+            pairs = []
+            for chip in range(chips):
+                for core in range(CORES):
+                    for grid in range(grids):
+                        place = [chip, grid]
+                        moved(place, pair[0], shift % pair[0][2])
+                        moved(place, pair[-1], shift // pair[0][2])
+                        pairs.append(((chip * CORES + core) * grids + grid, (place[0] * CORES + 1 - core) * grids + place[1]))
+            group.append(pairs)
+        stages.append(group)
+    return stages
+
+
 def local(rhs, blocks, offsets, donor_elem, fringe_elem, donor_weight, fringe_count):
     _, elem_count, n, unknowns = rhs.shape
     chips, cores, grids = (lax.axis_size(a) for a in ("chip", "core", "grid"))
@@ -233,6 +273,7 @@
     edge_type = jax.ShapeDtypeStruct((n, unknowns), jnp.float32)
     acc_type = jax.ShapeDtypeStruct((elem_count, n, unknowns), jnp.float32)
     half_type = jax.ShapeDtypeStruct((n, 8 * n), jnp.float32)
+    gram_type = jax.ShapeDtypeStruct((2, n, 8 * n), jnp.float32)
     limit = pltpu.CompilerParams(vmem_limit_bytes=24 << 20)
     rhs, blocks = rhs[0], blocks[0]
     flops = 2 * blocks.size * n
@@ -277,24 +318,25 @@
                 early_gram_kernel, out_shape=(half_type, half_type),
                 in_specs=[VMEM] * S, out_specs=(VMEM, VMEM), compiler_params=limit, name="early_gram", cost_estimate=cost,
             )(*basis)
-            field, keep, send = pl.pallas_call(
-                functools.partial(last_kernel, grids), out_shape=(field_type, half_type, half_type),
-                in_specs=[SMEM] * 4 + [VMEM] * (3 + grids - 1 + S + 2), out_specs=(VMEM,) * 3,
+            field, gram = pl.pallas_call(
+                functools.partial(last_kernel, grids), out_shape=(field_type, gram_type),
+                in_specs=[SMEM] * 4 + [VMEM] * (3 + grids - 1 + S + 2), out_specs=(VMEM,) * 2,
                 compiler_params=limit, name="last",
             )(*shared, *others, *side_in, *basis, *early)
         basis.append(field)
-    half = keep + lax.ppermute(send, "core", swap)
-    parts = lax.all_to_all(jnp.broadcast_to(half[None], (chips * grids, n, 8 * n)), ("chip", "grid"), 0, 0, tiled=True)
-    mine = parts.sum(axis=0)
-    other = lax.ppermute(mine, "core", swap)
+    gram = gram + lax.ppermute(gram, "core", swap)
+    for group in sum_stages(chips, grids):
+        arrived = [lax.ppermute(gram, axes, pairs) for pairs in group]
+        for part in arrived:
+            gram = gram + part
     columns = (S + 1) * n
     row_total = grids * chips * cores * elem_count * unknowns
     r_factor = pl.pallas_call(
         functools.partial(factor_kernel, 1.0 / row_total),
         out_shape=jax.ShapeDtypeStruct((columns, columns), jnp.float32),
-        in_specs=[VMEM] * 2, out_specs=VMEM,
+        in_specs=[VMEM], out_specs=VMEM,
         compiler_params=limit, name="factor",
-    )(mine, other)
+    )(gram)
     powers = jnp.stack(basis[1:], axis=1)[None]
     return (powers, r_factor)
 

time: 41.4 us -> 39.4 us (0.952)
  blocking collectives: 11.9 us -> 0 us
  starting transfers between devices: 11.5 us -> 18.2 us
  waiting for transfers between devices: 7.46 us -> 10.6 us
    all_to_all x1 -> x0, blocking collectives: 11.9 us -> none  [local(): lax.all_to_all(jnp.broadcast_to(half[None], (chips * grids, n, 8 * n)), (...]
    ppermute x2 -> x7, starting transfers between devices: 0.14 us -> 6.93 us  [the longest x6 6.86 us: local(): arrived = [lax.ppermute(gram, axes, pairs) for pairs in group]]
    ppermute x2 -> x7, waiting for transfers between devices: 1.49 us -> 4.63 us  [the longest x6 3.46 us: local(): arrived = [lax.ppermute(gram, axes, pairs) for pairs in group]]
  transfers between devices with their start and end apart: 15 -> 20, of which waited for: 12 -> 15; matrix products, arithmetic and copies ran while one was open for 2% -> 2% of each run, Pallas kernels for 13% -> 14%
where the time goes in v6:
time: 39.4 us; the launch traced here: 39.3 us
  starting transfers between devices  18.2 us (46%)
  waiting for transfers between devices  10.6 us (27%)
  Pallas kernels  8.81 us (22%)
  between operations  0.77 us (2%)
  local copies, waits for them, and re-layouts  0.75 us (2%)
    ppermute x6, starting transfers between devices, local(): arrived = [lax.ppermute(gram, axes, pairs) for pairs in group]  6.86 us
    ppermute x4, starting transfers between devices, exchange(): from_side = lax.ppermute(to_side, axes, side)  6.29 us
    ppermute x6, waiting for transfers between devices, local(): arrived = [lax.ppermute(gram, axes, pairs) for pairs in group]  3.46 us
    ppermute x4, starting transfers between devices, exchange(): lax.ppermute(v, 'grid', pairs)  3.06 us
    pallas_call x4, Pallas kernels, local(): pl.pallas_call(inner_kernel, out_shape=acc_type, in_specs=[SMEM, VMEM, VM...  2.93 us
    pallas_call x1, Pallas kernels, local(): pl.pallas_call(functools.partial(factor_kernel, 1.0 / row_total), out_sha...  2.61 us
    ppermute x4, waiting for transfers between devices, exchange(): lax.ppermute(v, 'grid', pairs)  2.5 us
    pallas_call x7, Pallas kernels, local(): pl.pallas_call(functools.partial(edge_kernel, in_chip), out_shape=edge_ty...  1.34 us
  transfers between devices with their start and end apart: 20, of which 15 were waited for; matrix products, arithmetic and copies ran while one was open for 2% of the time, Pallas kernels for 14%

profile of v6, /device:TPU:0, one launch (start us, length us, event | category | flops | bytes accessed | tf_op | source)
XLA Modules:
  0.0 39.3 jit_solution(11770905690995776305)
XLA Ops:
  0.6 3.0 %collective-permute-start.3 = (bf16[6,16,320]{2,1,0:T(8,128)(2,1)}, bf16[6,16,320]{2,1,0:T(8,128)(2,1)S(1)}, u32[]{:S(2)}, u32[]{:S(2)}) collective-permute-start(bf16[6,16,320]{2,1,0:T(8,128)(2,1)} %bitcast.25), channel_id=1, source_target_pairs={{2,4},{4,2},{6,8},{8,6},{10,12},{12,10},{14,16},{16,14},{18,20},{2... | collective-permute-start | bytes 184328 | tf_op jit(solution)/shard_map/ppermute | solution.py:264
  3.7 1.3 %collective-permute-start = (bf16[6,16,320]{2,1,0:T(8,128)(2,1)}, bf16[6,16,320]{2,1,0:T(8,128)(2,1)S(1)}, u32[]{:S(2)}, u32[]{:S(2)}) collective-permute-start(bf16[6,16,320]{2,1,0:T(8,128)(2,1)} %bitcast.27), channel_id=1, source_target_pairs={{0,2},{2,0},{1,3},{3,1},{4,6},{6,4},{5,7},{7,5},{8,10},{10,8},{9,1... | collective-permute-start | bytes 184328 | tf_op jit(solution)/shard_map/ppermute | solution.py:266
  5.0 0.7 %collective-permute-start.1 = (s32[1,1,2,2]{3,2,1,0:T(2,128)}, s32[1,1,2,2]{3,2,1,0:T(2,128)S(1)}, u32[]{:S(2)}, u32[]{:S(2)}) collective-permute-start(s32[1,1,2,2]{3,2,1,0:T(2,128)} %refs_2_.1), channel_id=1, source_target_pairs={{0,1},{1,0},{2,3},{3,2},{4,5},{5,4},{6,7},{7,6},{8,9},{9,8},{10,11... | collective-permute-start | bytes 56 | tf_op jit(solution)/shard_map/ppermute | solution.py:285
  5.7 1.0 %start.1 = (bf16[6,16,320]{2,1,0:T(8,128)(2,1)S(1)}, s32[3,1,6]{2,1,0:T(1,128)S(4)}, s32[1,1,2,2]{3,2,1,0:T(2,128)S(4)}, s32[1,1,2,2]{3,2,1,0:T(2,128)S(4)}, f32...) custom-call(bf16[6,16,320]{2,1,0:T(8,128)(2,1)} %bitcast.28, s32[3,1,6]{2,1,0:T(1,128)} %bitcast.29, ...), custom_call_target="tpu_custom_call" | custom-call | flops 2000000000 | bytes 1000000 | tf_op jit(solution)/shard_map/start/pallas_call | solution.py:286
  6.7 0.7 %inner.4.refs_4_ = f32[6,16,320]{2,1,0:T(8,128)S(1)} custom-call(s32[3,1,6]{2,1,0:T(1,128)S(4)} %get-tuple-element.28.offsets_ref.refs_8_, bf16[6,16,320]{2,1,0:T(8,128)(2,1)S(1)} %get-tuple-element.29.v_ref.refs_0_.refs_8_, bf16[6,3,320,320]{3,2,1,0:T(8,128)(2,1)S(1)} %bitcast.9), custom_call_target="tpu_custom_call" | custom-call | flops 58982400 | bytes 3686400 | tf_op jit(solution)/shard_map/inner/pallas_call | solution.py:297
  7.6 1.2 %collective-permute-done.1.refs_6_ = s32[1,1,2,2]{3,2,1,0:T(2,128)S(1)} collective-permute-done((s32[1,1,2,2]{3,2,1,0:T(2,128)}, s32[1,1,2,2]{3,2,1,0:T(2,128)S(1)}, u32[]{:S(2)}, u32[]{:S(2)}) %collective-permute-start.1) | collective-permute-done | bytes 48 | tf_op jit(solution)/shard_map/ppermute | solution.py:285
  9.0 1.1 %collective-permute-start.6 = (bf16[2,16,320]{2,1,0:T(8,128)(2,1)S(1)}, bf16[2,16,320]{2,1,0:T(8,128)(2,1)S(1)}, u32[]{:S(2)}, u32[]{:S(2)}) collective-permute-start(bf16[2,16,320]{2,1,0:T(8,128)(2,1)S(1)} %get-tuple-element.33), channel_id=1, source_target_pairs={{2,4},{4,2},{6,8},{8,6},{10,12},{12,10},{14,16},{16,14},{18,20},{2... | collective-permute-start | bytes 61448 | tf_op jit(solution)/shard_map/ppermute | solution.py:264
  10.2 1.0 %collective-permute-start.5 = (bf16[2,16,320]{2,1,0:T(8,128)(2,1)S(1)}, bf16[2,16,320]{2,1,0:T(8,128)(2,1)S(1)}, u32[]{:S(2)}, u32[]{:S(2)}) collective-permute-start(bf16[2,16,320]{2,1,0:T(8,128)(2,1)S(1)} %get-tuple-element.32), channel_id=1, source_target_pairs={{0,1},{1,0},{2,3},{3,2},{4,5},{5,4},{6,7},{7,6},{8,9},{9,8},{10,11... | collective-permute-start | bytes 61448 | tf_op jit(solution)/shard_map/ppermute | solution.py:265
  11.1 0.7 %inner.5.refs_4_ = f32[6,16,320]{2,1,0:T(8,128)S(1)} custom-call(s32[3,1,6]{2,1,0:T(1,128)S(4)} %get-tuple-element.28.offsets_ref.refs_8_, bf16[6,16,320]{2,1,0:T(8,128)(2,1)S(1)} %get-tuple-element.30.v_ref.refs_1_.refs_9_, bf16[6,3,320,320]{3,2,1,0:T(8,128)(2,1)S(1)} %bitcast.12), custom_call_target="tpu_custom_call" | custom-call | flops 58982400 | bytes 3686400 | tf_op jit(solution)/shard_map/inner/pallas_call | solution.py:297
  11.9 0.4 %collective-permute-done.4.halo_ref = bf16[16,320]{1,0:T(8,128)(2,1)S(1)} collective-permute-done((bf16[16,320]{1,0:T(8,128)(2,1)S(1)}, bf16[16,320]{1,0:T(8,128)(2,1)S(1)}, u32[]{:S(2)}, u32[]{:S(2)}) %collective-permute-start.4) | collective-permute-done | bytes 10272 | tf_op jit(solution)/shard_map/ppermute | solution.py:266
  12.5 0.4 %collective-permute-done.6.halo_ref = bf16[2,16,320]{2,1,0:T(8,128)(2,1)S(1)} collective-permute-done((bf16[2,16,320]{2,1,0:T(8,128)(2,1)S(1)}, bf16[2,16,320]{2,1,0:T(8,128)(2,1)S(1)}, u32[]{:S(2)}, u32[]{:S(2)}) %collective-permute-start.6) | collective-permute-done | bytes 20512 | tf_op jit(solution)/shard_map/ppermute | solution.py:264
  13.1 0.9 %collective-permute-done.5.refs_7_ = bf16[2,16,320]{2,1,0:T(8,128)(2,1)S(1)} collective-permute-done((bf16[2,16,320]{2,1,0:T(8,128)(2,1)S(1)}, bf16[2,16,320]{2,1,0:T(8,128)(2,1)S(1)}, u32[]{:S(2)}, u32[]{:S(2)}) %collective-permute-start.5) | collective-permute-done | bytes 20512 | tf_op jit(solution)/shard_map/ppermute | solution.py:265
  14.1 1.0 %collective-permute-start.9 = (bf16[2,16,320]{2,1,0:T(8,128)(2,1)S(1)}, bf16[2,16,320]{2,1,0:T(8,128)(2,1)S(1)}, u32[]{:S(2)}, u32[]{:S(2)}) collective-permute-start(bf16[2,16,320]{2,1,0:T(8,128)(2,1)S(1)} %get-tuple-element.37), channel_id=1, source_target_pairs={{2,4},{4,2},{6,8},{8,6},{10,12},{12,10},{14,16},{16,14},{18,20},{2... | collective-permute-start | bytes 61448 | tf_op jit(solution)/shard_map/ppermute | solution.py:264
  15.1 1.1 %collective-permute-start.8 = (bf16[2,16,320]{2,1,0:T(8,128)(2,1)S(1)}, bf16[2,16,320]{2,1,0:T(8,128)(2,1)S(1)}, u32[]{:S(2)}, u32[]{:S(2)}) collective-permute-start(bf16[2,16,320]{2,1,0:T(8,128)(2,1)S(1)} %get-tuple-element.36), channel_id=1, source_target_pairs={{0,1},{1,0},{2,3},{3,2},{4,5},{5,4},{6,7},{7,6},{8,9},{9,8},{10,11... | collective-permute-start | bytes 61448 | tf_op jit(solution)/shard_map/ppermute | solution.py:265
  16.2 0.7 %inner.6.refs_4_ = f32[6,16,320]{2,1,0:T(8,128)S(1)} custom-call(s32[3,1,6]{2,1,0:T(1,128)S(4)} %get-tuple-element.28.offsets_ref.refs_8_, bf16[6,16,320]{2,1,0:T(8,128)(2,1)S(1)} %get-tuple-element.34.v_ref.refs_2_.refs_10_, bf16[6,3,320,320]{3,2,1,0:T(8,128)(2,1)S(1)} %bitcast.15), custom_call_target="tpu_custom_call" | custom-call | flops 58982400 | bytes 3686400 | tf_op jit(solution)/shard_map/inner/pallas_call | solution.py:297
  16.9 0.4 %collective-permute-done.7.halo_ref = bf16[16,320]{1,0:T(8,128)(2,1)S(1)} collective-permute-done((bf16[16,320]{1,0:T(8,128)(2,1)S(1)}, bf16[16,320]{1,0:T(8,128)(2,1)S(1)}, u32[]{:S(2)}, u32[]{:S(2)}) %collective-permute-start.7) | collective-permute-done | bytes 10272 | tf_op jit(solution)/shard_map/ppermute | solution.py:266
  17.6 0.4 %collective-permute-done.9.halo_ref = bf16[2,16,320]{2,1,0:T(8,128)(2,1)S(1)} collective-permute-done((bf16[2,16,320]{2,1,0:T(8,128)(2,1)S(1)}, bf16[2,16,320]{2,1,0:T(8,128)(2,1)S(1)}, u32[]{:S(2)}, u32[]{:S(2)}) %collective-permute-start.9) | collective-permute-done | bytes 20512 | tf_op jit(solution)/shard_map/ppermute | solution.py:264
  18.2 0.8 %collective-permute-done.8.refs_7_ = bf16[2,16,320]{2,1,0:T(8,128)(2,1)S(1)} collective-permute-done((bf16[2,16,320]{2,1,0:T(8,128)(2,1)S(1)}, bf16[2,16,320]{2,1,0:T(8,128)(2,1)S(1)}, u32[]{:S(2)}, u32[]{:S(2)}) %collective-permute-start.8) | collective-permute-done | bytes 20512 | tf_op jit(solution)/shard_map/ppermute | solution.py:265
  19.0 1.1 %collective-permute-start.12 = (bf16[2,16,320]{2,1,0:T(8,128)(2,1)S(1)}, bf16[2,16,320]{2,1,0:T(8,128)(2,1)S(1)}, u32[]{:S(2)}, u32[]{:S(2)}) collective-permute-start(bf16[2,16,320]{2,1,0:T(8,128)(2,1)S(1)} %get-tuple-element.41), channel_id=1, source_target_pairs={{2,4},{4,2},{6,8},{8,6},{10,12},{12,10},{14,16},{16,14},{18,20},{2... | collective-permute-start | bytes 61448 | tf_op jit(solution)/shard_map/ppermute | solution.py:264
  20.2 1.0 %collective-permute-start.11 = (bf16[2,16,320]{2,1,0:T(8,128)(2,1)S(1)}, bf16[2,16,320]{2,1,0:T(8,128)(2,1)S(1)}, u32[]{:S(2)}, u32[]{:S(2)}) collective-permute-start(bf16[2,16,320]{2,1,0:T(8,128)(2,1)S(1)} %get-tuple-element.40), channel_id=1, source_target_pairs={{0,1},{1,0},{2,3},{3,2},{4,5},{5,4},{6,7},{7,6},{8,9},{9,8},{10,11... | collective-permute-start | bytes 61448 | tf_op jit(solution)/shard_map/ppermute | solution.py:265
  21.4 0.7 %inner.7.refs_4_ = f32[6,16,320]{2,1,0:T(8,128)S(1)} custom-call(s32[3,1,6]{2,1,0:T(1,128)S(4)} %get-tuple-element.28.offsets_ref.refs_8_, bf16[6,16,320]{2,1,0:T(8,128)(2,1)S(1)} %get-tuple-element.38.v_ref.refs_3_.refs_11_, bf16[6,3,320,320]{3,2,1,0:T(8,128)(2,1)S(1)} %bitcast.18), custom_call_target="tpu_custom_call" | custom-call | flops 58982400 | bytes 3686400 | tf_op jit(solution)/shard_map/inner/pallas_call | solution.py:297
  23.1 0.9 %collective-permute-done.11.refs_6_ = bf16[2,16,320]{2,1,0:T(8,128)(2,1)S(1)} collective-permute-done((bf16[2,16,320]{2,1,0:T(8,128)(2,1)S(1)}, bf16[2,16,320]{2,1,0:T(8,128)(2,1)S(1)}, u32[]{:S(2)}, u32[]{:S(2)}) %collective-permute-start.11) | collective-permute-done | bytes 20512 | tf_op jit(solution)/shard_map/ppermute | solution.py:265
  24.3 1.2 %collective-permute-done.13 = f32[2,16,128]{2,1,0:T(8,128)S(1)} collective-permute-done((f32[2,16,128]{2,1,0:T(8,128)S(1)}, f32[2,16,128]{2,1,0:T(8,128)S(1)}, u32[]{:S(2)}, u32[]{:S(2)}) %collective-permute-start.13) | collective-permute-done | bytes 16416 | tf_op jit(solution)/shard_map/ppermute | solution.py:327
  25.9 0.9 %collective-permute-start.15 = (f32[2,16,128]{2,1,0:T(8,128)S(1)}, f32[2,16,128]{2,1,0:T(8,128)S(1)}, u32[]{:S(2)}, u32[]{:S(2)}) collective-permute-start(f32[2,16,128]{2,1,0:T(8,128)S(1)} %add.21), channel_id=1, source_target_pairs={{0,3},{1,2},{2,1},{3,0},{4,7},{5,6},{6,5},{7,4},{8,11},{9,10},{10,... | collective-permute-start | bytes 49160 | tf_op jit(solution)/shard_map/ppermute | solution.py:329
  26.7 1.7 %collective-permute-start.14 = (f32[2,16,128]{2,1,0:T(8,128)S(1)}, f32[2,16,128]{2,1,0:T(8,128)S(1)}, u32[]{:S(2)}, u32[]{:S(2)}) collective-permute-start(f32[2,16,128]{2,1,0:T(8,128)S(1)} %add.21), channel_id=1, source_target_pairs={{0,6},{1,7},{2,4},{3,5},{4,2},{5,3},{6,0},{7,1},{8,14},{9,15},{10,... | collective-permute-start | bytes 49160 | tf_op jit(solution)/shard_map/ppermute | solution.py:329
  28.5 1.1 %collective-permute-done.16 = f32[2,16,128]{2,1,0:T(8,128)S(1)} collective-permute-done((f32[2,16,128]{2,1,0:T(8,128)S(1)}, f32[2,16,128]{2,1,0:T(8,128)S(1)}, u32[]{:S(2)}, u32[]{:S(2)}) %collective-permute-start.16) | collective-permute-done | bytes 16416 | tf_op jit(solution)/shard_map/ppermute | solution.py:329
  29.6 0.5 %collective-permute-done.14 = f32[2,16,128]{2,1,0:T(8,128)S(1)} collective-permute-done((f32[2,16,128]{2,1,0:T(8,128)S(1)}, f32[2,16,128]{2,1,0:T(8,128)S(1)}, u32[]{:S(2)}, u32[]{:S(2)}) %collective-permute-start.14) | collective-permute-done | bytes 16416 | tf_op jit(solution)/shard_map/ppermute | solution.py:329
  30.1 2.3 %collective-permute-start.19 = (f32[2,16,128]{2,1,0:T(8,128)S(1)}, f32[2,16,128]{2,1,0:T(8,128)S(1)}, u32[]{:S(2)}, u32[]{:S(2)}) collective-permute-start(f32[2,16,128]{2,1,0:T(8,128)S(1)} %add_add_fusion.1), channel_id=1, source_target_pairs={{0,26},{1,27},{2,24},{3,25},{4,30},{5,31},{6,28},{7,29},{8,18},{9,... | collective-permute-start | bytes 49160 | tf_op jit(solution)/shard_map/ppermute | solution.py:329
  32.7 1.3 %collective-permute-start.17 = (f32[2,16,128]{2,1,0:T(8,128)S(1)}, f32[2,16,128]{2,1,0:T(8,128)S(1)}, u32[]{:S(2)}, u32[]{:S(2)}) collective-permute-start(f32[2,16,128]{2,1,0:T(8,128)S(1)} %add_add_fusion.1), channel_id=1, source_target_pairs={{0,10},{1,11},{2,8},{3,9},{4,14},{5,15},{6,12},{7,13},{8,2},{9,3},... | collective-permute-start | bytes 49160 | tf_op jit(solution)/shard_map/ppermute | solution.py:329
  34.0 0.7 %copy.9 = bf16[1,6,4,16,320]{4,3,2,1,0:T(8,128)(2,1)} copy(bf16[1,6,4,16,320]{4,3,1,2,0:T(8,128)(2,1)S(1)} %maximum_bitcast_fusion) | data formatting | bytes 491520
  35.1 1.6 %collective-permute-done.18 = f32[2,16,128]{2,1,0:T(8,128)S(1)} collective-permute-done((f32[2,16,128]{2,1,0:T(8,128)S(1)}, f32[2,16,128]{2,1,0:T(8,128)S(1)}, u32[]{:S(2)}, u32[]{:S(2)}) %collective-permute-start.18) | collective-permute-done | bytes 16416 | tf_op jit(solution)/shard_map/ppermute | solution.py:329
  36.7 2.6 %factor.1 = f32[80,80]{1,0:T(8,128)} custom-call(f32[2,16,128]{2,1,0:T(8,128)S(1)} %add_add_fusion.gram_ref), custom_call_target="tpu_custom_call" | custom-call | tf_op jit(solution)/shard_map/factor/pallas_call | solution.py:334
  (33 shorter events, 4.0 us)
Async XLA Ops:
  0.6 6.0 %copy-start = (bf16[1,6,3,320,320]{4,3,2,1,0:T(8,128)(2,1)S(1)}, bf16[1,6,3,320,320]{4,3,2,1,0:T(8,128)(2,1)}, u32[]{:S(2)}) copy-start(bf16[1,6,3,320,320]{4,3,2,1,0:T(8,128)(2,1)} %param.8) | copy-start | bytes 11059204
  0.6 8.1 %collective-permute-start.3 = (bf16[6,16,320]{2,1,0:T(8,128)(2,1)}, bf16[6,16,320]{2,1,0:T(8,128)(2,1)S(1)}, u32[]{:S(2)}, u32[]{:S(2)}) collective-permute-start(bf16[6,16,320]{2,1,0:T(8,128)(2,1)} %bitcast.25), channel_id=1, source_target_pairs={{2,4},{4,2},{6,8},{8,6},{10,12},{12,10},{14,16},{16,14},{18,20},{2... | collective-permute-start | bytes 184328 | tf_op jit(solution)/shard_map/ppermute | solution.py:264
  3.6 5.1 %collective-permute-start.2 = (bf16[6,16,320]{2,1,0:T(8,128)(2,1)}, bf16[6,16,320]{2,1,0:T(8,128)(2,1)S(1)}, u32[]{:S(2)}, u32[]{:S(2)}) collective-permute-start(bf16[6,16,320]{2,1,0:T(8,128)(2,1)} %bitcast.26), channel_id=1, source_target_pairs={{0,1},{1,0},{2,3},{3,2},{4,5},{5,4},{6,7},{7,6},{8,9},{9,8},{10,11... | collective-permute-start | bytes 184328 | tf_op jit(solution)/shard_map/ppermute | solution.py:265
  3.7 3.7 %collective-permute-start = (bf16[6,16,320]{2,1,0:T(8,128)(2,1)}, bf16[6,16,320]{2,1,0:T(8,128)(2,1)S(1)}, u32[]{:S(2)}, u32[]{:S(2)}) collective-permute-start(bf16[6,16,320]{2,1,0:T(8,128)(2,1)} %bitcast.27), channel_id=1, source_target_pairs={{0,2},{2,0},{1,3},{3,1},{4,6},{6,4},{5,7},{7,5},{8,10},{10,8},{9,1... | collective-permute-start | bytes 184328 | tf_op jit(solution)/shard_map/ppermute | solution.py:266
  5.0 3.8 %collective-permute-start.1 = (s32[1,1,2,2]{3,2,1,0:T(2,128)}, s32[1,1,2,2]{3,2,1,0:T(2,128)S(1)}, u32[]{:S(2)}, u32[]{:S(2)}) collective-permute-start(s32[1,1,2,2]{3,2,1,0:T(2,128)} %refs_2_.1), channel_id=1, source_target_pairs={{0,1},{1,0},{2,3},{3,2},{4,5},{5,4},{6,7},{7,6},{8,9},{9,8},{10,11... | collective-permute-start | bytes 56 | tf_op jit(solution)/shard_map/ppermute | solution.py:285
  9.0 3.9 %collective-permute-start.6 = (bf16[2,16,320]{2,1,0:T(8,128)(2,1)S(1)}, bf16[2,16,320]{2,1,0:T(8,128)(2,1)S(1)}, u32[]{:S(2)}, u32[]{:S(2)}) collective-permute-start(bf16[2,16,320]{2,1,0:T(8,128)(2,1)S(1)} %get-tuple-element.33), channel_id=1, source_target_pairs={{2,4},{4,2},{6,8},{8,6},{10,12},{12,10},{14,16},{16,14},{18,20},{2... | collective-permute-start | bytes 61448 | tf_op jit(solution)/shard_map/ppermute | solution.py:264
  10.2 3.8 %collective-permute-start.5 = (bf16[2,16,320]{2,1,0:T(8,128)(2,1)S(1)}, bf16[2,16,320]{2,1,0:T(8,128)(2,1)S(1)}, u32[]{:S(2)}, u32[]{:S(2)}) collective-permute-start(bf16[2,16,320]{2,1,0:T(8,128)(2,1)S(1)} %get-tuple-element.32), channel_id=1, source_target_pairs={{0,1},{1,0},{2,3},{3,2},{4,5},{5,4},{6,7},{7,6},{8,9},{9,8},{10,11... | collective-permute-start | bytes 61448 | tf_op jit(solution)/shard_map/ppermute | solution.py:265
  11.1 1.2 %collective-permute-start.4 = (bf16[16,320]{1,0:T(8,128)(2,1)S(1)}, bf16[16,320]{1,0:T(8,128)(2,1)S(1)}, u32[]{:S(2)}, u32[]{:S(2)}) collective-permute-start(bf16[16,320]{1,0:T(8,128)(2,1)S(1)} %get-tuple-element.31), channel_id=1, source_target_pairs={{0,2},{2,0},{1,3},{3,1},{4,6},{6,4},{5,7},{7,5},{8,10},{10,8},{9,1... | collective-permute-start | bytes 30728 | tf_op jit(solution)/shard_map/ppermute | solution.py:266
  14.1 3.9 %collective-permute-start.9 = (bf16[2,16,320]{2,1,0:T(8,128)(2,1)S(1)}, bf16[2,16,320]{2,1,0:T(8,128)(2,1)S(1)}, u32[]{:S(2)}, u32[]{:S(2)}) collective-permute-start(bf16[2,16,320]{2,1,0:T(8,128)(2,1)S(1)} %get-tuple-element.37), channel_id=1, source_target_pairs={{2,4},{4,2},{6,8},{8,6},{10,12},{12,10},{14,16},{16,14},{18,20},{2... | collective-permute-start | bytes 61448 | tf_op jit(solution)/shard_map/ppermute | solution.py:264
  15.1 3.8 %collective-permute-start.8 = (bf16[2,16,320]{2,1,0:T(8,128)(2,1)S(1)}, bf16[2,16,320]{2,1,0:T(8,128)(2,1)S(1)}, u32[]{:S(2)}, u32[]{:S(2)}) collective-permute-start(bf16[2,16,320]{2,1,0:T(8,128)(2,1)S(1)} %get-tuple-element.36), channel_id=1, source_target_pairs={{0,1},{1,0},{2,3},{3,2},{4,5},{5,4},{6,7},{7,6},{8,9},{9,8},{10,11... | collective-permute-start | bytes 61448 | tf_op jit(solution)/shard_map/ppermute | solution.py:265
  16.2 1.2 %collective-permute-start.7 = (bf16[16,320]{1,0:T(8,128)(2,1)S(1)}, bf16[16,320]{1,0:T(8,128)(2,1)S(1)}, u32[]{:S(2)}, u32[]{:S(2)}) collective-permute-start(bf16[16,320]{1,0:T(8,128)(2,1)S(1)} %get-tuple-element.35), channel_id=1, source_target_pairs={{0,2},{2,0},{1,3},{3,1},{4,6},{6,4},{5,7},{7,5},{8,10},{10,8},{9,1... | collective-permute-start | bytes 30728 | tf_op jit(solution)/shard_map/ppermute | solution.py:266
  19.0 3.9 %collective-permute-start.12 = (bf16[2,16,320]{2,1,0:T(8,128)(2,1)S(1)}, bf16[2,16,320]{2,1,0:T(8,128)(2,1)S(1)}, u32[]{:S(2)}, u32[]{:S(2)}) collective-permute-start(bf16[2,16,320]{2,1,0:T(8,128)(2,1)S(1)} %get-tuple-element.41), channel_id=1, source_target_pairs={{2,4},{4,2},{6,8},{8,6},{10,12},{12,10},{14,16},{16,14},{18,20},{2... | collective-permute-start | bytes 61448 | tf_op jit(solution)/shard_map/ppermute | solution.py:264
  20.2 3.8 %collective-permute-start.11 = (bf16[2,16,320]{2,1,0:T(8,128)(2,1)S(1)}, bf16[2,16,320]{2,1,0:T(8,128)(2,1)S(1)}, u32[]{:S(2)}, u32[]{:S(2)}) collective-permute-start(bf16[2,16,320]{2,1,0:T(8,128)(2,1)S(1)} %get-tuple-element.40), channel_id=1, source_target_pairs={{0,1},{1,0},{2,3},{3,2},{4,5},{5,4},{6,7},{7,6},{8,9},{9,8},{10,11... | collective-permute-start | bytes 61448 | tf_op jit(solution)/shard_map/ppermute | solution.py:265
  21.1 1.2 %collective-permute-start.10 = (bf16[16,320]{1,0:T(8,128)(2,1)S(1)}, bf16[16,320]{1,0:T(8,128)(2,1)S(1)}, u32[]{:S(2)}, u32[]{:S(2)}) collective-permute-start(bf16[16,320]{1,0:T(8,128)(2,1)S(1)} %get-tuple-element.39), channel_id=1, source_target_pairs={{0,2},{2,0},{1,3},{3,1},{4,6},{6,4},{5,7},{7,5},{8,10},{10,8},{9,1... | collective-permute-start | bytes 30728 | tf_op jit(solution)/shard_map/ppermute | solution.py:266
  24.2 1.2 %collective-permute-start.13 = (f32[2,16,128]{2,1,0:T(8,128)S(1)}, f32[2,16,128]{2,1,0:T(8,128)S(1)}, u32[]{:S(2)}, u32[]{:S(2)}) collective-permute-start(f32[2,16,128]{2,1,0:T(8,128)S(1)} %get-tuple-element.45), channel_id=1, source_target_pairs={{0,2},{2,0},{1,3},{3,1},{4,6},{6,4},{5,7},{7,5},{8,10},{10,8},{9,1... | collective-permute-start | bytes 49160 | tf_op jit(solution)/shard_map/ppermute | solution.py:327
  25.5 4.1 %collective-permute-start.16 = (f32[2,16,128]{2,1,0:T(8,128)S(1)}, f32[2,16,128]{2,1,0:T(8,128)S(1)}, u32[]{:S(2)}, u32[]{:S(2)}) collective-permute-start(f32[2,16,128]{2,1,0:T(8,128)S(1)} %add.21), channel_id=1, source_target_pairs={{0,7},{1,6},{2,5},{3,4},{4,3},{5,2},{6,1},{7,0},{8,15},{9,14},{10,... | collective-permute-start | bytes 49160 | tf_op jit(solution)/shard_map/ppermute | solution.py:329
  25.9 3.7 %collective-permute-start.15 = (f32[2,16,128]{2,1,0:T(8,128)S(1)}, f32[2,16,128]{2,1,0:T(8,128)S(1)}, u32[]{:S(2)}, u32[]{:S(2)}) collective-permute-start(f32[2,16,128]{2,1,0:T(8,128)S(1)} %add.21), channel_id=1, source_target_pairs={{0,3},{1,2},{2,1},{3,0},{4,7},{5,6},{6,5},{7,4},{8,11},{9,10},{10,... | collective-permute-start | bytes 49160 | tf_op jit(solution)/shard_map/ppermute | solution.py:329
  26.7 3.3 %collective-permute-start.14 = (f32[2,16,128]{2,1,0:T(8,128)S(1)}, f32[2,16,128]{2,1,0:T(8,128)S(1)}, u32[]{:S(2)}, u32[]{:S(2)}) collective-permute-start(f32[2,16,128]{2,1,0:T(8,128)S(1)} %add.21), channel_id=1, source_target_pairs={{0,6},{1,7},{2,4},{3,5},{4,2},{5,3},{6,0},{7,1},{8,14},{9,15},{10,... | collective-permute-start | bytes 49160 | tf_op jit(solution)/shard_map/ppermute | solution.py:329
  30.1 5.0 %collective-permute-start.19 = (f32[2,16,128]{2,1,0:T(8,128)S(1)}, f32[2,16,128]{2,1,0:T(8,128)S(1)}, u32[]{:S(2)}, u32[]{:S(2)}) collective-permute-start(f32[2,16,128]{2,1,0:T(8,128)S(1)} %add_add_fusion.1), channel_id=1, source_target_pairs={{0,26},{1,27},{2,24},{3,25},{4,30},{5,31},{6,28},{7,29},{8,18},{9,... | collective-permute-start | bytes 49160 | tf_op jit(solution)/shard_map/ppermute | solution.py:329
  32.4 4.2 %collective-permute-start.18 = (f32[2,16,128]{2,1,0:T(8,128)S(1)}, f32[2,16,128]{2,1,0:T(8,128)S(1)}, u32[]{:S(2)}, u32[]{:S(2)}) collective-permute-start(f32[2,16,128]{2,1,0:T(8,128)S(1)} %add_add_fusion.1), channel_id=1, source_target_pairs={{0,18},{1,19},{2,16},{3,17},{4,22},{5,23},{6,20},{7,21},{8,26},{9,... | collective-permute-start | bytes 49160 | tf_op jit(solution)/shard_map/ppermute | solution.py:329
  32.7 4.0 %collective-permute-start.17 = (f32[2,16,128]{2,1,0:T(8,128)S(1)}, f32[2,16,128]{2,1,0:T(8,128)S(1)}, u32[]{:S(2)}, u32[]{:S(2)}) collective-permute-start(f32[2,16,128]{2,1,0:T(8,128)S(1)} %add_add_fusion.1), channel_id=1, source_target_pairs={{0,10},{1,11},{2,8},{3,9},{4,14},{5,15},{6,12},{7,13},{8,2},{9,3},... | collective-permute-start | bytes 49160 | tf_op jit(solution)/shard_map/ppermute | solution.py:329

commit v7 on v6

--- a/solution.py
+++ b/solution.py
@@ -42,16 +42,20 @@
         acc_ref[e] = total
 
 
-def edge_product(in_chip, offsets_ref, halo_ref, blocks_ref):
-    count, kinds = blocks_ref.shape[:2]
+def edge_place(in_chip, count, halo_ref):
     last = count - 1
     chip, core = lax.axis_index("chip"), lax.axis_index("core")
     upper = core == 0 if in_chip else core == 1
     edge = jnp.where(upper, last, 0)
     there = True if in_chip else jnp.where(core == 0, chip > 0, chip < lax.axis_size("chip") - 1)
-    halo = halo_ref[...]
-    if len(halo_ref.shape) == 3:
-        halo = halo_ref[last - edge] if halo_ref.shape[0] == count else halo_ref[0]
+    if len(halo_ref.shape) == 2:
+        return upper, edge, there, halo_ref[...]
+    return upper, edge, there, halo_ref[last - edge] if halo_ref.shape[0] == count else halo_ref[0]
+
+
+def edge_product(in_chip, offsets_ref, halo_ref, blocks_ref):
+    count, kinds = blocks_ref.shape[:2]
+    upper, edge, there, halo = edge_place(in_chip, count, halo_ref)
     total = None
     for k in range(kinds):
         used = jnp.logical_and(offsets_ref[k, 0, edge] == jnp.where(upper, H, -H), there)
@@ -62,7 +66,22 @@
 
 
 def edge_kernel(in_chip, offsets_ref, halo_ref, blocks_ref, out_ref):
-    out_ref[...] = edge_product(in_chip, offsets_ref, halo_ref, blocks_ref)
+    count, kinds = blocks_ref.shape[:2]
+    upper, edge, there, halo = edge_place(in_chip, count, halo_ref)
+    hits = [jnp.logical_and(offsets_ref[k, 0, edge] == jnp.where(upper, H, -H), there) for k in range(kinds)]
+    number = sum(hit.astype(jnp.int32) for hit in hits)
+    first = jnp.int32(kinds - 1)
+    for k in range(kinds - 2, -1, -1):
+        first = jnp.where(hits[k], k, first)
+
+    @pl.when(number <= 1)
+    def _():
+        lhs = jnp.where(number > 0, halo, jnp.zeros_like(halo))
+        out_ref[...] = jnp.dot(lhs, blocks_ref[edge, first], preferred_element_type=jnp.float32)
+
+    @pl.when(number > 1)
+    def _():
+        out_ref[...] = edge_product(in_chip, offsets_ref, halo_ref, blocks_ref)
 
 
 def next_field(grids, first, donor_ref, fringe_ref, weight_ref, live_ref, acc_ref, chip_ref, side, others):
@@ -89,8 +108,10 @@
     asked, rest = take(rest, grids - 1)
     others, rest = take(rest, grids - 1)
     side, rest = take(rest, 3 if first else 1)
-    v_ref, side_ref, chip_ref, *sends = rest
-    side = edge_product(False, *side) if first else side[0][...]
+    v_ref, side_ref, chip_ref, *sends, edge_ref = rest if first else (*rest, None)
+    if first:
+        edge_kernel(False, *side, edge_ref)
+    side = edge_ref[...] if first else side[0][...]
     totals = next_field(grids, first, *shared, side, others)
     count = len(totals)
     fields = [t.astype(jnp.bfloat16) for t in totals]
@@ -310,6 +331,7 @@
                 out_shape=(field_type, side_type, halo_type, *[donor_type] * (grids - 1)),
                 in_specs=[SMEM] * 4 + [VMEM] * (2 + 2 * (grids - 1)) + ([SMEM] if level == 0 else []) + [VMEM] * len(side_in[-2:]),
                 out_specs=(VMEM,) * (3 + grids - 1),
+                scratch_shapes=[pltpu.VMEM((n, unknowns), jnp.float32)] if level == 0 else [],
                 compiler_params=limit, name="outer",
             )(*shared, *asked, *others, *side_in)
             messages = exchange(*sends)

time: 39.4 us -> 39.3 us (level)
  Pallas kernels: 8.81 us -> 8.37 us
    pallas_call x7, Pallas kernels: 1.34 us -> 0.88 us  [local(): pl.pallas_call(functools.partial(edge_kernel, in_chip), out_shape=edge_ty...]
  transfers between devices with their start and end apart: 20 -> 20, of which waited for: 15 -> 15; matrix products, arithmetic and copies ran while one was open for 2% -> 2% of each run, Pallas kernels for 14% -> 13%
where the time goes in v7:
time: 39.3 us; the launch traced here: 39.1 us
  starting transfers between devices  18.3 us (47%)
  waiting for transfers between devices  10.9 us (28%)
  Pallas kernels  8.37 us (21%)
  local copies, waits for them, and re-layouts  0.75 us (2%)
  between operations  0.72 us (2%)
    ppermute x6, starting transfers between devices, local(): arrived = [lax.ppermute(gram, axes, pairs) for pairs in group]  6.93 us
    ppermute x4, starting transfers between devices, exchange(): from_side = lax.ppermute(to_side, axes, side)  6.29 us
    ppermute x6, waiting for transfers between devices, local(): arrived = [lax.ppermute(gram, axes, pairs) for pairs in group]  3.25 us
    ppermute x4, starting transfers between devices, exchange(): lax.ppermute(v, 'grid', pairs)  3.06 us
    pallas_call x4, Pallas kernels, local(): pl.pallas_call(inner_kernel, out_shape=acc_type, in_specs=[SMEM, VMEM, VM...  2.93 us
    ppermute x4, waiting for transfers between devices, exchange(): lax.ppermute(v, 'grid', pairs)  2.73 us
    pallas_call x1, Pallas kernels, local(): pl.pallas_call(functools.partial(factor_kernel, 1.0 / row_total), out_sha...  2.61 us
    ppermute x4, waiting for transfers between devices, exchange(): from_side = lax.ppermute(to_side, axes, side)  1.5 us
  transfers between devices with their start and end apart: 20, of which 15 were waited for; matrix products, arithmetic and copies ran while one was open for 2% of the time, Pallas kernels for 13%

profile of v7, /device:TPU:0, one launch (start us, length us, event | category | flops | bytes accessed | tf_op | source)
XLA Modules:
  0.0 39.1 jit_solution(1796048689677645654)
XLA Ops:
  0.6 3.0 %collective-permute-start.3 = (bf16[6,16,320]{2,1,0:T(8,128)(2,1)}, bf16[6,16,320]{2,1,0:T(8,128)(2,1)S(1)}, u32[]{:S(2)}, u32[]{:S(2)}) collective-permute-start(bf16[6,16,320]{2,1,0:T(8,128)(2,1)} %bitcast.25), channel_id=1, source_target_pairs={{2,4},{4,2},{6,8},{8,6},{10,12},{12,10},{14,16},{16,14},{18,20},{2... | collective-permute-start | bytes 184328 | tf_op jit(solution)/shard_map/ppermute | solution.py:285
  3.7 1.3 %collective-permute-start = (bf16[6,16,320]{2,1,0:T(8,128)(2,1)}, bf16[6,16,320]{2,1,0:T(8,128)(2,1)S(1)}, u32[]{:S(2)}, u32[]{:S(2)}) collective-permute-start(bf16[6,16,320]{2,1,0:T(8,128)(2,1)} %bitcast.27), channel_id=1, source_target_pairs={{0,2},{2,0},{1,3},{3,1},{4,6},{6,4},{5,7},{7,5},{8,10},{10,8},{9,1... | collective-permute-start | bytes 184328 | tf_op jit(solution)/shard_map/ppermute | solution.py:287
  5.0 0.7 %collective-permute-start.1 = (s32[1,1,2,2]{3,2,1,0:T(2,128)}, s32[1,1,2,2]{3,2,1,0:T(2,128)S(1)}, u32[]{:S(2)}, u32[]{:S(2)}) collective-permute-start(s32[1,1,2,2]{3,2,1,0:T(2,128)} %refs_2_.1), channel_id=1, source_target_pairs={{0,1},{1,0},{2,3},{3,2},{4,5},{5,4},{6,7},{7,6},{8,9},{9,8},{10,11... | collective-permute-start | bytes 56 | tf_op jit(solution)/shard_map/ppermute | solution.py:306
  5.7 1.0 %start.1 = (bf16[6,16,320]{2,1,0:T(8,128)(2,1)S(1)}, s32[3,1,6]{2,1,0:T(1,128)S(4)}, s32[1,1,2,2]{3,2,1,0:T(2,128)S(4)}, s32[1,1,2,2]{3,2,1,0:T(2,128)S(4)}, f32...) custom-call(bf16[6,16,320]{2,1,0:T(8,128)(2,1)} %bitcast.28, s32[3,1,6]{2,1,0:T(1,128)} %bitcast.29, ...), custom_call_target="tpu_custom_call" | custom-call | flops 2000000000 | bytes 1000000 | tf_op jit(solution)/shard_map/start/pallas_call | solution.py:307
  6.7 0.7 %inner.4.refs_4_ = f32[6,16,320]{2,1,0:T(8,128)S(1)} custom-call(s32[3,1,6]{2,1,0:T(1,128)S(4)} %get-tuple-element.28.offsets_ref.refs_8_, bf16[6,16,320]{2,1,0:T(8,128)(2,1)S(1)} %get-tuple-element.29.v_ref.refs_0_.refs_8_, bf16[6,3,320,320]{3,2,1,0:T(8,128)(2,1)S(1)} %bitcast.9), custom_call_target="tpu_custom_call" | custom-call | flops 58982400 | bytes 3686400 | tf_op jit(solution)/shard_map/inner/pallas_call | solution.py:318
  7.6 1.2 %collective-permute-done.1.refs_6_ = s32[1,1,2,2]{3,2,1,0:T(2,128)S(1)} collective-permute-done((s32[1,1,2,2]{3,2,1,0:T(2,128)}, s32[1,1,2,2]{3,2,1,0:T(2,128)S(1)}, u32[]{:S(2)}, u32[]{:S(2)}) %collective-permute-start.1) | collective-permute-done | bytes 48 | tf_op jit(solution)/shard_map/ppermute | solution.py:306
  9.0 1.1 %collective-permute-start.6 = (bf16[2,16,320]{2,1,0:T(8,128)(2,1)S(1)}, bf16[2,16,320]{2,1,0:T(8,128)(2,1)S(1)}, u32[]{:S(2)}, u32[]{:S(2)}) collective-permute-start(bf16[2,16,320]{2,1,0:T(8,128)(2,1)S(1)} %get-tuple-element.33), channel_id=1, source_target_pairs={{2,4},{4,2},{6,8},{8,6},{10,12},{12,10},{14,16},{16,14},{18,20},{2... | collective-permute-start | bytes 61448 | tf_op jit(solution)/shard_map/ppermute | solution.py:285
  10.2 1.0 %collective-permute-start.5 = (bf16[2,16,320]{2,1,0:T(8,128)(2,1)S(1)}, bf16[2,16,320]{2,1,0:T(8,128)(2,1)S(1)}, u32[]{:S(2)}, u32[]{:S(2)}) collective-permute-start(bf16[2,16,320]{2,1,0:T(8,128)(2,1)S(1)} %get-tuple-element.32), channel_id=1, source_target_pairs={{0,1},{1,0},{2,3},{3,2},{4,5},{5,4},{6,7},{7,6},{8,9},{9,8},{10,11... | collective-permute-start | bytes 61448 | tf_op jit(solution)/shard_map/ppermute | solution.py:286
  11.1 0.7 %inner.5.refs_4_ = f32[6,16,320]{2,1,0:T(8,128)S(1)} custom-call(s32[3,1,6]{2,1,0:T(1,128)S(4)} %get-tuple-element.28.offsets_ref.refs_8_, bf16[6,16,320]{2,1,0:T(8,128)(2,1)S(1)} %get-tuple-element.30.v_ref.refs_1_.refs_9_, bf16[6,3,320,320]{3,2,1,0:T(8,128)(2,1)S(1)} %bitcast.12), custom_call_target="tpu_custom_call" | custom-call | flops 58982400 | bytes 3686400 | tf_op jit(solution)/shard_map/inner/pallas_call | solution.py:318
  12.4 0.5 %collective-permute-done.6.halo_ref = bf16[2,16,320]{2,1,0:T(8,128)(2,1)S(1)} collective-permute-done((bf16[2,16,320]{2,1,0:T(8,128)(2,1)S(1)}, bf16[2,16,320]{2,1,0:T(8,128)(2,1)S(1)}, u32[]{:S(2)}, u32[]{:S(2)}) %collective-permute-start.6) | collective-permute-done | bytes 20512 | tf_op jit(solution)/shard_map/ppermute | solution.py:285
  13.1 0.9 %collective-permute-done.5.refs_7_ = bf16[2,16,320]{2,1,0:T(8,128)(2,1)S(1)} collective-permute-done((bf16[2,16,320]{2,1,0:T(8,128)(2,1)S(1)}, bf16[2,16,320]{2,1,0:T(8,128)(2,1)S(1)}, u32[]{:S(2)}, u32[]{:S(2)}) %collective-permute-start.5) | collective-permute-done | bytes 20512 | tf_op jit(solution)/shard_map/ppermute | solution.py:286
  14.1 1.0 %collective-permute-start.9 = (bf16[2,16,320]{2,1,0:T(8,128)(2,1)S(1)}, bf16[2,16,320]{2,1,0:T(8,128)(2,1)S(1)}, u32[]{:S(2)}, u32[]{:S(2)}) collective-permute-start(bf16[2,16,320]{2,1,0:T(8,128)(2,1)S(1)} %get-tuple-element.37), channel_id=1, source_target_pairs={{2,4},{4,2},{6,8},{8,6},{10,12},{12,10},{14,16},{16,14},{18,20},{2... | collective-permute-start | bytes 61448 | tf_op jit(solution)/shard_map/ppermute | solution.py:285
  15.1 1.1 %collective-permute-start.8 = (bf16[2,16,320]{2,1,0:T(8,128)(2,1)S(1)}, bf16[2,16,320]{2,1,0:T(8,128)(2,1)S(1)}, u32[]{:S(2)}, u32[]{:S(2)}) collective-permute-start(bf16[2,16,320]{2,1,0:T(8,128)(2,1)S(1)} %get-tuple-element.36), channel_id=1, source_target_pairs={{0,1},{1,0},{2,3},{3,2},{4,5},{5,4},{6,7},{7,6},{8,9},{9,8},{10,11... | collective-permute-start | bytes 61448 | tf_op jit(solution)/shard_map/ppermute | solution.py:286
  16.2 0.7 %inner.6.refs_4_ = f32[6,16,320]{2,1,0:T(8,128)S(1)} custom-call(s32[3,1,6]{2,1,0:T(1,128)S(4)} %get-tuple-element.28.offsets_ref.refs_8_, bf16[6,16,320]{2,1,0:T(8,128)(2,1)S(1)} %get-tuple-element.34.v_ref.refs_2_.refs_10_, bf16[6,3,320,320]{3,2,1,0:T(8,128)(2,1)S(1)} %bitcast.15), custom_call_target="tpu_custom_call" | custom-call | flops 58982400 | bytes 3686400 | tf_op jit(solution)/shard_map/inner/pallas_call | solution.py:318
  17.5 0.5 %collective-permute-done.9.halo_ref = bf16[2,16,320]{2,1,0:T(8,128)(2,1)S(1)} collective-permute-done((bf16[2,16,320]{2,1,0:T(8,128)(2,1)S(1)}, bf16[2,16,320]{2,1,0:T(8,128)(2,1)S(1)}, u32[]{:S(2)}, u32[]{:S(2)}) %collective-permute-start.9) | collective-permute-done | bytes 20512 | tf_op jit(solution)/shard_map/ppermute | solution.py:285
  18.1 0.8 %collective-permute-done.8.refs_7_ = bf16[2,16,320]{2,1,0:T(8,128)(2,1)S(1)} collective-permute-done((bf16[2,16,320]{2,1,0:T(8,128)(2,1)S(1)}, bf16[2,16,320]{2,1,0:T(8,128)(2,1)S(1)}, u32[]{:S(2)}, u32[]{:S(2)}) %collective-permute-start.8) | collective-permute-done | bytes 20512 | tf_op jit(solution)/shard_map/ppermute | solution.py:286
  19.1 1.1 %collective-permute-start.12 = (bf16[2,16,320]{2,1,0:T(8,128)(2,1)S(1)}, bf16[2,16,320]{2,1,0:T(8,128)(2,1)S(1)}, u32[]{:S(2)}, u32[]{:S(2)}) collective-permute-start(bf16[2,16,320]{2,1,0:T(8,128)(2,1)S(1)} %get-tuple-element.41), channel_id=1, source_target_pairs={{2,4},{4,2},{6,8},{8,6},{10,12},{12,10},{14,16},{16,14},{18,20},{2... | collective-permute-start | bytes 61448 | tf_op jit(solution)/shard_map/ppermute | solution.py:285
  20.2 1.0 %collective-permute-start.11 = (bf16[2,16,320]{2,1,0:T(8,128)(2,1)S(1)}, bf16[2,16,320]{2,1,0:T(8,128)(2,1)S(1)}, u32[]{:S(2)}, u32[]{:S(2)}) collective-permute-start(bf16[2,16,320]{2,1,0:T(8,128)(2,1)S(1)} %get-tuple-element.40), channel_id=1, source_target_pairs={{0,1},{1,0},{2,3},{3,2},{4,5},{5,4},{6,7},{7,6},{8,9},{9,8},{10,11... | collective-permute-start | bytes 61448 | tf_op jit(solution)/shard_map/ppermute | solution.py:286
  21.4 0.7 %inner.7.refs_4_ = f32[6,16,320]{2,1,0:T(8,128)S(1)} custom-call(s32[3,1,6]{2,1,0:T(1,128)S(4)} %get-tuple-element.28.offsets_ref.refs_8_, bf16[6,16,320]{2,1,0:T(8,128)(2,1)S(1)} %get-tuple-element.38.v_ref.refs_3_.refs_11_, bf16[6,3,320,320]{3,2,1,0:T(8,128)(2,1)S(1)} %bitcast.18), custom_call_target="tpu_custom_call" | custom-call | flops 58982400 | bytes 3686400 | tf_op jit(solution)/shard_map/inner/pallas_call | solution.py:318
  22.4 0.5 %collective-permute-done.12.halo_ref = bf16[2,16,320]{2,1,0:T(8,128)(2,1)S(1)} collective-permute-done((bf16[2,16,320]{2,1,0:T(8,128)(2,1)S(1)}, bf16[2,16,320]{2,1,0:T(8,128)(2,1)S(1)}, u32[]{:S(2)}, u32[]{:S(2)}) %collective-permute-start.12) | collective-permute-done | bytes 20512 | tf_op jit(solution)/shard_map/ppermute | solution.py:285
  23.1 0.9 %collective-permute-done.11.refs_6_ = bf16[2,16,320]{2,1,0:T(8,128)(2,1)S(1)} collective-permute-done((bf16[2,16,320]{2,1,0:T(8,128)(2,1)S(1)}, bf16[2,16,320]{2,1,0:T(8,128)(2,1)S(1)}, u32[]{:S(2)}, u32[]{:S(2)}) %collective-permute-start.11) | collective-permute-done | bytes 20512 | tf_op jit(solution)/shard_map/ppermute | solution.py:286
  24.3 1.2 %collective-permute-done.13 = f32[2,16,128]{2,1,0:T(8,128)S(1)} collective-permute-done((f32[2,16,128]{2,1,0:T(8,128)S(1)}, f32[2,16,128]{2,1,0:T(8,128)S(1)}, u32[]{:S(2)}, u32[]{:S(2)}) %collective-permute-start.13) | collective-permute-done | bytes 16416 | tf_op jit(solution)/shard_map/ppermute | solution.py:349
  25.5 0.5 %collective-permute-start.16 = (f32[2,16,128]{2,1,0:T(8,128)S(1)}, f32[2,16,128]{2,1,0:T(8,128)S(1)}, u32[]{:S(2)}, u32[]{:S(2)}) collective-permute-start(f32[2,16,128]{2,1,0:T(8,128)S(1)} %add.21), channel_id=1, source_target_pairs={{0,7},{1,6},{2,5},{3,4},{4,3},{5,2},{6,1},{7,0},{8,15},{9,14},{10,... | collective-permute-start | bytes 49160 | tf_op jit(solution)/shard_map/ppermute | solution.py:351
  26.0 0.9 %collective-permute-start.15 = (f32[2,16,128]{2,1,0:T(8,128)S(1)}, f32[2,16,128]{2,1,0:T(8,128)S(1)}, u32[]{:S(2)}, u32[]{:S(2)}) collective-permute-start(f32[2,16,128]{2,1,0:T(8,128)S(1)} %add.21), channel_id=1, source_target_pairs={{0,3},{1,2},{2,1},{3,0},{4,7},{5,6},{6,5},{7,4},{8,11},{9,10},{10,... | collective-permute-start | bytes 49160 | tf_op jit(solution)/shard_map/ppermute | solution.py:351
  26.8 1.7 %collective-permute-start.14 = (f32[2,16,128]{2,1,0:T(8,128)S(1)}, f32[2,16,128]{2,1,0:T(8,128)S(1)}, u32[]{:S(2)}, u32[]{:S(2)}) collective-permute-start(f32[2,16,128]{2,1,0:T(8,128)S(1)} %add.21), channel_id=1, source_target_pairs={{0,6},{1,7},{2,4},{3,5},{4,2},{5,3},{6,0},{7,1},{8,14},{9,15},{10,... | collective-permute-start | bytes 49160 | tf_op jit(solution)/shard_map/ppermute | solution.py:351
  28.5 1.1 %collective-permute-done.16 = f32[2,16,128]{2,1,0:T(8,128)S(1)} collective-permute-done((f32[2,16,128]{2,1,0:T(8,128)S(1)}, f32[2,16,128]{2,1,0:T(8,128)S(1)}, u32[]{:S(2)}, u32[]{:S(2)}) %collective-permute-start.16) | collective-permute-done | bytes 16416 | tf_op jit(solution)/shard_map/ppermute | solution.py:351
  29.6 0.5 %collective-permute-done.14 = f32[2,16,128]{2,1,0:T(8,128)S(1)} collective-permute-done((f32[2,16,128]{2,1,0:T(8,128)S(1)}, f32[2,16,128]{2,1,0:T(8,128)S(1)}, u32[]{:S(2)}, u32[]{:S(2)}) %collective-permute-start.14) | collective-permute-done | bytes 16416 | tf_op jit(solution)/shard_map/ppermute | solution.py:351
  30.1 2.3 %collective-permute-start.19 = (f32[2,16,128]{2,1,0:T(8,128)S(1)}, f32[2,16,128]{2,1,0:T(8,128)S(1)}, u32[]{:S(2)}, u32[]{:S(2)}) collective-permute-start(f32[2,16,128]{2,1,0:T(8,128)S(1)} %add_add_fusion.1), channel_id=1, source_target_pairs={{0,26},{1,27},{2,24},{3,25},{4,30},{5,31},{6,28},{7,29},{8,18},{9,... | collective-permute-start | bytes 49160 | tf_op jit(solution)/shard_map/ppermute | solution.py:351
  32.7 1.4 %collective-permute-start.17 = (f32[2,16,128]{2,1,0:T(8,128)S(1)}, f32[2,16,128]{2,1,0:T(8,128)S(1)}, u32[]{:S(2)}, u32[]{:S(2)}) collective-permute-start(f32[2,16,128]{2,1,0:T(8,128)S(1)} %add_add_fusion.1), channel_id=1, source_target_pairs={{0,10},{1,11},{2,8},{3,9},{4,14},{5,15},{6,12},{7,13},{8,2},{9,3},... | collective-permute-start | bytes 49160 | tf_op jit(solution)/shard_map/ppermute | solution.py:351
  34.1 0.7 %copy.9 = bf16[1,6,4,16,320]{4,3,2,1,0:T(8,128)(2,1)} copy(bf16[1,6,4,16,320]{4,3,1,2,0:T(8,128)(2,1)S(1)} %maximum_bitcast_fusion) | data formatting | bytes 491520
  35.1 1.5 %collective-permute-done.18 = f32[2,16,128]{2,1,0:T(8,128)S(1)} collective-permute-done((f32[2,16,128]{2,1,0:T(8,128)S(1)}, f32[2,16,128]{2,1,0:T(8,128)S(1)}, u32[]{:S(2)}, u32[]{:S(2)}) %collective-permute-start.18) | collective-permute-done | bytes 16416 | tf_op jit(solution)/shard_map/ppermute | solution.py:351
  36.5 2.6 %factor.1 = f32[80,80]{1,0:T(8,128)} custom-call(f32[2,16,128]{2,1,0:T(8,128)S(1)} %add_add_fusion.gram_ref), custom_call_target="tpu_custom_call" | custom-call | tf_op jit(solution)/shard_map/factor/pallas_call | solution.py:356
  (33 shorter events, 3.7 us)
Async XLA Ops:
  0.6 6.0 %copy-start = (bf16[1,6,3,320,320]{4,3,2,1,0:T(8,128)(2,1)S(1)}, bf16[1,6,3,320,320]{4,3,2,1,0:T(8,128)(2,1)}, u32[]{:S(2)}) copy-start(bf16[1,6,3,320,320]{4,3,2,1,0:T(8,128)(2,1)} %param.8) | copy-start | bytes 11059204
  0.6 8.1 %collective-permute-start.3 = (bf16[6,16,320]{2,1,0:T(8,128)(2,1)}, bf16[6,16,320]{2,1,0:T(8,128)(2,1)S(1)}, u32[]{:S(2)}, u32[]{:S(2)}) collective-permute-start(bf16[6,16,320]{2,1,0:T(8,128)(2,1)} %bitcast.25), channel_id=1, source_target_pairs={{2,4},{4,2},{6,8},{8,6},{10,12},{12,10},{14,16},{16,14},{18,20},{2... | collective-permute-start | bytes 184328 | tf_op jit(solution)/shard_map/ppermute | solution.py:285
  3.6 5.1 %collective-permute-start.2 = (bf16[6,16,320]{2,1,0:T(8,128)(2,1)}, bf16[6,16,320]{2,1,0:T(8,128)(2,1)S(1)}, u32[]{:S(2)}, u32[]{:S(2)}) collective-permute-start(bf16[6,16,320]{2,1,0:T(8,128)(2,1)} %bitcast.26), channel_id=1, source_target_pairs={{0,1},{1,0},{2,3},{3,2},{4,5},{5,4},{6,7},{7,6},{8,9},{9,8},{10,11... | collective-permute-start | bytes 184328 | tf_op jit(solution)/shard_map/ppermute | solution.py:286
  3.7 3.7 %collective-permute-start = (bf16[6,16,320]{2,1,0:T(8,128)(2,1)}, bf16[6,16,320]{2,1,0:T(8,128)(2,1)S(1)}, u32[]{:S(2)}, u32[]{:S(2)}) collective-permute-start(bf16[6,16,320]{2,1,0:T(8,128)(2,1)} %bitcast.27), channel_id=1, source_target_pairs={{0,2},{2,0},{1,3},{3,1},{4,6},{6,4},{5,7},{7,5},{8,10},{10,8},{9,1... | collective-permute-start | bytes 184328 | tf_op jit(solution)/shard_map/ppermute | solution.py:287
  5.0 3.8 %collective-permute-start.1 = (s32[1,1,2,2]{3,2,1,0:T(2,128)}, s32[1,1,2,2]{3,2,1,0:T(2,128)S(1)}, u32[]{:S(2)}, u32[]{:S(2)}) collective-permute-start(s32[1,1,2,2]{3,2,1,0:T(2,128)} %refs_2_.1), channel_id=1, source_target_pairs={{0,1},{1,0},{2,3},{3,2},{4,5},{5,4},{6,7},{7,6},{8,9},{9,8},{10,11... | collective-permute-start | bytes 56 | tf_op jit(solution)/shard_map/ppermute | solution.py:306
  9.0 3.9 %collective-permute-start.6 = (bf16[2,16,320]{2,1,0:T(8,128)(2,1)S(1)}, bf16[2,16,320]{2,1,0:T(8,128)(2,1)S(1)}, u32[]{:S(2)}, u32[]{:S(2)}) collective-permute-start(bf16[2,16,320]{2,1,0:T(8,128)(2,1)S(1)} %get-tuple-element.33), channel_id=1, source_target_pairs={{2,4},{4,2},{6,8},{8,6},{10,12},{12,10},{14,16},{16,14},{18,20},{2... | collective-permute-start | bytes 61448 | tf_op jit(solution)/shard_map/ppermute | solution.py:285
  10.2 3.8 %collective-permute-start.5 = (bf16[2,16,320]{2,1,0:T(8,128)(2,1)S(1)}, bf16[2,16,320]{2,1,0:T(8,128)(2,1)S(1)}, u32[]{:S(2)}, u32[]{:S(2)}) collective-permute-start(bf16[2,16,320]{2,1,0:T(8,128)(2,1)S(1)} %get-tuple-element.32), channel_id=1, source_target_pairs={{0,1},{1,0},{2,3},{3,2},{4,5},{5,4},{6,7},{7,6},{8,9},{9,8},{10,11... | collective-permute-start | bytes 61448 | tf_op jit(solution)/shard_map/ppermute | solution.py:286
  11.1 1.2 %collective-permute-start.4 = (bf16[16,320]{1,0:T(8,128)(2,1)S(1)}, bf16[16,320]{1,0:T(8,128)(2,1)S(1)}, u32[]{:S(2)}, u32[]{:S(2)}) collective-permute-start(bf16[16,320]{1,0:T(8,128)(2,1)S(1)} %get-tuple-element.31), channel_id=1, source_target_pairs={{0,2},{2,0},{1,3},{3,1},{4,6},{6,4},{5,7},{7,5},{8,10},{10,8},{9,1... | collective-permute-start | bytes 30728 | tf_op jit(solution)/shard_map/ppermute | solution.py:287
  14.1 3.9 %collective-permute-start.9 = (bf16[2,16,320]{2,1,0:T(8,128)(2,1)S(1)}, bf16[2,16,320]{2,1,0:T(8,128)(2,1)S(1)}, u32[]{:S(2)}, u32[]{:S(2)}) collective-permute-start(bf16[2,16,320]{2,1,0:T(8,128)(2,1)S(1)} %get-tuple-element.37), channel_id=1, source_target_pairs={{2,4},{4,2},{6,8},{8,6},{10,12},{12,10},{14,16},{16,14},{18,20},{2... | collective-permute-start | bytes 61448 | tf_op jit(solution)/shard_map/ppermute | solution.py:285
  15.1 3.8 %collective-permute-start.8 = (bf16[2,16,320]{2,1,0:T(8,128)(2,1)S(1)}, bf16[2,16,320]{2,1,0:T(8,128)(2,1)S(1)}, u32[]{:S(2)}, u32[]{:S(2)}) collective-permute-start(bf16[2,16,320]{2,1,0:T(8,128)(2,1)S(1)} %get-tuple-element.36), channel_id=1, source_target_pairs={{0,1},{1,0},{2,3},{3,2},{4,5},{5,4},{6,7},{7,6},{8,9},{9,8},{10,11... | collective-permute-start | bytes 61448 | tf_op jit(solution)/shard_map/ppermute | solution.py:286
  16.2 1.2 %collective-permute-start.7 = (bf16[16,320]{1,0:T(8,128)(2,1)S(1)}, bf16[16,320]{1,0:T(8,128)(2,1)S(1)}, u32[]{:S(2)}, u32[]{:S(2)}) collective-permute-start(bf16[16,320]{1,0:T(8,128)(2,1)S(1)} %get-tuple-element.35), channel_id=1, source_target_pairs={{0,2},{2,0},{1,3},{3,1},{4,6},{6,4},{5,7},{7,5},{8,10},{10,8},{9,1... | collective-permute-start | bytes 30728 | tf_op jit(solution)/shard_map/ppermute | solution.py:287
  19.1 3.9 %collective-permute-start.12 = (bf16[2,16,320]{2,1,0:T(8,128)(2,1)S(1)}, bf16[2,16,320]{2,1,0:T(8,128)(2,1)S(1)}, u32[]{:S(2)}, u32[]{:S(2)}) collective-permute-start(bf16[2,16,320]{2,1,0:T(8,128)(2,1)S(1)} %get-tuple-element.41), channel_id=1, source_target_pairs={{2,4},{4,2},{6,8},{8,6},{10,12},{12,10},{14,16},{16,14},{18,20},{2... | collective-permute-start | bytes 61448 | tf_op jit(solution)/shard_map/ppermute | solution.py:285
  20.2 3.8 %collective-permute-start.11 = (bf16[2,16,320]{2,1,0:T(8,128)(2,1)S(1)}, bf16[2,16,320]{2,1,0:T(8,128)(2,1)S(1)}, u32[]{:S(2)}, u32[]{:S(2)}) collective-permute-start(bf16[2,16,320]{2,1,0:T(8,128)(2,1)S(1)} %get-tuple-element.40), channel_id=1, source_target_pairs={{0,1},{1,0},{2,3},{3,2},{4,5},{5,4},{6,7},{7,6},{8,9},{9,8},{10,11... | collective-permute-start | bytes 61448 | tf_op jit(solution)/shard_map/ppermute | solution.py:286
  21.1 1.2 %collective-permute-start.10 = (bf16[16,320]{1,0:T(8,128)(2,1)S(1)}, bf16[16,320]{1,0:T(8,128)(2,1)S(1)}, u32[]{:S(2)}, u32[]{:S(2)}) collective-permute-start(bf16[16,320]{1,0:T(8,128)(2,1)S(1)} %get-tuple-element.39), channel_id=1, source_target_pairs={{0,2},{2,0},{1,3},{3,1},{4,6},{6,4},{5,7},{7,5},{8,10},{10,8},{9,1... | collective-permute-start | bytes 30728 | tf_op jit(solution)/shard_map/ppermute | solution.py:287
  24.2 1.2 %collective-permute-start.13 = (f32[2,16,128]{2,1,0:T(8,128)S(1)}, f32[2,16,128]{2,1,0:T(8,128)S(1)}, u32[]{:S(2)}, u32[]{:S(2)}) collective-permute-start(f32[2,16,128]{2,1,0:T(8,128)S(1)} %get-tuple-element.45), channel_id=1, source_target_pairs={{0,2},{2,0},{1,3},{3,1},{4,6},{6,4},{5,7},{7,5},{8,10},{10,8},{9,1... | collective-permute-start | bytes 49160 | tf_op jit(solution)/shard_map/ppermute | solution.py:349
  25.5 4.1 %collective-permute-start.16 = (f32[2,16,128]{2,1,0:T(8,128)S(1)}, f32[2,16,128]{2,1,0:T(8,128)S(1)}, u32[]{:S(2)}, u32[]{:S(2)}) collective-permute-start(f32[2,16,128]{2,1,0:T(8,128)S(1)} %add.21), channel_id=1, source_target_pairs={{0,7},{1,6},{2,5},{3,4},{4,3},{5,2},{6,1},{7,0},{8,15},{9,14},{10,... | collective-permute-start | bytes 49160 | tf_op jit(solution)/shard_map/ppermute | solution.py:351
  26.0 3.6 %collective-permute-start.15 = (f32[2,16,128]{2,1,0:T(8,128)S(1)}, f32[2,16,128]{2,1,0:T(8,128)S(1)}, u32[]{:S(2)}, u32[]{:S(2)}) collective-permute-start(f32[2,16,128]{2,1,0:T(8,128)S(1)} %add.21), channel_id=1, source_target_pairs={{0,3},{1,2},{2,1},{3,0},{4,7},{5,6},{6,5},{7,4},{8,11},{9,10},{10,... | collective-permute-start | bytes 49160 | tf_op jit(solution)/shard_map/ppermute | solution.py:351
  26.8 3.3 %collective-permute-start.14 = (f32[2,16,128]{2,1,0:T(8,128)S(1)}, f32[2,16,128]{2,1,0:T(8,128)S(1)}, u32[]{:S(2)}, u32[]{:S(2)}) collective-permute-start(f32[2,16,128]{2,1,0:T(8,128)S(1)} %add.21), channel_id=1, source_target_pairs={{0,6},{1,7},{2,4},{3,5},{4,2},{5,3},{6,0},{7,1},{8,14},{9,15},{10,... | collective-permute-start | bytes 49160 | tf_op jit(solution)/shard_map/ppermute | solution.py:351
  30.1 5.0 %collective-permute-start.19 = (f32[2,16,128]{2,1,0:T(8,128)S(1)}, f32[2,16,128]{2,1,0:T(8,128)S(1)}, u32[]{:S(2)}, u32[]{:S(2)}) collective-permute-start(f32[2,16,128]{2,1,0:T(8,128)S(1)} %add_add_fusion.1), channel_id=1, source_target_pairs={{0,26},{1,27},{2,24},{3,25},{4,30},{5,31},{6,28},{7,29},{8,18},{9,... | collective-permute-start | bytes 49160 | tf_op jit(solution)/shard_map/ppermute | solution.py:351
  32.3 4.2 %collective-permute-start.18 = (f32[2,16,128]{2,1,0:T(8,128)S(1)}, f32[2,16,128]{2,1,0:T(8,128)S(1)}, u32[]{:S(2)}, u32[]{:S(2)}) collective-permute-start(f32[2,16,128]{2,1,0:T(8,128)S(1)} %add_add_fusion.1), channel_id=1, source_target_pairs={{0,18},{1,19},{2,16},{3,17},{4,22},{5,23},{6,20},{7,21},{8,26},{9,... | collective-permute-start | bytes 49160 | tf_op jit(solution)/shard_map/ppermute | solution.py:351
  32.7 3.8 %collective-permute-start.17 = (f32[2,16,128]{2,1,0:T(8,128)S(1)}, f32[2,16,128]{2,1,0:T(8,128)S(1)}, u32[]{:S(2)}, u32[]{:S(2)}) collective-permute-start(f32[2,16,128]{2,1,0:T(8,128)S(1)} %add_add_fusion.1), channel_id=1, source_target_pairs={{0,10},{1,11},{2,8},{3,9},{4,14},{5,15},{6,12},{7,13},{8,2},{9,3},... | collective-permute-start | bytes 49160 | tf_op jit(solution)/shard_map/ppermute | solution.py:351

commit v8 on v7

--- a/solution.py
+++ b/solution.py
@@ -304,14 +304,15 @@
     small = (jnp.transpose(offsets, (2, 0, 1)), donor_elem, fringe_elem, donor_weight, fringe_count)
     messages = exchange(rhs, rhs, *[rhs] * (grids - 1))
     asked = [lax.ppermute(donor_elem, "grid", pairs) for pairs in around]
-    field, offset, *small = pl.pallas_call(
+    offset, *small = pl.pallas_call(
         start_kernel,
-        out_shape=(field_type, *(pltpu.SMEM(x.shape, x.dtype) for x in small)),
-        in_specs=[HBM] * 6, out_specs=(VMEM, *[SMEM] * 5),
-        scratch_shapes=[pltpu.SemaphoreType.DMA((6,))],
+        out_shape=tuple(pltpu.SMEM(x.shape, x.dtype) for x in small),
+        in_specs=[HBM] * 5, out_specs=(SMEM,) * 5,
+        scratch_shapes=[pltpu.SemaphoreType.DMA((5,))],
         compiler_params=limit, name="start",
         cost_estimate=pl.CostEstimate(flops=2 * 10**9, bytes_accessed=10**6, transcendentals=0),
-    )(*(pltpu.with_memory_space_constraint(x, pltpu.HBM) for x in (rhs, *small)))
+    )(*(pltpu.with_memory_space_constraint(x, pltpu.HBM) for x in small))
+    field = rhs
     basis = [field]
     for level in range(S):
         from_side, from_chip, others = messages

time: 39.3 us -> 39.5 us (level)
  waiting for transfers between devices: 10.9 us -> 11.3 us
  transfers between devices with their start and end apart: 20 -> 20, of which waited for: 15 -> 15; matrix products, arithmetic and copies ran while one was open for 2% -> 2% of each run, Pallas kernels for 13% -> 12%
where the time goes in v8:
time: 39.5 us; the launch traced here: 39.4 us
  starting transfers between devices  18.3 us (46%)
  waiting for transfers between devices  11.3 us (29%)
  Pallas kernels  8.18 us (21%)
  local copies, waits for them, and re-layouts  0.76 us (2%)
  between operations  0.74 us (2%)
    ppermute x6, starting transfers between devices, local(): arrived = [lax.ppermute(gram, axes, pairs) for pairs in group]  6.93 us
    ppermute x4, starting transfers between devices, exchange(): from_side = lax.ppermute(to_side, axes, side)  6.29 us
    ppermute x6, waiting for transfers between devices, local(): arrived = [lax.ppermute(gram, axes, pairs) for pairs in group]  3.46 us
    ppermute x4, starting transfers between devices, exchange(): lax.ppermute(v, 'grid', pairs)  3.06 us
    pallas_call x4, Pallas kernels, local(): pl.pallas_call(inner_kernel, out_shape=acc_type, in_specs=[SMEM, VMEM, VM...  2.92 us
    ppermute x4, waiting for transfers between devices, exchange(): lax.ppermute(v, 'grid', pairs)  2.73 us
    pallas_call x1, Pallas kernels, local(): pl.pallas_call(functools.partial(factor_kernel, 1.0 / row_total), out_sha...  2.61 us
    ppermute x4, waiting for transfers between devices, exchange(): from_side = lax.ppermute(to_side, axes, side)  1.5 us
  transfers between devices with their start and end apart: 20, of which 15 were waited for; matrix products, arithmetic and copies ran while one was open for 2% of the time, Pallas kernels for 12%

profile of v8, /device:TPU:0, one launch (start us, length us, event | category | flops | bytes accessed | tf_op | source)
XLA Modules:
  0.0 39.4 jit_solution(241006541170588129)
XLA Ops:
  0.7 3.0 %collective-permute-start.3 = (bf16[6,16,320]{2,1,0:T(8,128)(2,1)}, bf16[6,16,320]{2,1,0:T(8,128)(2,1)S(1)}, u32[]{:S(2)}, u32[]{:S(2)}) collective-permute-start(bf16[6,16,320]{2,1,0:T(8,128)(2,1)} %bitcast.24), channel_id=1, source_target_pairs={{2,4},{4,2},{6,8},{8,6},{10,12},{12,10},{14,16},{16,14},{18,20},{2... | collective-permute-start | bytes 184328 | tf_op jit(solution)/shard_map/ppermute | solution.py:285
  3.7 1.3 %collective-permute-start = (bf16[6,16,320]{2,1,0:T(8,128)(2,1)}, bf16[6,16,320]{2,1,0:T(8,128)(2,1)S(1)}, u32[]{:S(2)}, u32[]{:S(2)}) collective-permute-start(bf16[6,16,320]{2,1,0:T(8,128)(2,1)} %bitcast.26), channel_id=1, source_target_pairs={{0,2},{2,0},{1,3},{3,1},{4,6},{6,4},{5,7},{7,5},{8,10},{10,8},{9,1... | collective-permute-start | bytes 184328 | tf_op jit(solution)/shard_map/ppermute | solution.py:287
  5.0 0.7 %collective-permute-start.1 = (s32[1,1,2,2]{3,2,1,0:T(2,128)}, s32[1,1,2,2]{3,2,1,0:T(2,128)S(1)}, u32[]{:S(2)}, u32[]{:S(2)}) collective-permute-start(s32[1,1,2,2]{3,2,1,0:T(2,128)} %refs_1_.1), channel_id=1, source_target_pairs={{0,1},{1,0},{2,3},{3,2},{4,5},{5,4},{6,7},{7,6},{8,9},{9,8},{10,11... | collective-permute-start | bytes 56 | tf_op jit(solution)/shard_map/ppermute | solution.py:306
  5.7 0.8 %start.1 = (s32[3,1,6]{2,1,0:T(1,128)S(4)}, s32[1,1,2,2]{3,2,1,0:T(2,128)S(4)}, s32[1,1,2,2]{3,2,1,0:T(2,128)S(4)}, f32[1,1,2,2]{3,2,1,0:T(2,128)S(4)}, s32[1,1,2]{2,1,0:T(1,128)S(4)}) custom-call(s32[3,1,6]{2,1,0:T(1,128)} %bitcast.31, s32[1,1,2,2]{3,2,1,0:T(2,128)} %refs_1_.1, s32[1,1,2,2]{3,2,1,0:T(2,128)} %refs_2_.1, f32[1,1,2,2]{3,2,1,0:T(2,128)} %refs_3_.1, ...), custom_call_target="tpu_custom_call" | custom-call | flops 2000000000 | bytes 1000000 | tf_op jit(solution)/shard_map/start/pallas_call | solution.py:307
  6.5 0.7 %inner.4.refs_4_ = f32[6,16,320]{2,1,0:T(8,128)S(1)} custom-call(s32[3,1,6]{2,1,0:T(1,128)S(4)} %get-tuple-element.27.offsets_ref.refs_8_, bf16[6,16,320]{2,1,0:T(8,128)(2,1)S(1)} %bitcast.27, bf16[6,3,320,320]{3,2,1,0:T(8,128)(2,1)S(1)} %bitcast.9), custom_call_target="tpu_custom_call" | custom-call | flops 58982400 | bytes 3686400 | tf_op jit(solution)/shard_map/inner/pallas_call | solution.py:319
  7.4 1.4 %collective-permute-done.1.refs_6_ = s32[1,1,2,2]{3,2,1,0:T(2,128)S(1)} collective-permute-done((s32[1,1,2,2]{3,2,1,0:T(2,128)}, s32[1,1,2,2]{3,2,1,0:T(2,128)S(1)}, u32[]{:S(2)}, u32[]{:S(2)}) %collective-permute-start.1) | collective-permute-done | bytes 48 | tf_op jit(solution)/shard_map/ppermute | solution.py:306
  9.1 1.1 %collective-permute-start.6 = (bf16[2,16,320]{2,1,0:T(8,128)(2,1)S(1)}, bf16[2,16,320]{2,1,0:T(8,128)(2,1)S(1)}, u32[]{:S(2)}, u32[]{:S(2)}) collective-permute-start(bf16[2,16,320]{2,1,0:T(8,128)(2,1)S(1)} %get-tuple-element.31), channel_id=1, source_target_pairs={{2,4},{4,2},{6,8},{8,6},{10,12},{12,10},{14,16},{16,14},{18,20},{2... | collective-permute-start | bytes 61448 | tf_op jit(solution)/shard_map/ppermute | solution.py:285
  10.2 1.0 %collective-permute-start.5 = (bf16[2,16,320]{2,1,0:T(8,128)(2,1)S(1)}, bf16[2,16,320]{2,1,0:T(8,128)(2,1)S(1)}, u32[]{:S(2)}, u32[]{:S(2)}) collective-permute-start(bf16[2,16,320]{2,1,0:T(8,128)(2,1)S(1)} %get-tuple-element.30), channel_id=1, source_target_pairs={{0,1},{1,0},{2,3},{3,2},{4,5},{5,4},{6,7},{7,6},{8,9},{9,8},{10,11... | collective-permute-start | bytes 61448 | tf_op jit(solution)/shard_map/ppermute | solution.py:286
  11.2 0.7 %inner.5.refs_4_ = f32[6,16,320]{2,1,0:T(8,128)S(1)} custom-call(s32[3,1,6]{2,1,0:T(1,128)S(4)} %get-tuple-element.27.offsets_ref.refs_8_, bf16[6,16,320]{2,1,0:T(8,128)(2,1)S(1)} %get-tuple-element.28.v_ref.refs_1_.refs_9_, bf16[6,3,320,320]{3,2,1,0:T(8,128)(2,1)S(1)} %bitcast.12), custom_call_target="tpu_custom_call" | custom-call | flops 58982400 | bytes 3686400 | tf_op jit(solution)/shard_map/inner/pallas_call | solution.py:319
  12.4 0.5 %collective-permute-done.6.halo_ref = bf16[2,16,320]{2,1,0:T(8,128)(2,1)S(1)} collective-permute-done((bf16[2,16,320]{2,1,0:T(8,128)(2,1)S(1)}, bf16[2,16,320]{2,1,0:T(8,128)(2,1)S(1)}, u32[]{:S(2)}, u32[]{:S(2)}) %collective-permute-start.6) | collective-permute-done | bytes 20512 | tf_op jit(solution)/shard_map/ppermute | solution.py:285
  13.1 0.9 %collective-permute-done.5.refs_7_ = bf16[2,16,320]{2,1,0:T(8,128)(2,1)S(1)} collective-permute-done((bf16[2,16,320]{2,1,0:T(8,128)(2,1)S(1)}, bf16[2,16,320]{2,1,0:T(8,128)(2,1)S(1)}, u32[]{:S(2)}, u32[]{:S(2)}) %collective-permute-start.5) | collective-permute-done | bytes 20512 | tf_op jit(solution)/shard_map/ppermute | solution.py:286
  14.1 1.0 %collective-permute-start.9 = (bf16[2,16,320]{2,1,0:T(8,128)(2,1)S(1)}, bf16[2,16,320]{2,1,0:T(8,128)(2,1)S(1)}, u32[]{:S(2)}, u32[]{:S(2)}) collective-permute-start(bf16[2,16,320]{2,1,0:T(8,128)(2,1)S(1)} %get-tuple-element.35), channel_id=1, source_target_pairs={{2,4},{4,2},{6,8},{8,6},{10,12},{12,10},{14,16},{16,14},{18,20},{2... | collective-permute-start | bytes 61448 | tf_op jit(solution)/shard_map/ppermute | solution.py:285
  15.1 1.1 %collective-permute-start.8 = (bf16[2,16,320]{2,1,0:T(8,128)(2,1)S(1)}, bf16[2,16,320]{2,1,0:T(8,128)(2,1)S(1)}, u32[]{:S(2)}, u32[]{:S(2)}) collective-permute-start(bf16[2,16,320]{2,1,0:T(8,128)(2,1)S(1)} %get-tuple-element.34), channel_id=1, source_target_pairs={{0,1},{1,0},{2,3},{3,2},{4,5},{5,4},{6,7},{7,6},{8,9},{9,8},{10,11... | collective-permute-start | bytes 61448 | tf_op jit(solution)/shard_map/ppermute | solution.py:286
  16.2 0.7 %inner.6.refs_4_ = f32[6,16,320]{2,1,0:T(8,128)S(1)} custom-call(s32[3,1,6]{2,1,0:T(1,128)S(4)} %get-tuple-element.27.offsets_ref.refs_8_, bf16[6,16,320]{2,1,0:T(8,128)(2,1)S(1)} %get-tuple-element.32.v_ref.refs_2_.refs_10_, bf16[6,3,320,320]{3,2,1,0:T(8,128)(2,1)S(1)} %bitcast.15), custom_call_target="tpu_custom_call" | custom-call | flops 58982400 | bytes 3686400 | tf_op jit(solution)/shard_map/inner/pallas_call | solution.py:319
  16.9 0.4 %collective-permute-done.7.halo_ref = bf16[16,320]{1,0:T(8,128)(2,1)S(1)} collective-permute-done((bf16[16,320]{1,0:T(8,128)(2,1)S(1)}, bf16[16,320]{1,0:T(8,128)(2,1)S(1)}, u32[]{:S(2)}, u32[]{:S(2)}) %collective-permute-start.7) | collective-permute-done | bytes 10272 | tf_op jit(solution)/shard_map/ppermute | solution.py:287
  17.5 0.5 %collective-permute-done.9.halo_ref = bf16[2,16,320]{2,1,0:T(8,128)(2,1)S(1)} collective-permute-done((bf16[2,16,320]{2,1,0:T(8,128)(2,1)S(1)}, bf16[2,16,320]{2,1,0:T(8,128)(2,1)S(1)}, u32[]{:S(2)}, u32[]{:S(2)}) %collective-permute-start.9) | collective-permute-done | bytes 20512 | tf_op jit(solution)/shard_map/ppermute | solution.py:285
  18.1 0.8 %collective-permute-done.8.refs_7_ = bf16[2,16,320]{2,1,0:T(8,128)(2,1)S(1)} collective-permute-done((bf16[2,16,320]{2,1,0:T(8,128)(2,1)S(1)}, bf16[2,16,320]{2,1,0:T(8,128)(2,1)S(1)}, u32[]{:S(2)}, u32[]{:S(2)}) %collective-permute-start.8) | collective-permute-done | bytes 20512 | tf_op jit(solution)/shard_map/ppermute | solution.py:286
  19.1 1.1 %collective-permute-start.12 = (bf16[2,16,320]{2,1,0:T(8,128)(2,1)S(1)}, bf16[2,16,320]{2,1,0:T(8,128)(2,1)S(1)}, u32[]{:S(2)}, u32[]{:S(2)}) collective-permute-start(bf16[2,16,320]{2,1,0:T(8,128)(2,1)S(1)} %get-tuple-element.39), channel_id=1, source_target_pairs={{2,4},{4,2},{6,8},{8,6},{10,12},{12,10},{14,16},{16,14},{18,20},{2... | collective-permute-start | bytes 61448 | tf_op jit(solution)/shard_map/ppermute | solution.py:285
  20.2 1.0 %collective-permute-start.11 = (bf16[2,16,320]{2,1,0:T(8,128)(2,1)S(1)}, bf16[2,16,320]{2,1,0:T(8,128)(2,1)S(1)}, u32[]{:S(2)}, u32[]{:S(2)}) collective-permute-start(bf16[2,16,320]{2,1,0:T(8,128)(2,1)S(1)} %get-tuple-element.38), channel_id=1, source_target_pairs={{0,1},{1,0},{2,3},{3,2},{4,5},{5,4},{6,7},{7,6},{8,9},{9,8},{10,11... | collective-permute-start | bytes 61448 | tf_op jit(solution)/shard_map/ppermute | solution.py:286
  21.5 0.7 %inner.7.refs_4_ = f32[6,16,320]{2,1,0:T(8,128)S(1)} custom-call(s32[3,1,6]{2,1,0:T(1,128)S(4)} %get-tuple-element.27.offsets_ref.refs_8_, bf16[6,16,320]{2,1,0:T(8,128)(2,1)S(1)} %get-tuple-element.36.v_ref.refs_3_.refs_11_, bf16[6,3,320,320]{3,2,1,0:T(8,128)(2,1)S(1)} %bitcast.18), custom_call_target="tpu_custom_call" | custom-call | flops 58982400 | bytes 3686400 | tf_op jit(solution)/shard_map/inner/pallas_call | solution.py:319
  22.5 0.5 %collective-permute-done.12.halo_ref = bf16[2,16,320]{2,1,0:T(8,128)(2,1)S(1)} collective-permute-done((bf16[2,16,320]{2,1,0:T(8,128)(2,1)S(1)}, bf16[2,16,320]{2,1,0:T(8,128)(2,1)S(1)}, u32[]{:S(2)}, u32[]{:S(2)}) %collective-permute-start.12) | collective-permute-done | bytes 20512 | tf_op jit(solution)/shard_map/ppermute | solution.py:285
  23.1 0.9 %collective-permute-done.11.refs_6_ = bf16[2,16,320]{2,1,0:T(8,128)(2,1)S(1)} collective-permute-done((bf16[2,16,320]{2,1,0:T(8,128)(2,1)S(1)}, bf16[2,16,320]{2,1,0:T(8,128)(2,1)S(1)}, u32[]{:S(2)}, u32[]{:S(2)}) %collective-permute-start.11) | collective-permute-done | bytes 20512 | tf_op jit(solution)/shard_map/ppermute | solution.py:286
  24.3 1.2 %collective-permute-done.13 = f32[2,16,128]{2,1,0:T(8,128)S(1)} collective-permute-done((f32[2,16,128]{2,1,0:T(8,128)S(1)}, f32[2,16,128]{2,1,0:T(8,128)S(1)}, u32[]{:S(2)}, u32[]{:S(2)}) %collective-permute-start.13) | collective-permute-done | bytes 16416 | tf_op jit(solution)/shard_map/ppermute | solution.py:350
  25.9 0.9 %collective-permute-start.15 = (f32[2,16,128]{2,1,0:T(8,128)S(1)}, f32[2,16,128]{2,1,0:T(8,128)S(1)}, u32[]{:S(2)}, u32[]{:S(2)}) collective-permute-start(f32[2,16,128]{2,1,0:T(8,128)S(1)} %add.21), channel_id=1, source_target_pairs={{0,3},{1,2},{2,1},{3,0},{4,7},{5,6},{6,5},{7,4},{8,11},{9,10},{10,... | collective-permute-start | bytes 49160 | tf_op jit(solution)/shard_map/ppermute | solution.py:352
  26.8 1.7 %collective-permute-start.14 = (f32[2,16,128]{2,1,0:T(8,128)S(1)}, f32[2,16,128]{2,1,0:T(8,128)S(1)}, u32[]{:S(2)}, u32[]{:S(2)}) collective-permute-start(f32[2,16,128]{2,1,0:T(8,128)S(1)} %add.21), channel_id=1, source_target_pairs={{0,6},{1,7},{2,4},{3,5},{4,2},{5,3},{6,0},{7,1},{8,14},{9,15},{10,... | collective-permute-start | bytes 49160 | tf_op jit(solution)/shard_map/ppermute | solution.py:352
  28.5 1.1 %collective-permute-done.16 = f32[2,16,128]{2,1,0:T(8,128)S(1)} collective-permute-done((f32[2,16,128]{2,1,0:T(8,128)S(1)}, f32[2,16,128]{2,1,0:T(8,128)S(1)}, u32[]{:S(2)}, u32[]{:S(2)}) %collective-permute-start.16) | collective-permute-done | bytes 16416 | tf_op jit(solution)/shard_map/ppermute | solution.py:352
  29.6 0.5 %collective-permute-done.14 = f32[2,16,128]{2,1,0:T(8,128)S(1)} collective-permute-done((f32[2,16,128]{2,1,0:T(8,128)S(1)}, f32[2,16,128]{2,1,0:T(8,128)S(1)}, u32[]{:S(2)}, u32[]{:S(2)}) %collective-permute-start.14) | collective-permute-done | bytes 16416 | tf_op jit(solution)/shard_map/ppermute | solution.py:352
  30.1 2.4 %collective-permute-start.19 = (f32[2,16,128]{2,1,0:T(8,128)S(1)}, f32[2,16,128]{2,1,0:T(8,128)S(1)}, u32[]{:S(2)}, u32[]{:S(2)}) collective-permute-start(f32[2,16,128]{2,1,0:T(8,128)S(1)} %add_add_fusion.1), channel_id=1, source_target_pairs={{0,26},{1,27},{2,24},{3,25},{4,30},{5,31},{6,28},{7,29},{8,18},{9,... | collective-permute-start | bytes 49160 | tf_op jit(solution)/shard_map/ppermute | solution.py:352
  32.7 1.4 %collective-permute-start.17 = (f32[2,16,128]{2,1,0:T(8,128)S(1)}, f32[2,16,128]{2,1,0:T(8,128)S(1)}, u32[]{:S(2)}, u32[]{:S(2)}) collective-permute-start(f32[2,16,128]{2,1,0:T(8,128)S(1)} %add_add_fusion.1), channel_id=1, source_target_pairs={{0,10},{1,11},{2,8},{3,9},{4,14},{5,15},{6,12},{7,13},{8,2},{9,3},... | collective-permute-start | bytes 49160 | tf_op jit(solution)/shard_map/ppermute | solution.py:352
  34.1 0.7 %copy.9 = bf16[1,6,4,16,320]{4,3,2,1,0:T(8,128)(2,1)} copy(bf16[1,6,4,16,320]{4,3,1,2,0:T(8,128)(2,1)S(1)} %maximum_bitcast_fusion) | data formatting | bytes 491520
  35.1 1.7 %collective-permute-done.18 = f32[2,16,128]{2,1,0:T(8,128)S(1)} collective-permute-done((f32[2,16,128]{2,1,0:T(8,128)S(1)}, f32[2,16,128]{2,1,0:T(8,128)S(1)}, u32[]{:S(2)}, u32[]{:S(2)}) %collective-permute-start.18) | collective-permute-done | bytes 16416 | tf_op jit(solution)/shard_map/ppermute | solution.py:352
  36.7 2.6 %factor.1 = f32[80,80]{1,0:T(8,128)} custom-call(f32[2,16,128]{2,1,0:T(8,128)S(1)} %add_add_fusion.gram_ref), custom_call_target="tpu_custom_call" | custom-call | tf_op jit(solution)/shard_map/factor/pallas_call | solution.py:357
  (35 shorter events, 3.5 us)
Async XLA Ops:
  0.6 5.9 %copy-start.1 = (bf16[1,6,16,320]{3,2,1,0:T(8,128)(2,1)S(1)}, bf16[1,6,16,320]{3,2,1,0:T(8,128)(2,1)}, u32[]{:S(2)}) copy-start(bf16[1,6,16,320]{3,2,1,0:T(8,128)(2,1)} %param.7) | copy-start | bytes 184324
  0.6 5.9 %copy-start = (bf16[1,6,3,320,320]{4,3,2,1,0:T(8,128)(2,1)S(1)}, bf16[1,6,3,320,320]{4,3,2,1,0:T(8,128)(2,1)}, u32[]{:S(2)}) copy-start(bf16[1,6,3,320,320]{4,3,2,1,0:T(8,128)(2,1)} %param.8) | copy-start | bytes 11059204
  0.7 8.1 %collective-permute-start.3 = (bf16[6,16,320]{2,1,0:T(8,128)(2,1)}, bf16[6,16,320]{2,1,0:T(8,128)(2,1)S(1)}, u32[]{:S(2)}, u32[]{:S(2)}) collective-permute-start(bf16[6,16,320]{2,1,0:T(8,128)(2,1)} %bitcast.24), channel_id=1, source_target_pairs={{2,4},{4,2},{6,8},{8,6},{10,12},{12,10},{14,16},{16,14},{18,20},{2... | collective-permute-start | bytes 184328 | tf_op jit(solution)/shard_map/ppermute | solution.py:285
  3.7 5.1 %collective-permute-start.2 = (bf16[6,16,320]{2,1,0:T(8,128)(2,1)}, bf16[6,16,320]{2,1,0:T(8,128)(2,1)S(1)}, u32[]{:S(2)}, u32[]{:S(2)}) collective-permute-start(bf16[6,16,320]{2,1,0:T(8,128)(2,1)} %bitcast.25), channel_id=1, source_target_pairs={{0,1},{1,0},{2,3},{3,2},{4,5},{5,4},{6,7},{7,6},{8,9},{9,8},{10,11... | collective-permute-start | bytes 184328 | tf_op jit(solution)/shard_map/ppermute | solution.py:286
  3.7 3.5 %collective-permute-start = (bf16[6,16,320]{2,1,0:T(8,128)(2,1)}, bf16[6,16,320]{2,1,0:T(8,128)(2,1)S(1)}, u32[]{:S(2)}, u32[]{:S(2)}) collective-permute-start(bf16[6,16,320]{2,1,0:T(8,128)(2,1)} %bitcast.26), channel_id=1, source_target_pairs={{0,2},{2,0},{1,3},{3,1},{4,6},{6,4},{5,7},{7,5},{8,10},{10,8},{9,1... | collective-permute-start | bytes 184328 | tf_op jit(solution)/shard_map/ppermute | solution.py:287
  5.0 3.8 %collective-permute-start.1 = (s32[1,1,2,2]{3,2,1,0:T(2,128)}, s32[1,1,2,2]{3,2,1,0:T(2,128)S(1)}, u32[]{:S(2)}, u32[]{:S(2)}) collective-permute-start(s32[1,1,2,2]{3,2,1,0:T(2,128)} %refs_1_.1), channel_id=1, source_target_pairs={{0,1},{1,0},{2,3},{3,2},{4,5},{5,4},{6,7},{7,6},{8,9},{9,8},{10,11... | collective-permute-start | bytes 56 | tf_op jit(solution)/shard_map/ppermute | solution.py:306
  9.1 3.9 %collective-permute-start.6 = (bf16[2,16,320]{2,1,0:T(8,128)(2,1)S(1)}, bf16[2,16,320]{2,1,0:T(8,128)(2,1)S(1)}, u32[]{:S(2)}, u32[]{:S(2)}) collective-permute-start(bf16[2,16,320]{2,1,0:T(8,128)(2,1)S(1)} %get-tuple-element.31), channel_id=1, source_target_pairs={{2,4},{4,2},{6,8},{8,6},{10,12},{12,10},{14,16},{16,14},{18,20},{2... | collective-permute-start | bytes 61448 | tf_op jit(solution)/shard_map/ppermute | solution.py:285
  10.2 3.8 %collective-permute-start.5 = (bf16[2,16,320]{2,1,0:T(8,128)(2,1)S(1)}, bf16[2,16,320]{2,1,0:T(8,128)(2,1)S(1)}, u32[]{:S(2)}, u32[]{:S(2)}) collective-permute-start(bf16[2,16,320]{2,1,0:T(8,128)(2,1)S(1)} %get-tuple-element.30), channel_id=1, source_target_pairs={{0,1},{1,0},{2,3},{3,2},{4,5},{5,4},{6,7},{7,6},{8,9},{9,8},{10,11... | collective-permute-start | bytes 61448 | tf_op jit(solution)/shard_map/ppermute | solution.py:286
  11.1 1.2 %collective-permute-start.4 = (bf16[16,320]{1,0:T(8,128)(2,1)S(1)}, bf16[16,320]{1,0:T(8,128)(2,1)S(1)}, u32[]{:S(2)}, u32[]{:S(2)}) collective-permute-start(bf16[16,320]{1,0:T(8,128)(2,1)S(1)} %get-tuple-element.29), channel_id=1, source_target_pairs={{0,2},{2,0},{1,3},{3,1},{4,6},{6,4},{5,7},{7,5},{8,10},{10,8},{9,1... | collective-permute-start | bytes 30728 | tf_op jit(solution)/shard_map/ppermute | solution.py:287
  14.1 3.9 %collective-permute-start.9 = (bf16[2,16,320]{2,1,0:T(8,128)(2,1)S(1)}, bf16[2,16,320]{2,1,0:T(8,128)(2,1)S(1)}, u32[]{:S(2)}, u32[]{:S(2)}) collective-permute-start(bf16[2,16,320]{2,1,0:T(8,128)(2,1)S(1)} %get-tuple-element.35), channel_id=1, source_target_pairs={{2,4},{4,2},{6,8},{8,6},{10,12},{12,10},{14,16},{16,14},{18,20},{2... | collective-permute-start | bytes 61448 | tf_op jit(solution)/shard_map/ppermute | solution.py:285
  15.1 3.8 %collective-permute-start.8 = (bf16[2,16,320]{2,1,0:T(8,128)(2,1)S(1)}, bf16[2,16,320]{2,1,0:T(8,128)(2,1)S(1)}, u32[]{:S(2)}, u32[]{:S(2)}) collective-permute-start(bf16[2,16,320]{2,1,0:T(8,128)(2,1)S(1)} %get-tuple-element.34), channel_id=1, source_target_pairs={{0,1},{1,0},{2,3},{3,2},{4,5},{5,4},{6,7},{7,6},{8,9},{9,8},{10,11... | collective-permute-start | bytes 61448 | tf_op jit(solution)/shard_map/ppermute | solution.py:286
  16.2 1.2 %collective-permute-start.7 = (bf16[16,320]{1,0:T(8,128)(2,1)S(1)}, bf16[16,320]{1,0:T(8,128)(2,1)S(1)}, u32[]{:S(2)}, u32[]{:S(2)}) collective-permute-start(bf16[16,320]{1,0:T(8,128)(2,1)S(1)} %get-tuple-element.33), channel_id=1, source_target_pairs={{0,2},{2,0},{1,3},{3,1},{4,6},{6,4},{5,7},{7,5},{8,10},{10,8},{9,1... | collective-permute-start | bytes 30728 | tf_op jit(solution)/shard_map/ppermute | solution.py:287
  19.1 3.9 %collective-permute-start.12 = (bf16[2,16,320]{2,1,0:T(8,128)(2,1)S(1)}, bf16[2,16,320]{2,1,0:T(8,128)(2,1)S(1)}, u32[]{:S(2)}, u32[]{:S(2)}) collective-permute-start(bf16[2,16,320]{2,1,0:T(8,128)(2,1)S(1)} %get-tuple-element.39), channel_id=1, source_target_pairs={{2,4},{4,2},{6,8},{8,6},{10,12},{12,10},{14,16},{16,14},{18,20},{2... | collective-permute-start | bytes 61448 | tf_op jit(solution)/shard_map/ppermute | solution.py:285
  20.2 3.8 %collective-permute-start.11 = (bf16[2,16,320]{2,1,0:T(8,128)(2,1)S(1)}, bf16[2,16,320]{2,1,0:T(8,128)(2,1)S(1)}, u32[]{:S(2)}, u32[]{:S(2)}) collective-permute-start(bf16[2,16,320]{2,1,0:T(8,128)(2,1)S(1)} %get-tuple-element.38), channel_id=1, source_target_pairs={{0,1},{1,0},{2,3},{3,2},{4,5},{5,4},{6,7},{7,6},{8,9},{9,8},{10,11... | collective-permute-start | bytes 61448 | tf_op jit(solution)/shard_map/ppermute | solution.py:286
  21.2 1.2 %collective-permute-start.10 = (bf16[16,320]{1,0:T(8,128)(2,1)S(1)}, bf16[16,320]{1,0:T(8,128)(2,1)S(1)}, u32[]{:S(2)}, u32[]{:S(2)}) collective-permute-start(bf16[16,320]{1,0:T(8,128)(2,1)S(1)} %get-tuple-element.37), channel_id=1, source_target_pairs={{0,2},{2,0},{1,3},{3,1},{4,6},{6,4},{5,7},{7,5},{8,10},{10,8},{9,1... | collective-permute-start | bytes 30728 | tf_op jit(solution)/shard_map/ppermute | solution.py:287
  24.3 1.2 %collective-permute-start.13 = (f32[2,16,128]{2,1,0:T(8,128)S(1)}, f32[2,16,128]{2,1,0:T(8,128)S(1)}, u32[]{:S(2)}, u32[]{:S(2)}) collective-permute-start(f32[2,16,128]{2,1,0:T(8,128)S(1)} %get-tuple-element.43), channel_id=1, source_target_pairs={{0,2},{2,0},{1,3},{3,1},{4,6},{6,4},{5,7},{7,5},{8,10},{10,8},{9,1... | collective-permute-start | bytes 49160 | tf_op jit(solution)/shard_map/ppermute | solution.py:350
  25.5 4.1 %collective-permute-start.16 = (f32[2,16,128]{2,1,0:T(8,128)S(1)}, f32[2,16,128]{2,1,0:T(8,128)S(1)}, u32[]{:S(2)}, u32[]{:S(2)}) collective-permute-start(f32[2,16,128]{2,1,0:T(8,128)S(1)} %add.21), channel_id=1, source_target_pairs={{0,7},{1,6},{2,5},{3,4},{4,3},{5,2},{6,1},{7,0},{8,15},{9,14},{10,... | collective-permute-start | bytes 49160 | tf_op jit(solution)/shard_map/ppermute | solution.py:352
  25.9 3.7 %collective-permute-start.15 = (f32[2,16,128]{2,1,0:T(8,128)S(1)}, f32[2,16,128]{2,1,0:T(8,128)S(1)}, u32[]{:S(2)}, u32[]{:S(2)}) collective-permute-start(f32[2,16,128]{2,1,0:T(8,128)S(1)} %add.21), channel_id=1, source_target_pairs={{0,3},{1,2},{2,1},{3,0},{4,7},{5,6},{6,5},{7,4},{8,11},{9,10},{10,... | collective-permute-start | bytes 49160 | tf_op jit(solution)/shard_map/ppermute | solution.py:352
  26.8 3.3 %collective-permute-start.14 = (f32[2,16,128]{2,1,0:T(8,128)S(1)}, f32[2,16,128]{2,1,0:T(8,128)S(1)}, u32[]{:S(2)}, u32[]{:S(2)}) collective-permute-start(f32[2,16,128]{2,1,0:T(8,128)S(1)} %add.21), channel_id=1, source_target_pairs={{0,6},{1,7},{2,4},{3,5},{4,2},{5,3},{6,0},{7,1},{8,14},{9,15},{10,... | collective-permute-start | bytes 49160 | tf_op jit(solution)/shard_map/ppermute | solution.py:352
  30.1 5.0 %collective-permute-start.19 = (f32[2,16,128]{2,1,0:T(8,128)S(1)}, f32[2,16,128]{2,1,0:T(8,128)S(1)}, u32[]{:S(2)}, u32[]{:S(2)}) collective-permute-start(f32[2,16,128]{2,1,0:T(8,128)S(1)} %add_add_fusion.1), channel_id=1, source_target_pairs={{0,26},{1,27},{2,24},{3,25},{4,30},{5,31},{6,28},{7,29},{8,18},{9,... | collective-permute-start | bytes 49160 | tf_op jit(solution)/shard_map/ppermute | solution.py:352
  32.5 4.2 %collective-permute-start.18 = (f32[2,16,128]{2,1,0:T(8,128)S(1)}, f32[2,16,128]{2,1,0:T(8,128)S(1)}, u32[]{:S(2)}, u32[]{:S(2)}) collective-permute-start(f32[2,16,128]{2,1,0:T(8,128)S(1)} %add_add_fusion.1), channel_id=1, source_target_pairs={{0,18},{1,19},{2,16},{3,17},{4,22},{5,23},{6,20},{7,21},{8,26},{9,... | collective-permute-start | bytes 49160 | tf_op jit(solution)/shard_map/ppermute | solution.py:352
  32.7 4.0 %collective-permute-start.17 = (f32[2,16,128]{2,1,0:T(8,128)S(1)}, f32[2,16,128]{2,1,0:T(8,128)S(1)}, u32[]{:S(2)}, u32[]{:S(2)}) collective-permute-start(f32[2,16,128]{2,1,0:T(8,128)S(1)} %add_add_fusion.1), channel_id=1, source_target_pairs={{0,10},{1,11},{2,8},{3,9},{4,14},{5,15},{6,12},{7,13},{8,2},{9,3},... | collective-permute-start | bytes 49160 | tf_op jit(solution)/shard_map/ppermute | solution.py:352
